TPU v7x, 128 devices: a whole 4x4x4 slice. The times are simulated.
128 devices in a mesh: row: 16 (over x, y), col: 8 (over z, core).
Axes of the slice: x: 4, y: 4, z: 4, core: 2. Of those that a mesh axis runs over, the one named last changes fastest.
Arguments:
- features: bfloat16 [131072, 512], P(('row', 'col')), may hold values from -24 to 24
- weights: bfloat16 [1024, 512], replicated, may hold values from -0.25 to 0.25
- cotangent: bfloat16 [131072, 512], P(('row', 'col')), may hold values from -6 to 6
- neighbours: int32 [131072, 8], P(('row', 'col')), may hold values from 0 to 3071
- send_rows: int32 [128, 128, 8], P(('row', 'col')), may hold values from 0 to 1023
- send_count: int32 [128, 128], P(('row', 'col')), may hold values from 1 to 8, as said below
- hub_local: int32 [128, 8], P(('row', 'col')), may hold values from 0 to 1023
Outputs:
- activations: bfloat16 [131072, 512], P(('row', 'col'))
- grad_features: bfloat16 [131072, 512], P(('row', 'col'))
- grad_weights: float32 [1024, 512], P(('row', 'col'))
Inputs may be any that keep to these rules, and one draw needn't show every extreme that they name: send_count[p, q] counts the live leading slots of send_rows[p, q]; in every draw some pair has 8 live slots, and some partition receives 8 live slots from every partition.
All inputs are finite; a program needn't handle non-finite values.
Results may differ from a plain program's by a relative error of at most 0.0051.
Values may be sent and summed in bfloat16 or wider, within the bound.
No kernel may reach another device: no remote copies, remote signals or barrier semaphores. Data moves between devices by JAX's collectives and lax.ppermute only.
A program may use at most 128 MiB of HBM per device.

v0:
```python
import jax
import jax.numpy as jnp
from jax import lax
from jax.sharding import PartitionSpec as P

DEG = 8


def local(features, weights, cotangent, neighbours, send_rows, send_count, hub_local):
    node_rows = features.shape[0]
    width = features.shape[1]
    part_count = lax.axis_size(("row", "col"))
    slot_count = send_rows.shape[2]
    live_slot = (
        lax.broadcasted_iota(jnp.int32, (part_count, slot_count), 1) < send_count[0][:, None]
    )
    outgoing = jnp.where(
        live_slot[:, :, None], features[send_rows[0]], jnp.zeros((), features.dtype)
    )
    incoming = lax.all_to_all(outgoing, ("row", "col"), split_axis=0, concat_axis=0, tiled=True)
    incoming = incoming.reshape(part_count * slot_count, width)
    owned_hubs = features[hub_local[0]]
    hub_rows = lax.all_gather(owned_hubs, ("row", "col"), axis=0, tiled=True)
    table = jnp.concatenate([features, incoming, hub_rows], axis=0)
    summed = jnp.zeros((node_rows, width), jnp.float32)
    for slot_index in range(DEG):
        summed = summed + table[neighbours[:, slot_index]].astype(jnp.float32)
    mean_rows = (summed / DEG).astype(jnp.bfloat16)
    pre = jnp.dot(features, weights[:width], preferred_element_type=jnp.float32)
    pre = pre + jnp.dot(mean_rows, weights[width:], preferred_element_type=jnp.float32)
    sigma = jax.nn.sigmoid(pre)
    activations = (pre * sigma).astype(jnp.bfloat16)
    delta = (cotangent.astype(jnp.float32) * sigma * (1.0 + pre * (1.0 - sigma))).astype(
        jnp.bfloat16
    )
    stacked = jnp.concatenate([features, mean_rows], axis=1)
    grad_weights = lax.psum_scatter(
        lax.dot_general(
            stacked, delta, (((0,), (0,)), ((), ())), preferred_element_type=jnp.float32
        ),
        ("row", "col"),
        scatter_dimension=0,
        tiled=True,
    )
    contract_last = (((1,), (1,)), ((), ()))
    grad_mean = (
        lax.dot_general(delta, weights[width:], contract_last, preferred_element_type=jnp.float32)
        / DEG
    )
    grad_rows = lax.dot_general(
        delta, weights[:width], contract_last, preferred_element_type=jnp.float32
    )
    grad_table = jnp.zeros((table.shape[0], width), jnp.float32)
    for slot_index in range(DEG):
        grad_table = grad_table.at[neighbours[:, slot_index]].add(grad_mean)
    halo_end = node_rows + part_count * slot_count
    halo_grad = grad_table[node_rows:halo_end].reshape(part_count, slot_count, width)
    hub_grad = grad_table[halo_end:]
    returned = lax.all_to_all(
        halo_grad.astype(jnp.bfloat16), ("row", "col"), split_axis=0, concat_axis=0, tiled=True
    ).astype(halo_grad.dtype)
    returned = jnp.where(live_slot[:, :, None], returned, 0.0)
    hub_owned = lax.psum_scatter(hub_grad, ("row", "col"), scatter_dimension=0, tiled=True)
    grad_rows = grad_rows + grad_table[:node_rows]
    grad_rows = grad_rows.at[send_rows[0].reshape(-1)].add(
        returned.reshape(part_count * slot_count, width)
    )
    grad_rows = grad_rows.at[hub_local[0]].add(hub_owned)
    return (activations, grad_rows.astype(jnp.bfloat16), grad_weights)


def solution(mesh):
    placed = (
        P(("row", "col"), None),
        P(),
        P(("row", "col"), None),
        P(("row", "col"), None),
        P(("row", "col"), None, None),
        P(("row", "col"), None),
        P(("row", "col"), None),
    )
    return jax.shard_map(
        local,
        mesh=mesh,
        in_specs=placed,
        out_specs=(P(("row", "col"), None), P(("row", "col"), None), P(("row", "col"), None)),
        check_vma=False,
    )
```

profile of v0, /device:TPU:1, one launch (start us, length us, event | category | flops | bytes accessed | tf_op | source)
XLA Modules:
  0.0 1508.1 jit_solution(6891610673111612483)
XLA Ops:
  12.1 5.4 gather_fusion
  18.6 11.5 all-to-all-start
  32.4 17.0 %all-to-all-done = bf16[128,8,512]{2,1,0:T(8,128)(2,1)S(1)} async-done(((bf16[128,8,512]{2,1,0:T(8,128)(2,1)}), bf16[128,8,512]{2,1,0:T(8,128)(2,1)S(1)}, u32[]{:S(2)}, u32[]{:S(2)}) %all-to-all-start) | async-done | bytes 1048608 | tf_op jit(solution)/shard_map/all_to_all | solution.py:20
  49.5 36.3 %all-gather.3.cloned.1.call-done = bf16[1024,512]{1,0:T(8,128)(2,1)} async-done(((bf16[8,512]{1,0:T(8,128)(2,1)}), bf16[1024,512]{1,0:T(8,128)(2,1)}) %all-gather.3.cloned.1.call-update) | async-done | bytes 1048592 | tf_op jit(solution)/shard_map/all_gather | solution.py:23
  87.7 5.1 gather_fusion.9
  92.8 5.1 gather_fusion.8
  97.9 5.1 gather_fusion.7
  102.9 5.1 gather_fusion.6
  108.0 5.1 gather_fusion.5
  113.0 5.1 gather_fusion.4
  123.1 5.1 gather_fusion.2
  136.2 10.0 scatter_custom_fusion
  146.3 12.0 scatter_fusion
  158.3 12.0 scatter_fusion.1
  170.2 12.0 scatter_fusion.2
  182.2 12.1 scatter_fusion.3
  194.3 12.0 scatter_fusion.4
  206.3 12.0 scatter_fusion.5
  218.3 12.0 scatter_fusion.6
  240.3 5.8 all-to-all-start.1
  248.9 16.2 %all-to-all-done.1 = bf16[128,8,512]{2,1,0:T(8,128)(2,1)} async-done(((bf16[128,8,512]{2,1,0:T(8,128)(2,1)}), bf16[128,8,512]{2,1,0:T(8,128)(2,1)}, u32[]{:S(2)}, u32[]{:S(2)}) %all-to-all-start.1) | async-done | bytes 1048608 | tf_op jit(solution)/shard_map/all_to_all | solution.py:59
  265.1 8.3 scatter_custom_fusion.8
  273.4 591.5 %reduce-scatter.3.cloned.1.call-done = f32[8,512]{1,0:T(8,128)} async-done(((f32[1024,512]{1,0:T(8,128)}), f32[8,512]{1,0:T(8,128)}) %reduce-scatter.3.cloned.1.call-update) | async-done | bytes 16400 | tf_op jit(solution)/shard_map/reduce_scatter | solution.py:63
  867.7 633.7 %reduce-scatter.5.cloned.1.call-done = f32[8,512]{1,0:T(8,128)} async-done(((f32[1024,512]{1,0:T(8,128)}), f32[8,512]{1,0:T(8,128)}) %reduce-scatter.5.cloned.1.call-update) | async-done | bytes 16400 | tf_op jit(solution)/shard_map/reduce_scatter | solution.py:37
  (61 shorter events, 38.7 us)
Async XLA Ops:
  7.2 78.5 %all-gather.3.cloned.1.call-start = ((), (), s32[]{:S(2)}) async-start(), calls=%async_computation.6 | async-start | bytes 1056768 | tf_op jit(solution)/shard_map/all_gather | solution.py:23
  17.4 12.8 copy-start.8
  17.4 12.9 copy-start
  17.5 12.9 copy-start.3
  18.6 30.8 %all-to-all-start = ((bf16[128,8,512]{2,1,0:T(8,128)(2,1)}), bf16[128,8,512]{2,1,0:T(8,128)(2,1)S(1)}, u32[]{:S(2)}, u32[]{:S(2)}) async-start(bf16[128,8,512]{2,1,0:T(8,128)(2,1)} %bitcast_select_fusion), calls=%async_computation | async-start | bytes 2097152 | tf_op jit(solution)/shard_map/all_to_all | solution.py:20
  30.1 834.8 %reduce-scatter.3.cloned.1.call-start = ((), (), s32[]{:S(2)}) async-start(), calls=%async_computation.4 | async-start | bytes 2113536 | tf_op jit(solution)/shard_map/reduce_scatter | solution.py:63
  49.5 36.3 %copy-start.2 = (bf16[128,8,512]{2,1,0:T(8,128)(2,1)}, bf16[128,8,512]{2,1,0:T(8,128)(2,1)S(1)}, u32[]{:S(2)}) copy-start(bf16[128,8,512]{2,1,0:T(8,128)(2,1)S(1)} %all-to-all-done) | copy-start | bytes 3145732
  128.2 4.7 copy-start.4
  128.2 4.7 copy-start.5
  128.2 4.7 copy-start.10
  133.0 2.5 copy-start.6
  233.4 1.2 copy-start.1
  233.4 1.5 copy-start.7
  233.4 1268.0 %reduce-scatter.5.cloned.1.call-start = ((), (), s32[]{:S(2)}) async-start(), calls=%async_computation.5 | async-start | bytes 2113536 | tf_op jit(solution)/shard_map/reduce_scatter | solution.py:37
  237.6 8.5 copy-start.9
  240.3 24.8 %all-to-all-start.1 = ((bf16[128,8,512]{2,1,0:T(8,128)(2,1)}), bf16[128,8,512]{2,1,0:T(8,128)(2,1)}, u32[]{:S(2)}, u32[]{:S(2)}) async-start(bf16[128,8,512]{2,1,0:T(8,128)(2,1)} %fusion.10), calls=%async_computation.1 | async-start | bytes 2097152 | tf_op jit(solution)/shard_map/all_to_all | solution.py:59
Sparse Core Ops, SparseCore 0:
  11.4 74.3 all-gather.2
  233.5 631.4 reduce-scatter.2
  868.0 633.2 reduce-scatter.4
where the time goes:
time: 1520 us; the launch traced here: 1510 us
  waiting for transfers between devices  1290 us (85%)
  other arithmetic  115 us (8%)
  local copies, waits for them, and re-layouts  56.1 us (4%)
  starting transfers between devices  17.4 us (1%)
    reduce_scatter x1, waiting for transfers between devices, local(): lax.psum_scatter(lax.dot_general(stacked, delta, (((0,), (0,)), ((), ()))...  634 us
    reduce_scatter x1, waiting for transfers between devices, local(): lax.psum_scatter(hub_grad, ('row', 'col'), scatter_dimension=0, tiled=True)  592 us
    scatter-add x8, other arithmetic, local(): grad_table = grad_table.at[neighbours[:, slot_index]].add(grad_mean)  94 us
    gather x8, local copies, waits for them, and re-layouts, local(): summed = summed + table[neighbours[:, slot_index]].astype(jnp.float32)  40.5 us
    all_gather x1, waiting for transfers between devices, local(): hub_rows = lax.all_gather(owned_hubs, ('row', 'col'), axis=0, tiled=True)  36.3 us
  transfers between devices with their start and end apart: 5, of which 5 were waited for; matrix products, arithmetic and copies ran while one was open for 2% of the time, Pallas kernels for 0%

commit v1 on v0

v1 whole, which is shorter than its diff:
```python
import jax
import jax.numpy as jnp
from jax import lax
from jax.experimental import pallas as pl
from jax.experimental.pallas import tpu as pltpu
from jax.sharding import PartitionSpec as P

BF = jnp.bfloat16
F32 = jnp.float32
DEG = 8
AXES = ("row", "col")
ROWS = 256
VM = pl.BlockSpec(memory_space=pltpu.VMEM)
SM = pl.BlockSpec(memory_space=pltpu.SMEM)
MIB = 1024 * 1024


def iota(shape, dim):
    return lax.broadcasted_iota(jnp.int32, shape, dim)


def mm(a, b):
    return jnp.dot(a, b, preferred_element_type=F32)


def mm_last(a, b):
    return lax.dot_general(a, b, (((1,), (1,)), ((), ())), preferred_element_type=F32)


def mm_first(a, b):
    return lax.dot_general(a, b, (((0,), (0,)), ((), ())), preferred_element_type=F32)


def params(mib):
    return pltpu.CompilerParams(vmem_limit_bytes=mib * MIB)


def send_kernel(f_ref, rows_ref, count_ref, hub_ref, out_ref, idx_ref):
    parts = rows_ref.shape[1]
    nodes = f_ref.shape[0]
    live = iota((8, parts), 0) < count_ref[...]
    idx = jnp.where(live, rows_ref[...], -1).astype(F32)
    idx_ref[...] = idx.T
    hub = jnp.broadcast_to(hub_ref[...], (8, 8))
    hub_col = jnp.sum(jnp.where(iota((8, 8), 0) == iota((8, 8), 1), hub, 0), axis=1, keepdims=True)
    hub_hot = (iota((8, nodes), 1) == hub_col).astype(F32).astype(BF)
    hub_rows = mm(hub_hot, f_ref[...])
    step = 16

    @pl.loop(0, parts // step)
    def _(b):
        blk = idx_ref[pl.ds(b * step, step), :]
        wide = jnp.broadcast_to(blk[:, None, :], (step, 8, 8)).reshape(step * 8, 8)
        pick = iota((step * 8, 8), 0) % 8 == iota((step * 8, 8), 1)
        col = jnp.sum(jnp.where(pick, wide, 0.0), axis=1, keepdims=True).astype(jnp.int32)
        hot = (iota((step * 8, nodes), 1) == col).astype(F32).astype(BF)
        listed = mm(hot, f_ref[...]).reshape(step, 8, -1)
        both = jnp.concatenate(
            [listed, jnp.broadcast_to(hub_rows[None], (step, 8, hub_rows.shape[1]))], axis=1
        )
        out_ref[pl.ds(b * step, step)] = both.astype(BF)


def hot_kernel(nb_ref, slot_ref, f_ref, w_ref, ar_ref, at_ref, st_ref, mown_ref, pre_ref, nbt_ref, ao_ref):
    nodes, width = f_ref.shape
    table = at_ref.shape[0]
    nb = nb_ref[...]
    w = nb - nodes
    is_hub = w >= (table - nodes) // 2
    v = jnp.where(is_hub, w - (table - nodes) // 2, w)
    v = nodes + (v // 8) * 16 + v % 8 + jnp.where(is_hub, 8, 0)
    t = jnp.where(nb < nodes, nb, v).astype(F32)
    nbt_ref[...] = t.T
    high = 32
    lanes = 256
    for c in range(nodes // lanes):
        rows = [jnp.broadcast_to(t[k : k + 1, c * lanes : (c + 1) * lanes], (high, lanes)) for k in range(DEG)]

        @pl.loop(0, table // high)
        def _(b):
            it = (iota((high, lanes), 0) + b * high).astype(F32)
            acc = jnp.where(it == rows[0], 1.0, 0.0)
            for k in range(1, DEG):
                acc = acc + jnp.where(it == rows[k], 1.0, 0.0)
            at_ref[pl.ds(b * high, high), c * lanes : (c + 1) * lanes] = acc.astype(BF)

    high = 16

    @pl.loop(0, nodes // high)
    def _(b):
        blk = nbt_ref[pl.ds(b * high, high), :]
        cols = [jnp.broadcast_to(blk[:, k : k + 1], (high, lanes)) for k in range(DEG)]
        base = iota((high, lanes), 1).astype(F32)
        for c in range(table // lanes):
            it = base + float(c * lanes)
            acc = jnp.where(it == cols[0], 1.0, 0.0)
            for k in range(1, DEG):
                acc = acc + jnp.where(it == cols[k], 1.0, 0.0)
            if c * lanes < nodes:
                ao_ref[pl.ds(b * high, high), c * lanes : (c + 1) * lanes] = acc.astype(BF)
            else:
                lo = c * lanes - nodes
                ar_ref[pl.ds(b * high, high), lo : lo + lanes] = acc.astype(BF)

    slot = slot_ref[...]

    @pl.loop(0, nodes // 16)
    def _(b):
        it = iota((16, slot.shape[1]), 0) + b * 16
        st_ref[pl.ds(b * 16, 16), :] = (it == slot).astype(F32).astype(BF)

    @pl.loop(0, nodes // ROWS)
    def _(b):
        r = pl.ds(b * ROWS, ROWS)
        mown_ref[r, :] = mm(ao_ref[r, :], f_ref[...])
        pre_ref[r, :] = mm(f_ref[r, :], w_ref[:width, :])


def mid_kernel(me_ref, recv_ref, ar_ref, at_ref, mown_ref, pre_ref, w_ref, f_ref, cot_ref,
               act_ref, delta_ref, gm_ref, pay_ref, gw_ref, mean_ref, acc_ref):
    nodes, width = delta_ref.shape
    w2 = w_ref[width:, :]

    @pl.loop(0, nodes // ROWS)
    def _(b):
        r = pl.ds(b * ROWS, ROWS)
        mean = ((mm(ar_ref[r, :], recv_ref[...]) + mown_ref[r, :]) / DEG).astype(BF)
        mean_ref[r, :] = mean
        pre = pre_ref[r, :] + mm(mean, w2)
        sig = jax.nn.sigmoid(pre)
        act_ref[r, :] = (pre * sig).astype(BF)
        delta = (cot_ref[r, :].astype(F32) * sig * (1.0 + pre * (1.0 - sig))).astype(BF)
        delta_ref[r, :] = delta
        gm_ref[r, :] = (mm_last(delta, w2) / DEG).astype(BF)

    own = nodes

    @pl.loop(0, pay_ref.shape[0] // ROWS)
    def _(b):
        r = pl.ds(b * ROWS, ROWS)
        pay_ref[r, :] = mm(at_ref[pl.ds(own + b * ROWS, ROWS), :], gm_ref[...]).astype(BF)

    me = me_ref[0]
    for half, x_ref in ((0, f_ref), (1, mean_ref)):
        for b in range(width // ROWS):
            part = mm_first(x_ref[:, b * ROWS : (b + 1) * ROWS], delta_ref[...])
            first = half * (width // 8) + b * (ROWS // 8)
            for j in range(ROWS // 8):
                at = pl.multiple_of(((first + j) ^ me) * 8, 8)
                acc_ref[pl.ds(at, 8), :] = part[j * 8 : (j + 1) * 8, :]
    gw_ref[...] = acc_ref[...].astype(BF)


def own_kernel(delta_ref, gm_ref, at_ref, w_ref, out_ref):
    nodes, width = delta_ref.shape

    @pl.loop(0, nodes // ROWS)
    def _(b):
        r = pl.ds(b * ROWS, ROWS)
        out_ref[r, :] = mm(at_ref[r, :], gm_ref[...]) + mm_last(delta_ref[r, :], w_ref[:width, :])


def last_kernel(st_ref, back_ref, own_ref, out_ref):
    @pl.loop(0, out_ref.shape[0] // ROWS)
    def _(b):
        r = pl.ds(b * ROWS, ROWS)
        out_ref[r, :] = (own_ref[r, :] + mm(st_ref[r, :], back_ref[...])).astype(BF)


def swap(x, bits, parts):
    return lax.ppermute(x, AXES, [(i, i ^ bits) for i in range(parts)])


def call(kernel, ins, outs, scratch=(), flops=0, read=0, mib=40, specs=None, exps=0):
    return pl.pallas_call(
        kernel,
        out_shape=[jax.ShapeDtypeStruct(s, d) for s, d in outs],
        in_specs=specs or [VM] * len(ins),
        out_specs=[VM] * len(outs),
        scratch_shapes=list(scratch),
        compiler_params=params(mib),
        cost_estimate=pl.CostEstimate(flops=flops, bytes_accessed=read, transcendentals=exps),
    )(*ins)


def local(features, weights, cotangent, neighbours, send_rows, send_count, hub_local):
    nodes, width = features.shape
    parts = lax.axis_size(AXES)
    recv_rows = parts * 16
    table = nodes + recv_rows
    me = lax.axis_index(AXES).astype(jnp.int32).reshape(1)

    (pay,) = call(
        send_kernel,
        [features, send_rows[0].T, send_count, hub_local],
        [((parts, 16, width), BF)],
        [pltpu.VMEM((parts, 8), F32)],
        flops=2 * nodes * parts * 8 * width, read=3 * MIB,
    )
    recv = lax.all_to_all(pay, AXES, split_axis=0, concat_axis=0, tiled=True).reshape(recv_rows, width)

    live = iota((parts, 8), 1) < send_count[0][:, None]
    slot = jnp.concatenate(
        [jnp.where(live, send_rows[0], -1), jnp.broadcast_to(hub_local, (parts, 8))], axis=1
    ).reshape(1, recv_rows)
    a_recv, a_t, s_t, mean_own, pre_own = call(
        hot_kernel,
        [neighbours.T, slot, features, weights],
        [((nodes, recv_rows), BF), ((table, nodes), BF), ((nodes, recv_rows), BF), ((nodes, width), F32), ((nodes, width), F32)],
        [pltpu.VMEM((nodes, DEG), F32), pltpu.VMEM((nodes, nodes), BF)],
        flops=14 * 10**9, read=20 * MIB,
    )
    act, delta, gm, back, gw = call(
        mid_kernel,
        [me, recv, a_recv, a_t, mean_own, pre_own, weights, features, cotangent],
        [((nodes, width), BF), ((nodes, width), BF), ((nodes, width), BF), ((recv_rows, width), BF), ((2 * width, width), BF)],
        [pltpu.VMEM((nodes, width), BF), pltpu.VMEM((2 * width, width), F32)],
        flops=8 * 10**9, read=20 * MIB,
        specs=[SM] + [VM] * 8,
    )
    back = lax.all_to_all(
        back.reshape(parts, 16, width), AXES, split_axis=0, concat_axis=0, tiled=True
    ).reshape(recv_rows, width)
    (own,) = call(own_kernel, [delta, gm, a_t, weights], [((nodes, width), F32)], flops=2 * 10**9, read=8 * MIB)

    blocks = gw.reshape(4, 4, 4, 2, 8, width)
    acc = blocks[:, :, :, 0].astype(F32) + swap(blocks[:, :, :, 1], 1, parts).astype(F32)
    for bits in (32, 8, 2):
        piece = acc.astype(BF)
        acc = acc[0] + sum(swap(piece[j], bits * j, parts).astype(F32) for j in (1, 2, 3))

    (grad,) = call(last_kernel, [s_t, back, own], [((nodes, width), BF)], flops=2 * 10**9, read=8 * MIB)
    return act, grad, acc.reshape(8, width)


def solution(mesh):
    both = P(AXES, None)
    placed = (both, P(), both, both, P(AXES, None, None), both, both)
    return jax.shard_map(local, mesh=mesh, in_specs=placed, out_specs=(both, both, both), check_vma=False)
```

time: 1520 us -> 157 us (0.10)
  waiting for transfers between devices: 1290 us -> 29.3 us
  other arithmetic: 115 us -> 2.18 us
  Pallas kernels: 0 us -> 61 us
  local copies, waits for them, and re-layouts: 56.1 us -> 28.1 us
  starting transfers between devices: 17.4 us -> 33.4 us
    reduce_scatter x2 -> x0, waiting for transfers between devices: 1230 us -> none  [the longest x1 634 us: local(): lax.psum_scatter(lax.dot_general(stacked, delta, (((0,), (0,)), ((), ()))...]
    scatter-add x10 -> x0, other arithmetic: 104 us -> none  [the longest x8 94 us: local(): grad_table = grad_table.at[neighbours[:, slot_index]].add(grad_mean)]
    pallas_call x0 -> x5, Pallas kernels: none -> 61 us  [call(): pl.pallas_call(kernel, out_shape=[jax.ShapeDtypeStruct(s, d) for s, d in...]
    gather x10 -> x0, local copies, waits for them, and re-layouts: 48.4 us -> none  [the longest x8 40.5 us: local(): summed = summed + table[neighbours[:, slot_index]].astype(jnp.float32)]
    all_gather x1 -> x0, waiting for transfers between devices: 36.3 us -> none  [local(): hub_rows = lax.all_gather(owned_hubs, ('row', 'col'), axis=0, tiled=True)]
    all_to_all x2, waiting for transfers between devices: 33.2 us -> 0.01 us  [the longest x1 0.01 us: local(): lax.all_to_all(back.reshape(parts, 16, width), AXES, split_axis=0, concat...]
    ppermute x0 -> x10, waiting for transfers between devices: none -> 29.3 us  [swap(): return lax.ppermute(x, AXES, [(i, i ^ bits) for i in range(parts)])]
    unnamed x23 -> x56, local copies, waits for them, and re-layouts: 1.61 us -> 27 us
  transfers between devices with their start and end apart: 5 -> 12, of which waited for: 5 -> 5; matrix products, arithmetic and copies ran while one was open for 2% -> 2% of each run, Pallas kernels for 0% -> 25%
where the time goes in v1:
time: 157 us; the launch traced here: 155 us
  Pallas kernels  61 us (39%)
  starting transfers between devices  33.4 us (21%)
  waiting for transfers between devices  29.3 us (19%)
  local copies, waits for them, and re-layouts  28.1 us (18%)
  other arithmetic  2.18 us (1%)
    pallas_call x5, Pallas kernels, call(): pl.pallas_call(kernel, out_shape=[jax.ShapeDtypeStruct(s, d) for s, d in...  61 us
    ppermute x10, waiting for transfers between devices, swap(): return lax.ppermute(x, AXES, [(i, i ^ bits) for i in range(parts)])  29.3 us
    unnamed x56, local copies, waits for them, and re-layouts  27 us
    ppermute x10, starting transfers between devices, swap(): return lax.ppermute(x, AXES, [(i, i ^ bits) for i in range(parts)])  13.1 us
    all_to_all x1, starting transfers between devices, local(): lax.all_to_all(pay, AXES, split_axis=0, concat_axis=0, tiled=True)  11.4 us
    all_to_all x1, starting transfers between devices, local(): lax.all_to_all(back.reshape(parts, 16, width), AXES, split_axis=0, concat...  8.86 us
  transfers between devices with their start and end apart: 12, of which 5 were waited for; matrix products, arithmetic and copies ran while one was open for 2% of the time, Pallas kernels for 25%

profile of v1, /device:TPU:1, one launch (start us, length us, event | category | flops | bytes accessed | tf_op | source)
XLA Modules:
  0.0 155.0 jit_solution(11976721279071382317)
XLA Ops:
  3.9 3.5 %shard_map.94 = bf16[128,16,512]{2,1,0:T(8,128)(2,1)S(1)} custom-call(bf16[1024,512]{1,0:T(8,128)(2,1)S(1)} %copy-done.17, s32[8,128]{1,0:T(8,128)S(1)} %bitcast.62, s32[1,128]{1,0:T(1,128)S(1)} %copy-done.15, s32[1,8]{1,0:T(1,128)S(1)} %copy-done.22), custom_call_target="tpu_custom_call" | custom-call | flops 1073741824 | bytes 3145728 | tf_op jit(solution)/shard_map/pallas_call | solution.py:175
  8.7 11.4 %all-to-all-start = ((bf16[128,16,512]{2,1,0:T(8,128)(2,1)}), bf16[128,16,512]{2,1,0:T(8,128)(2,1)S(1)}, u32[]{:S(2)}, u32[]{:S(2)}) async-start(bf16[128,16,512]{2,1,0:T(8,128)(2,1)} %copy-done.5), calls=%async_computation | async-start | bytes 4194304 | tf_op jit(solution)/shard_map/all_to_all | solution.py:200
  21.8 35.8 %shard_map.95 = (bf16[1024,2048]{1,0:T(8,128)(2,1)S(1)}, bf16[3072,1024]{1,0:T(8,128)(2,1)}, bf16[1024,2048]{1,0:T(8,128)(2,1)}, f32[1024,512]{1,0:T(8,128)S(1)}, f32[1024,512]{1,0:T(8,128)S(1)}) custom-call(s32[8,1024]{1,0:T(8,128)S(1)} %bitcast.64, s32[1,2048]{1,0:T(1,128)S(1)} %reshape.29.slot_ref, bf16[1024,512]{1,0:T(8,128)(2,1)S(1)} %copy-done.18, ...), custom_call_target="tpu_custom_call" | custom-call | flops 14000000000 | bytes 20971520 | tf_op jit(solution)/shard_map/pallas_call | solution.py:175
  57.6 2.1 %copy-done.24 = bf16[1024,2048]{1,0:T(8,128)(2,1)} copy-done((bf16[1024,2048]{1,0:T(8,128)(2,1)}, bf16[1024,2048]{1,0:T(8,128)(2,1)S(1)}, u32[]{:S(2)}) %copy-start.24) | copy-done | bytes 4194328
  66.0 1.6 %copy-done.26 = f32[1024,512]{1,0:T(8,128)S(1)} copy-done((f32[1024,512]{1,0:T(8,128)S(1)}, f32[1024,512]{1,0:T(8,128)}, u32[]{:S(2)}) %copy-start.26) | copy-done | bytes 2097176
  67.6 15.5 %shard_map.96 = (bf16[1024,512]{1,0:T(8,128)(2,1)}, bf16[1024,512]{1,0:T(8,128)(2,1)S(1)}, bf16[1024,512]{1,0:T(8,128)(2,1)S(1)}, bf16[2048,512]{1,0:T(8,128)(2,1)S(1)}, bf16[1024,512]{1,0:T(8,128)(2,1)S(1)}) custom-call(s32[1]{0:T(128)} %bitcast.me_ref, bf16[2048,512]{1,0:T(8,128)(2,1)S(1)} %bitcast.59, bf16[1024,2048]{1,0:T(8,128)(2,1)} %copy-done.24, ...), custom_call_target="tpu_custom_call" | custom-call | flops 8000000000 | bytes 20971520 | tf_op jit(solution)/shard_map/pallas_call | solution.py:175
  83.1 1.4 copy-done.4
  88.3 8.9 %all-to-all-start.1 = ((bf16[128,16,512]{2,1,0:T(8,128)(2,1)}), bf16[128,16,512]{2,1,0:T(8,128)(2,1)S(1)}, u32[]{:S(2)}, u32[]{:S(2)}) async-start(bf16[128,16,512]{2,1,0:T(8,128)(2,1)} %bitcast.58), calls=%async_computation.1 | async-start | bytes 4194304 | tf_op jit(solution)/shard_map/all_to_all | solution.py:221
  97.2 1.4 convert_add_fusion
  98.7 1.5 collective-permute-start.1
  100.2 1.8 %collective-permute-start.3 = (bf16[4,4,8,512]{3,2,1,0:T(8,128)(2,1)S(1)}, bf16[4,4,8,512]{3,2,1,0:T(8,128)(2,1)S(1)}, u32[]{:S(2)}, u32[]{:S(2)}) collective-permute-start(bf16[4,4,8,512]{3,2,1,0:T(8,128)(2,1)S(1)} %get-tuple-element.30), channel_id=1, source_target_pairs={{0,96},{1,97},{2,98},{3,99},{4,100},{5,101},{6,102},{7,103},{8,104... | collective-permute-start | bytes 393224 | tf_op jit(solution)/shard_map/ppermute | solution.py:171
  102.6 21.4 %collective-permute-done.1 = bf16[4,4,8,512]{3,2,1,0:T(8,128)(2,1)S(1)} collective-permute-done((bf16[4,4,8,512]{3,2,1,0:T(8,128)(2,1)S(1)}, bf16[4,4,8,512]{3,2,1,0:T(8,128)(2,1)S(1)}, u32[]{:S(2)}, u32[]{:S(2)}) %collective-permute-start.1) | collective-permute-done | bytes 131104 | tf_op jit(solution)/shard_map/ppermute | solution.py:171
  124.0 1.4 collective-permute-done.3
  125.3 3.0 %collective-permute-done.2 = bf16[4,4,8,512]{3,2,1,0:T(8,128)(2,1)S(1)} collective-permute-done((bf16[4,4,8,512]{3,2,1,0:T(8,128)(2,1)S(1)}, bf16[4,4,8,512]{3,2,1,0:T(8,128)(2,1)S(1)}, u32[]{:S(2)}, u32[]{:S(2)}) %collective-permute-start.2) | collective-permute-done | bytes 131104 | tf_op jit(solution)/shard_map/ppermute | solution.py:171
  129.6 1.8 %collective-permute-start.6 = (bf16[4,8,512]{2,1,0:T(8,128)(2,1)S(1)}, bf16[4,8,512]{2,1,0:T(8,128)(2,1)S(1)}, u32[]{:S(2)}, u32[]{:S(2)}) collective-permute-start(bf16[4,8,512]{2,1,0:T(8,128)(2,1)S(1)} %get-tuple-element.33), channel_id=1, source_target_pairs={{0,24},{1,25},{2,26},{3,27},{4,28},{5,29},{6,30},{7,31},{8,16},{9,... | collective-permute-start | bytes 98312 | tf_op jit(solution)/shard_map/ppermute | solution.py:171
  132.1 1.5 collective-permute-done.6
  133.6 2.1 %collective-permute-done.5 = bf16[4,8,512]{2,1,0:T(8,128)(2,1)S(1)} collective-permute-done((bf16[4,8,512]{2,1,0:T(8,128)(2,1)S(1)}, bf16[4,8,512]{2,1,0:T(8,128)(2,1)S(1)}, u32[]{:S(2)}, u32[]{:S(2)}) %collective-permute-start.5) | collective-permute-done | bytes 32800 | tf_op jit(solution)/shard_map/ppermute | solution.py:171
  135.7 1.5 collective-permute-start.7
  137.3 2.1 %collective-permute-start.9 = (bf16[8,512]{1,0:T(8,128)(2,1)S(1)}, bf16[8,512]{1,0:T(8,128)(2,1)S(1)}, u32[]{:S(2)}, u32[]{:S(2)}) collective-permute-start(bf16[8,512]{1,0:T(8,128)(2,1)S(1)} %get-tuple-element.36), channel_id=1, source_target_pairs={{0,6},{1,7},{2,4},{3,5},{4,2},{5,3},{6,0},{7,1},{8,14},{9,15},{10,... | collective-permute-start | bytes 24584 | tf_op jit(solution)/shard_map/ppermute | solution.py:171
  140.2 2.8 %copy-done.2 = bf16[3072,1024]{1,0:T(8,128)(2,1)S(1)} copy-done((bf16[3072,1024]{1,0:T(8,128)(2,1)S(1)}, bf16[3072,1024]{1,0:T(8,128)(2,1)}, u32[]{:S(2)}) %copy-start.2) | copy-done | bytes 6291480
  143.0 2.4 %shard_map.97.own_ref = f32[1024,512]{1,0:T(8,128)S(1)} custom-call(bf16[1024,512]{1,0:T(8,128)(2,1)S(1)} %copy-done.10, bf16[1024,512]{1,0:T(8,128)(2,1)S(1)} %copy-done.12, bf16[3072,1024]{1,0:T(8,128)(2,1)S(1)} %copy-done.2, bf16[1024,512]{1,0:T(8,128)(2,1)S(1)} %copy-done.8), custom_call_target="tpu_custom_call" | custom-call | flops 2000000000 | bytes 8388608 | tf_op jit(solution)/shard_map/pallas_call | solution.py:175
  147.4 1.6 %copy-done.1 = f32[1024,512]{1,0:T(8,128)S(1)} copy-done((f32[1024,512]{1,0:T(8,128)S(1)}, f32[1024,512]{1,0:T(8,128)}, u32[]{:S(2)}) %copy-start.1) | copy-done | bytes 2097176
  149.0 2.2 %copy-done.3 = bf16[1024,2048]{1,0:T(8,128)(2,1)S(1)} copy-done((bf16[1024,2048]{1,0:T(8,128)(2,1)S(1)}, bf16[1024,2048]{1,0:T(8,128)(2,1)}, u32[]{:S(2)}) %copy-start.3) | copy-done | bytes 4194328
  151.2 3.8 %shard_map.98 = bf16[1024,512]{1,0:T(8,128)(2,1)} custom-call(bf16[1024,2048]{1,0:T(8,128)(2,1)S(1)} %copy-done.3, bf16[2048,512]{1,0:T(8,128)(2,1)S(1)} %bitcast.57, f32[1024,512]{1,0:T(8,128)S(1)} %copy-done.1), custom_call_target="tpu_custom_call" | custom-call | flops 2000000000 | bytes 8388608 | tf_op jit(solution)/shard_map/pallas_call | solution.py:175
  (74 shorter events, 21.8 us)
Async XLA Ops:
  8.7 11.5 %copy-start.23 = (s32[1,8]{1,0:T(1,128)S(1)}, s32[1,8]{1,0:T(1,128)}, u32[]{:S(2)}) copy-start(s32[1,8]{1,0:T(1,128)} %hub_ref.1) | copy-start | bytes 100
  8.7 11.6 %copy-start.14 = (s32[1,128,8]{1,2,0:T(8,128)S(1)}, s32[1,128,8]{1,2,0:T(8,128)}, u32[]{:S(2)}) copy-start(s32[1,128,8]{1,2,0:T(8,128)} %param.11) | copy-start | bytes 12292
  8.7 11.6 %copy-start.16 = (s32[1,128]{1,0:T(1,128)S(1)}, s32[1,128]{1,0:T(1,128)}, u32[]{:S(2)}) copy-start(s32[1,128]{1,0:T(1,128)} %count_ref.1) | copy-start | bytes 1540
  8.7 11.8 %copy-start.6 = (bf16[1024,512]{1,0:T(8,128)(2,1)S(1)}, bf16[1024,512]{1,0:T(8,128)(2,1)}, u32[]{:S(2)}) copy-start(bf16[1024,512]{1,0:T(8,128)(2,1)} %w_ref.5) | copy-start | bytes 3145732
  8.7 11.8 %copy-start.21 = (s32[1024,8]{0,1:T(8,128)S(1)}, s32[1024,8]{0,1:T(8,128)}, u32[]{:S(2)}) copy-start(s32[1024,8]{0,1:T(8,128)} %param.10) | copy-start | bytes 98308
  8.7 53.6 %all-to-all-start = ((bf16[128,16,512]{2,1,0:T(8,128)(2,1)}), bf16[128,16,512]{2,1,0:T(8,128)(2,1)S(1)}, u32[]{:S(2)}, u32[]{:S(2)}) async-start(bf16[128,16,512]{2,1,0:T(8,128)(2,1)} %copy-done.5), calls=%async_computation | async-start | bytes 4194304 | tf_op jit(solution)/shard_map/all_to_all | solution.py:200
  57.6 2.1 %copy-start.24 = (bf16[1024,2048]{1,0:T(8,128)(2,1)}, bf16[1024,2048]{1,0:T(8,128)(2,1)S(1)}, u32[]{:S(2)}) copy-start(bf16[1024,2048]{1,0:T(8,128)(2,1)S(1)} %get-tuple-element.13.ar_ref) | copy-start | bytes 12582916
  87.3 10.0 %collective-permute-start = (bf16[4,4,4,8,512]{4,3,2,1,0:T(8,128)(2,1)}, bf16[4,4,4,8,512]{4,3,2,1,0:T(8,128)(2,1)}, u32[]{:S(2)}, u32[]{:S(2)}) collective-permute-start(bf16[4,4,4,8,512]{4,3,2,1,0:T(8,128)(2,1)} %slice_bitcast_fusion), channel_id=1, source_target_pairs={{0,1},{1,0},{2,3},{3,2},{4,5},{5,4},{6,7},{7,6},{8,9},{9,8},{10,11... | collective-permute-start | bytes 1572872 | tf_op jit(solution)/shard_map/ppermute | solution.py:171
  88.3 59.0 %all-to-all-start.1 = ((bf16[128,16,512]{2,1,0:T(8,128)(2,1)}), bf16[128,16,512]{2,1,0:T(8,128)(2,1)S(1)}, u32[]{:S(2)}, u32[]{:S(2)}) async-start(bf16[128,16,512]{2,1,0:T(8,128)(2,1)} %bitcast.58), calls=%async_computation.1 | async-start | bytes 4194304 | tf_op jit(solution)/shard_map/all_to_all | solution.py:221
  97.2 43.0 %copy-start.8 = (bf16[1024,512]{1,0:T(8,128)(2,1)S(1)}, bf16[1024,512]{1,0:T(8,128)(2,1)}, u32[]{:S(2)}) copy-start(bf16[1024,512]{1,0:T(8,128)(2,1)} %w_ref.5) | copy-start | bytes 3145732
  97.2 43.0 %copy-start.10 = (bf16[1024,512]{1,0:T(8,128)(2,1)S(1)}, bf16[1024,512]{1,0:T(8,128)(2,1)}, u32[]{:S(2)}) copy-start(bf16[1024,512]{1,0:T(8,128)(2,1)} %copy-done.9) | copy-start | bytes 3145732
  97.2 43.0 %copy-start.12 = (bf16[1024,512]{1,0:T(8,128)(2,1)S(1)}, bf16[1024,512]{1,0:T(8,128)(2,1)}, u32[]{:S(2)}) copy-start(bf16[1024,512]{1,0:T(8,128)(2,1)} %copy-done.11) | copy-start | bytes 3145732
  98.7 25.3 %collective-permute-start.1 = (bf16[4,4,8,512]{3,2,1,0:T(8,128)(2,1)S(1)}, bf16[4,4,8,512]{3,2,1,0:T(8,128)(2,1)S(1)}, u32[]{:S(2)}, u32[]{:S(2)}) collective-permute-start(bf16[4,4,8,512]{3,2,1,0:T(8,128)(2,1)S(1)} %get-tuple-element.29), channel_id=1, source_target_pairs={{0,32},{1,33},{2,34},{3,35},{4,36},{5,37},{6,38},{7,39},{8,40},{9,... | collective-permute-start | bytes 393224 | tf_op jit(solution)/shard_map/ppermute | solution.py:171
  100.2 25.2 %collective-permute-start.3 = (bf16[4,4,8,512]{3,2,1,0:T(8,128)(2,1)S(1)}, bf16[4,4,8,512]{3,2,1,0:T(8,128)(2,1)S(1)}, u32[]{:S(2)}, u32[]{:S(2)}) collective-permute-start(bf16[4,4,8,512]{3,2,1,0:T(8,128)(2,1)S(1)} %get-tuple-element.30), channel_id=1, source_target_pairs={{0,96},{1,97},{2,98},{3,99},{4,100},{5,101},{6,102},{7,103},{8,104... | collective-permute-start | bytes 393224 | tf_op jit(solution)/shard_map/ppermute | solution.py:171
  102.0 26.3 %collective-permute-start.2 = (bf16[4,4,8,512]{3,2,1,0:T(8,128)(2,1)S(1)}, bf16[4,4,8,512]{3,2,1,0:T(8,128)(2,1)S(1)}, u32[]{:S(2)}, u32[]{:S(2)}) collective-permute-start(bf16[4,4,8,512]{3,2,1,0:T(8,128)(2,1)S(1)} %get-tuple-element.31), channel_id=1, source_target_pairs={{0,64},{1,65},{2,66},{3,67},{4,68},{5,69},{6,70},{7,71},{8,72},{9,... | collective-permute-start | bytes 393224 | tf_op jit(solution)/shard_map/ppermute | solution.py:171
  128.4 3.7 %collective-permute-start.4 = (bf16[4,8,512]{2,1,0:T(8,128)(2,1)S(1)}, bf16[4,8,512]{2,1,0:T(8,128)(2,1)S(1)}, u32[]{:S(2)}, u32[]{:S(2)}) collective-permute-start(bf16[4,8,512]{2,1,0:T(8,128)(2,1)S(1)} %get-tuple-element.32), channel_id=1, source_target_pairs={{0,8},{1,9},{2,10},{3,11},{4,12},{5,13},{6,14},{7,15},{8,0},{9,1},... | collective-permute-start | bytes 98312 | tf_op jit(solution)/shard_map/ppermute | solution.py:171
  129.6 4.0 %collective-permute-start.6 = (bf16[4,8,512]{2,1,0:T(8,128)(2,1)S(1)}, bf16[4,8,512]{2,1,0:T(8,128)(2,1)S(1)}, u32[]{:S(2)}, u32[]{:S(2)}) collective-permute-start(bf16[4,8,512]{2,1,0:T(8,128)(2,1)S(1)} %get-tuple-element.33), channel_id=1, source_target_pairs={{0,24},{1,25},{2,26},{3,27},{4,28},{5,29},{6,30},{7,31},{8,16},{9,... | collective-permute-start | bytes 98312 | tf_op jit(solution)/shard_map/ppermute | solution.py:171
  131.4 4.3 %collective-permute-start.5 = (bf16[4,8,512]{2,1,0:T(8,128)(2,1)S(1)}, bf16[4,8,512]{2,1,0:T(8,128)(2,1)S(1)}, u32[]{:S(2)}, u32[]{:S(2)}) collective-permute-start(bf16[4,8,512]{2,1,0:T(8,128)(2,1)S(1)} %get-tuple-element.34), channel_id=1, source_target_pairs={{0,16},{1,17},{2,18},{3,19},{4,20},{5,21},{6,22},{7,23},{8,24},{9,... | collective-permute-start | bytes 98312 | tf_op jit(solution)/shard_map/ppermute | solution.py:171
  135.7 11.0 %collective-permute-start.7 = (bf16[8,512]{1,0:T(8,128)(2,1)S(1)}, bf16[8,512]{1,0:T(8,128)(2,1)S(1)}, u32[]{:S(2)}, u32[]{:S(2)}) collective-permute-start(bf16[8,512]{1,0:T(8,128)(2,1)S(1)} %get-tuple-element.35), channel_id=1, source_target_pairs={{0,2},{1,3},{2,0},{3,1},{4,6},{5,7},{6,4},{7,5},{8,10},{9,11},{10,... | collective-permute-start | bytes 24584 | tf_op jit(solution)/shard_map/ppermute | solution.py:171
  137.3 9.5 %collective-permute-start.9 = (bf16[8,512]{1,0:T(8,128)(2,1)S(1)}, bf16[8,512]{1,0:T(8,128)(2,1)S(1)}, u32[]{:S(2)}, u32[]{:S(2)}) collective-permute-start(bf16[8,512]{1,0:T(8,128)(2,1)S(1)} %get-tuple-element.36), channel_id=1, source_target_pairs={{0,6},{1,7},{2,4},{3,5},{4,2},{5,3},{6,0},{7,1},{8,14},{9,15},{10,... | collective-permute-start | bytes 24584 | tf_op jit(solution)/shard_map/ppermute | solution.py:171
  139.3 7.4 %collective-permute-start.8 = (bf16[8,512]{1,0:T(8,128)(2,1)S(1)}, bf16[8,512]{1,0:T(8,128)(2,1)S(1)}, u32[]{:S(2)}, u32[]{:S(2)}) collective-permute-start(bf16[8,512]{1,0:T(8,128)(2,1)S(1)} %get-tuple-element.37), channel_id=1, source_target_pairs={{0,4},{1,5},{2,6},{3,7},{4,0},{5,1},{6,2},{7,3},{8,12},{9,13},{10,... | collective-permute-start | bytes 24584 | tf_op jit(solution)/shard_map/ppermute | solution.py:171
  140.2 2.8 %copy-start.2 = (bf16[3072,1024]{1,0:T(8,128)(2,1)S(1)}, bf16[3072,1024]{1,0:T(8,128)(2,1)}, u32[]{:S(2)}) copy-start(bf16[3072,1024]{1,0:T(8,128)(2,1)} %get-tuple-element.14.at_ref) | copy-start | bytes 18874372
  147.4 1.6 %copy-start.1 = (f32[1024,512]{1,0:T(8,128)S(1)}, f32[1024,512]{1,0:T(8,128)}, u32[]{:S(2)}) copy-start(f32[1024,512]{1,0:T(8,128)} %copy-done) | copy-start | bytes 6291460
  149.0 2.2 %copy-start.3 = (bf16[1024,2048]{1,0:T(8,128)(2,1)S(1)}, bf16[1024,2048]{1,0:T(8,128)(2,1)}, u32[]{:S(2)}) copy-start(bf16[1024,2048]{1,0:T(8,128)(2,1)} %get-tuple-element.18.st_ref) | copy-start | bytes 12582916
  (16 other events, 18.4 us)

commit v2 on v1

v2 whole, which is shorter than its diff:
```python
import jax
import jax.numpy as jnp
from jax import lax
from jax.experimental import pallas as pl
from jax.experimental.pallas import tpu as pltpu
from jax.sharding import PartitionSpec as P

BF = jnp.bfloat16
F32 = jnp.float32
DEG = 8
AXES = ("row", "col")
VM = pl.BlockSpec(memory_space=pltpu.VMEM)
SM = pl.BlockSpec(memory_space=pltpu.SMEM)
HB = pl.BlockSpec(memory_space=pltpu.HBM)
MIB = 1024 * 1024


def iota(shape, dim):
    return lax.broadcasted_iota(jnp.int32, shape, dim)


def mm(a, b):
    return jnp.dot(a, b, preferred_element_type=F32)


def mm_last(a, b):
    return lax.dot_general(a, b, (((1,), (1,)), ((), ())), preferred_element_type=F32)


def mm_first(a, b):
    return lax.dot_general(a, b, (((0,), (0,)), ((), ())), preferred_element_type=F32)


def send_kernel(f_hbm, rows_hbm, count_hbm, hub_hbm, out_hbm, f_ref, rows_ref, count_ref, hub_ref, idx_ref, out_ref, sem, out_sem):
    loads = [
        pltpu.make_async_copy(src, dst, sem.at[i])
        for i, (src, dst) in enumerate(
            ((f_hbm, f_ref), (rows_hbm, rows_ref), (count_hbm, count_ref), (hub_hbm, hub_ref))
        )
    ]
    for copy in loads:
        copy.start()
    for copy in loads[1:]:
        copy.wait()
    parts = rows_ref.shape[1]
    nodes = f_ref.shape[0]
    live = iota((8, parts), 0) < count_ref[...]
    idx = jnp.where(live, rows_ref[...], -1).astype(F32)
    idx_ref[...] = idx.T
    hub = jnp.broadcast_to(hub_ref[...], (8, 8))
    hub_col = jnp.sum(jnp.where(iota((8, 8), 0) == iota((8, 8), 1), hub, 0), axis=1, keepdims=True)
    hub_hot = (iota((8, nodes), 1) == hub_col).astype(F32).astype(BF)
    loads[0].wait()
    hub_rows = mm(hub_hot, f_ref[...])
    step = 32
    stores = []
    for b in range(parts // step):
        blk = idx_ref[b * step : (b + 1) * step, :]
        wide = jnp.broadcast_to(blk[:, None, :], (step, 8, 8)).reshape(step * 8, 8)
        pick = iota((step * 8, 8), 0) % 8 == iota((step * 8, 8), 1)
        col = jnp.sum(jnp.where(pick, wide, 0.0), axis=1, keepdims=True).astype(jnp.int32)
        hot = (iota((step * 8, nodes), 1) == col).astype(F32).astype(BF)
        listed = mm(hot, f_ref[...]).reshape(step, 8, -1)
        both = jnp.concatenate(
            [listed, jnp.broadcast_to(hub_rows[None], (step, 8, hub_rows.shape[1]))], axis=1
        )
        at = slice(b * step, (b + 1) * step)
        out_ref[at] = both.astype(BF)
        stores.append(pltpu.make_async_copy(out_ref.at[at], out_hbm.at[at], out_sem.at[b]))
        stores[-1].start()
    for copy in stores:
        copy.wait()


def unique(t):
    keep, count = [], []
    for k in range(DEG):
        row = t[k : k + 1]
        total = jnp.zeros_like(row)
        seen = None
        for j in range(DEG):
            same = t[j : j + 1] == row
            total = total + jnp.where(same, 1.0, 0.0)
            if j < k:
                seen = same if seen is None else seen | same
        keep.append(row if seen is None else jnp.where(seen, -1.0, row))
        count.append(total)
    return jnp.concatenate(keep, axis=0), jnp.concatenate(count, axis=0)


def count_matrix(u, m, out_ref):
    span, lanes = 256, 512
    nodes = u.shape[1]
    for c in range(nodes // lanes):
        at = slice(c * lanes, (c + 1) * lanes)
        counts = [jnp.broadcast_to(m[k : k + 1, at], (16, lanes)).astype(BF) for k in range(DEG)]
        base = iota((16, lanes), 0).astype(F32).astype(BF)

        @pl.loop(0, out_ref.shape[0] // span)
        def _(b):
            near = jnp.clip(u[:, at] - (b * span).astype(F32), -1.0, float(span))
            names = [jnp.broadcast_to(near[k : k + 1], (16, lanes)).astype(BF) for k in range(DEG)]
            for h in range(span // 16):
                it = base + BF(h * 16)
                acc = jnp.zeros((16, lanes), BF)
                for k in range(DEG):
                    acc = jnp.where(it == names[k], counts[k], acc)
                out_ref[pl.ds(pl.multiple_of(b * span + h * 16, 16), 16), at] = acc


def launch(pairs, sems, first=0):
    copies = [pltpu.make_async_copy(src, dst, sems.at[first + i]) for i, (src, dst) in enumerate(pairs)]
    for copy in copies:
        copy.start()
    return copies


def hot_kernel(nb_ref, slot_ref, f_ref, w_ref, at_hbm, mix_hbm, st_hbm, mown_hbm, pre_hbm,
               at_ref, mix_ref, st_ref, mown_ref, pre_ref, sems):
    nodes, width = f_ref.shape
    halo = mix_ref.shape[0] // 2
    u, m = unique(nb_ref[...].astype(F32))
    w = u.astype(jnp.int32) - nodes
    is_hub = w >= halo
    v = jnp.where(is_hub, w - halo, w)
    v = (v // 8) * 16 + v % 8 + jnp.where(is_hub, 8, 0)
    count_matrix(jnp.where(w < 0, -1, v).astype(F32), m, mix_ref)
    copies = launch([(mix_ref, mix_hbm)], sems, 0)
    count_matrix(u, m, at_ref)
    copies += launch([(at_ref, at_hbm)], sems, 1)
    mown_ref[...] = mm_first(at_ref[:nodes, :], f_ref[...])
    pre_ref[...] = mm(f_ref[...], w_ref[:width, :])
    copies += launch([(mown_ref, mown_hbm), (pre_ref, pre_hbm)], sems, 2)
    slot = slot_ref[...]

    @pl.loop(0, nodes // 16)
    def _(b):
        it = iota((16, slot.shape[1]), 0) + b * 16
        st_ref[pl.ds(pl.multiple_of(b * 16, 16), 16), :] = (it == slot).astype(F32).astype(BF)

    copies += launch([(st_ref, st_hbm)], sems, 4)
    for copy in copies:
        copy.wait()


def mid_kernel(core_ref, recv_hbm, mix_hbm, at_hbm, mown_hbm, pre_hbm, w_hbm, f_hbm, cot_hbm,
               act_hbm, delta_hbm, gm_hbm, give_hbm, keep_hbm,
               recv_ref, mix_ref, hub_ref, mown_ref, pre_ref, w2_ref, f_ref, cot_ref,
               act_ref, delta_ref, gm_ref, give_ref, keep_ref, mean_ref, in_sem, out_sem):
    nodes, width = delta_ref.shape
    step = 256
    steps = nodes // step
    rows = [slice(b * step, (b + 1) * step) for b in range(steps)]
    loads = launch(
        [(recv_hbm, recv_ref), (mix_hbm.at[:, rows[0]], mix_ref.at[:, rows[0]]), (w_hbm.at[width:, :], w2_ref)], in_sem, 0
    )
    blocks = []
    for b, r in enumerate(rows):
        pairs = [(x.at[r, :], y.at[r, :]) for x, y in ((mown_hbm, mown_ref), (pre_hbm, pre_ref), (cot_hbm, cot_ref))]
        if b:
            pairs.append((mix_hbm.at[:, r], mix_ref.at[:, r]))
        blocks.append(launch(pairs, in_sem, 3 + 4 * b))
    late = launch([(at_hbm.at[at_hbm.shape[0] - hub_ref.shape[0] :, :], hub_ref), (f_hbm, f_ref)], in_sem, 3 + 4 * steps)
    for copy in loads:
        copy.wait()
    stores = []
    for b, r in enumerate(rows):
        for copy in blocks[b]:
            copy.wait()
        mean = ((mm_first(mix_ref[:, r], recv_ref[...]) + mown_ref[r, :]) / DEG).astype(BF)
        mean_ref[r, :] = mean
        pre = pre_ref[r, :] + mm(mean, w2_ref[...])
        sig = jax.nn.sigmoid(pre)
        act_ref[r, :] = (pre * sig).astype(BF)
        delta = (cot_ref[r, :].astype(F32) * sig * (1.0 + pre * (1.0 - sig))).astype(BF)
        delta_ref[r, :] = delta
        gm_ref[r, :] = (mm_last(delta, w2_ref[...]) / DEG).astype(BF)
        stores += launch(
            [(x.at[r, :], y.at[r, :]) for x, y in ((act_ref, act_hbm), (delta_ref, delta_hbm), (gm_ref, gm_hbm))], out_sem, 3 * b
        )
    for copy in late:
        copy.wait()
    last = 3 * steps

    def fill(hub, weight):
        hub_ref_out, hub_hbm = hub
        weight_ref, weight_hbm = weight
        hub_ref_out[...] = mm(hub_ref[...], gm_ref[...]).astype(hub_ref_out.dtype)
        done = launch([(hub_ref_out, hub_hbm)], out_sem, last)
        for i, x in enumerate((f_ref, mean_ref)):
            r = slice(i * width, (i + 1) * width)
            weight_ref[r, :] = mm_first(x[...], delta_ref[...]).astype(weight_ref.dtype)
            done += launch([(weight_ref.at[r, :], weight_hbm.at[r, :])], out_sem, last + 1 + i)
        for copy in done:
            copy.wait()

    @pl.when(core_ref[0] == 0)
    def _():
        fill((keep_ref, keep_hbm), (give_ref, give_hbm))

    @pl.when(core_ref[0] != 0)
    def _():
        fill((give_ref, give_hbm), (keep_ref, keep_hbm))

    for copy in stores:
        copy.wait()


def own_kernel(delta_hbm, gm_hbm, at_hbm, w_hbm, own_hbm, halo_hbm,
               delta_ref, gm_ref, at_ref, w1_ref, own_ref, halo_ref, sems):
    nodes, width = delta_ref.shape
    rest = at_ref.shape[0]
    loads = launch(
        [
            (gm_hbm, gm_ref),
            (at_hbm.at[nodes:rest, :], at_ref.at[nodes:, :]),
            (at_hbm.at[:nodes, :], at_ref.at[:nodes, :]),
            (delta_hbm, delta_ref),
            (w_hbm.at[:width, :], w1_ref),
        ],
        sems,
    )
    loads[0].wait()
    loads[1].wait()
    halo_ref[...] = mm(at_ref[nodes:, :], gm_ref[...]).astype(BF)
    stores = launch([(halo_ref, halo_hbm)], sems, 5)
    for copy in loads[2:]:
        copy.wait()
    own_ref[...] = mm(at_ref[:nodes, :], gm_ref[...]) + mm_last(delta_ref[...], w1_ref[...])
    stores += launch([(own_ref, own_hbm)], sems, 6)
    for copy in stores:
        copy.wait()


def pack_kernel(halo_hbm, keep_hbm, got_hbm, out_hbm, halo_ref, keep_ref, got_ref, out_ref, in_sem, out_sem):
    parts = out_ref.shape[0]
    width = out_ref.shape[2]
    step = 32
    rows = [slice(b * step * 8, (b + 1) * step * 8) for b in range(parts // step)]
    loads = [
        launch([(x.at[r, :], y.at[r, :]) for x, y in ((halo_hbm, halo_ref), (keep_hbm, keep_ref), (got_hbm, got_ref))], in_sem, 3 * b)
        for b, r in enumerate(rows)
    ]
    stores = []
    for b, r in enumerate(rows):
        for copy in loads[b]:
            copy.wait()
        total = keep_ref[r, :] + got_ref[r, :].astype(F32)
        both = jnp.concatenate(
            [halo_ref[r, :].astype(F32).reshape(step, 8, width), total.reshape(step, 8, width)], axis=1
        )
        at = slice(b * step, (b + 1) * step)
        out_ref[at] = both.astype(BF)
        stores += launch([(out_ref.at[at], out_hbm.at[at])], out_sem, b)
    for copy in stores:
        copy.wait()


def last_kernel(st_ref, back_ref, own_ref, out_ref, weight_ref):
    out_ref[...] = (own_ref[...] + mm(st_ref[...], back_ref[...])).astype(BF)
    shape = (8, back_ref.shape[0])
    row = iota(shape, 1)
    odd = (row // 16) % 2 == 1
    take = jnp.where(odd & (row % 16 == iota(shape, 0) + 8), 1.0, 0.0).astype(BF)
    weight_ref[...] = mm(take, back_ref[...])


def call(kernel, ins, outs, scratch=(), flops=0, read=0, mib=60, in_specs=None, out_specs=None):
    return pl.pallas_call(
        kernel,
        out_shape=[jax.ShapeDtypeStruct(s, d) for s, d in outs],
        in_specs=in_specs or [HB] * len(ins),
        out_specs=out_specs or [HB] * len(outs),
        scratch_shapes=[pltpu.VMEM(*x) if isinstance(x, tuple) else x for x in scratch],
        compiler_params=pltpu.CompilerParams(vmem_limit_bytes=mib * MIB),
        cost_estimate=pl.CostEstimate(flops=flops, bytes_accessed=read, transcendentals=0),
    )(*ins)


def local(features, weights, cotangent, neighbours, send_rows, send_count, hub_local):
    nodes, width = features.shape
    parts = lax.axis_size(AXES)
    halo = parts * 8
    table = nodes + 2 * halo
    core = (lax.axis_index("col") % 2).astype(jnp.int32).reshape(1)
    sems = lambda n: pltpu.SemaphoreType.DMA((n,))
    wide, half = ((nodes, width), F32), ((nodes, width), BF)
    packed = ((parts, 16, width), BF)

    (pay,) = call(
        send_kernel,
        [features, send_rows[0].T, send_count, hub_local],
        [packed],
        [half, ((8, parts), jnp.int32), ((1, parts), jnp.int32), ((1, 8), jnp.int32), ((parts, 8), F32), packed, sems(4), sems(parts // 32)],
        flops=2 * nodes * halo * width, read=3 * MIB,
    )
    recv = lax.all_to_all(pay, AXES, split_axis=0, concat_axis=0, tiled=True).reshape(2 * halo, width)

    live = iota((parts, 8), 1) < send_count[0][:, None]
    even = iota((parts, 8), 0) % 2 == 0
    slot = jnp.concatenate(
        [jnp.where(live, send_rows[0], -1), jnp.where(even, hub_local, -1)], axis=1
    ).reshape(1, 2 * halo)
    hot = [((table, nodes), BF), ((2 * halo, nodes), BF), ((nodes, 2 * halo), BF), wide, wide]
    at, mix, st, mean_own, pre_own = call(
        hot_kernel, [neighbours.T, slot, features, weights], hot, hot + [sems(5)],
        flops=14 * 10**9, read=20 * MIB, in_specs=[VM] * 4,
    )
    mid = [half, half, half, ((2 * width, width), BF), ((2 * width, width), F32)]
    act, delta, gm, give, keep = call(
        mid_kernel,
        [core, recv, mix, at, mean_own, pre_own, weights, features, cotangent],
        mid,
        [((2 * halo, width), BF), ((2 * halo, nodes), BF), ((halo, nodes), BF), wide, wide, ((width, width), BF), half, half]
        + mid + [half, sems(21), sems(15)],
        flops=6 * 10**9, read=16 * MIB,
        in_specs=[SM] + [HB] * 8,
    )
    got = lax.ppermute(give, AXES, [(i, i ^ 1) for i in range(parts)])
    own_out = [wide, ((halo, width), BF)]
    own, halo_grad = call(
        own_kernel, [delta, gm, at, weights], own_out,
        [half, half, ((nodes + halo, nodes), BF), ((width, width), BF)] + own_out + [sems(7)],
        flops=3 * 10**9, read=8 * MIB,
    )
    (pay_back,) = call(
        pack_kernel, [halo_grad, keep, got], [packed],
        [((halo, width), BF), ((halo, width), F32), ((halo, width), BF), packed, sems(3 * parts // 32), sems(parts // 32)],
        flops=10**6, read=6 * MIB,
    )
    back = lax.all_to_all(pay_back, AXES, split_axis=0, concat_axis=0, tiled=True).reshape(2 * halo, width)
    grad, grad_weights = call(
        last_kernel, [st, back, own], [half, ((8, width), F32)], flops=2 * 10**9, read=8 * MIB, mib=16,
        in_specs=[VM] * 3, out_specs=[VM] * 2,
    )
    return act, grad, grad_weights


def solution(mesh):
    both = P(AXES, None)
    placed = (both, P(), both, both, P(AXES, None, None), both, both)
    return jax.shard_map(local, mesh=mesh, in_specs=placed, out_specs=(both, both, both), check_vma=False)
```

time: 157 us -> 109 us (0.69); the launches traced: 155 us -> 109 us
  blocking collectives: 0 us -> 34.8 us
  local copies, waits for them, and re-layouts: 28.1 us -> 3.12 us
  starting transfers between devices: 33.4 us -> 12.8 us
  Pallas kernels: 61 us -> 41.8 us
  waiting for transfers between devices: 29.3 us -> 15.8 us
  other arithmetic: 2.18 us -> 0.09 us
    all_to_all x0 -> x1, blocking collectives: none -> 34.8 us  [local(): lax.all_to_all(pay_back, AXES, split_axis=0, concat_axis=0, tiled=True)]
    ppermute x10 -> x1, waiting for transfers between devices: 29.3 us -> 0.01 us  [local(): got = lax.ppermute(give, AXES, [(i, i ^ 1) for i in range(parts)])]
    unnamed x56 -> x14, local copies, waits for them, and re-layouts: 27 us -> 2.33 us
    pallas_call x5 -> x6, Pallas kernels: 61 us -> 41.8 us  [call(): pl.pallas_call(kernel, out_shape=[jax.ShapeDtypeStruct(s, d) for s, d in...]
    all_to_all x1, waiting for transfers between devices: 0.01 us -> 15.8 us  [local(): lax.all_to_all(pay, AXES, split_axis=0, concat_axis=0, tiled=True)]
    ppermute x10 -> x1, starting transfers between devices: 13.1 us -> 1.25 us  [local(): got = lax.ppermute(give, AXES, [(i, i ^ 1) for i in range(parts)])]
    all_to_all x1 -> x0, starting transfers between devices: 8.86 us -> none  [local(): lax.all_to_all(back.reshape(parts, 16, width), AXES, split_axis=0, concat...]
    add x2 -> x0, other arithmetic: 2.02 us -> none  [the longest x1 1.41 us: local(): blocks[:, :, :, 0].astype(F32)]
  transfers between devices with their start and end apart: 12 -> 2, of which waited for: 5 -> 1; matrix products, arithmetic and copies ran while one was open for 2% -> 1% of each run, Pallas kernels for 25% -> 18%
where the time goes in v2:
time: 109 us
  Pallas kernels  41.8 us (38%)
  blocking collectives  34.8 us (32%)
  waiting for transfers between devices  15.8 us (14%)
  starting transfers between devices  12.8 us (12%)
  local copies, waits for them, and re-layouts  3.12 us (3%)
    pallas_call x6, Pallas kernels, call(): pl.pallas_call(kernel, out_shape=[jax.ShapeDtypeStruct(s, d) for s, d in...  41.8 us
    all_to_all x1, blocking collectives, local(): lax.all_to_all(pay_back, AXES, split_axis=0, concat_axis=0, tiled=True)  34.8 us
    all_to_all x1, waiting for transfers between devices, local(): lax.all_to_all(pay, AXES, split_axis=0, concat_axis=0, tiled=True)  15.8 us
    all_to_all x1, starting transfers between devices, local(): lax.all_to_all(pay, AXES, split_axis=0, concat_axis=0, tiled=True)  11.5 us
    unnamed x14, local copies, waits for them, and re-layouts  2.33 us
  transfers between devices with their start and end apart: 2, of which 1 were waited for; matrix products, arithmetic and copies ran while one was open for 1% of the time, Pallas kernels for 18%

profile of v2, /device:TPU:1, one launch (start us, length us, event | category | flops | bytes accessed | tf_op | source)
XLA Modules:
  0.0 109.1 jit_solution(12505098955854255506)
XLA Ops:
  0.6 3.8 %shard_map.94 = bf16[128,16,512]{2,1,0:T(8,128)(2,1)} custom-call(bf16[1024,512]{1,0:T(8,128)(2,1)} %f_hbm.3, s32[8,128]{1,0:T(8,128)} %bitcast.12, s32[1,128]{1,0:T(1,128)} %count_hbm.1, s32[1,8]{1,0:T(1,128)} %hub_hbm.1), custom_call_target="tpu_custom_call" | custom-call | flops 1073741824 | bytes 3145728 | tf_op jit(solution)/shard_map/pallas_call | solution.py:269
  4.4 0.0 copy-start.5
  4.4 0.0 copy-start.4
  4.4 0.0 copy-start.6
  4.5 11.5 %all-to-all-start = ((bf16[128,16,512]{2,1,0:T(8,128)(2,1)}), bf16[128,16,512]{2,1,0:T(8,128)(2,1)S(1)}, u32[]{:S(2)}, u32[]{:S(2)}) async-start(bf16[128,16,512]{2,1,0:T(8,128)(2,1)} %shard_map.94), calls=%async_computation | async-start | bytes 4194304 | tf_op jit(solution)/shard_map/all_to_all | solution.py:297
  16.0 0.0 copy-done.5
  16.0 0.1 fusion
  16.1 0.0 copy-done.4
  16.1 0.0 copy-done.6
  16.1 0.1 copy.11
  16.2 0.7 reshape.21.slot_ref
  16.9 13.8 %shard_map.95 = (bf16[3072,1024]{1,0:T(8,128)(2,1)}, bf16[2048,1024]{1,0:T(8,128)(2,1)}, bf16[1024,2048]{1,0:T(8,128)(2,1)}, f32[1024,512]{1,0:T(8,128)}, f32[1024,512]{1,0:T(8,128)}) custom-call(s32[8,1024]{1,0:T(8,128)} %bitcast.15, s32[1,2048]{1,0:T(1,128)} %reshape.21.slot_ref, bf16[1024,512]{1,0:T(8,128)(2,1)} %f_hbm.3, bf16[1024,512]{1,0:T(8,128)(2,1)} %w_hbm.3), custom_call_target="tpu_custom_call" | custom-call | flops 14000000000 | bytes 20971520 | tf_op jit(solution)/shard_map/pallas_call | solution.py:269
  30.7 15.8 %all-to-all-done = bf16[128,16,512]{2,1,0:T(8,128)(2,1)S(1)} async-done(((bf16[128,16,512]{2,1,0:T(8,128)(2,1)}), bf16[128,16,512]{2,1,0:T(8,128)(2,1)S(1)}, u32[]{:S(2)}, u32[]{:S(2)}) %all-to-all-start) | async-done | bytes 2097184 | tf_op jit(solution)/shard_map/all_to_all | solution.py:297
  46.5 1.3 %copy-done.2 = bf16[128,16,512]{2,1,0:T(8,128)(2,1)} copy-done((bf16[128,16,512]{2,1,0:T(8,128)(2,1)}, bf16[128,16,512]{2,1,0:T(8,128)(2,1)S(1)}, u32[]{:S(2)}) %copy-start.2) | copy-done | bytes 2097176
  47.8 11.2 %shard_map.96 = (bf16[1024,512]{1,0:T(8,128)(2,1)}, bf16[1024,512]{1,0:T(8,128)(2,1)}, bf16[1024,512]{1,0:T(8,128)(2,1)}, bf16[1024,512]{1,0:T(8,128)(2,1)}, f32[1024,512]{1,0:T(8,128)}) custom-call(s32[1]{0:T(128)} %bitcast.core_ref, bf16[2048,512]{1,0:T(8,128)(2,1)} %bitcast.11, bf16[2048,1024]{1,0:T(8,128)(2,1)} %get-tuple-element.17.mix_hbm, ...), custom_call_target="tpu_custom_call" | custom-call | flops 6000000000 | bytes 16777216 | tf_op jit(solution)/shard_map/pallas_call | solution.py:269
  59.1 1.2 %collective-permute-start = (bf16[1024,512]{1,0:T(8,128)(2,1)}, bf16[1024,512]{1,0:T(8,128)(2,1)S(1)}, u32[]{:S(2)}, u32[]{:S(2)}) collective-permute-start(bf16[1024,512]{1,0:T(8,128)(2,1)} %get-tuple-element.27), channel_id=1, source_target_pairs={{0,1},{1,0},{2,3},{3,2},{4,5},{5,4},{6,7},{7,6},{8,9},{9,8},{10,11... | collective-permute-start | bytes 3145736 | tf_op jit(solution)/shard_map/ppermute | solution.py:319
  60.3 6.4 %shard_map.97 = (f32[1024,512]{1,0:T(8,128)}, bf16[1024,512]{1,0:T(8,128)(2,1)}) custom-call(bf16[1024,512]{1,0:T(8,128)(2,1)} %get-tuple-element.23.delta_hbm, bf16[1024,512]{1,0:T(8,128)(2,1)} %get-tuple-element.24.gm_hbm, bf16[3072,1024]{1,0:T(8,128)(2,1)} %get-tuple-element.18.at_hbm, bf16[1024,512]{1,0:T(8,128)(2,1)} %w_hbm.3), custom_call_target="tpu_custom_call" | custom-call | flops 3000000000 | bytes 8388608 | tf_op jit(solution)/shard_map/pallas_call | solution.py:269
  66.7 0.0 collective-permute-done.got_hbm
  66.7 0.0 copy-start.3
  66.7 1.0 copy-done.3
  67.7 3.3 %shard_map.98 = bf16[128,16,512]{2,1,0:T(8,128)(2,1)} custom-call(bf16[1024,512]{1,0:T(8,128)(2,1)} %get-tuple-element.25.halo_hbm, f32[1024,512]{1,0:T(8,128)} %get-tuple-element.26.keep_hbm, bf16[1024,512]{1,0:T(8,128)(2,1)} %copy-done.3), custom_call_target="tpu_custom_call" | custom-call | flops 1000000 | bytes 6291456 | tf_op jit(solution)/shard_map/pallas_call | solution.py:269
  71.0 0.0 copy-start
  71.0 34.8 %all_to_all.10 = bf16[128,16,512]{2,1,0:T(8,128)(2,1)S(1)} all-to-all(bf16[128,16,512]{2,1,0:T(8,128)(2,1)} %shard_map.98), channel_id=1, replica_groups=mesh['row'=16,'col'=8] {'row','col'}, dimensions={0} | all-to-all | bytes 4194304 | tf_op jit(solution)/shard_map/all_to_all | solution.py:331
  105.8 3.3 %shard_map.99 = (bf16[1024,512]{1,0:T(8,128)(2,1)}, f32[8,512]{1,0:T(8,128)}) custom-call(bf16[1024,2048]{1,0:T(8,128)(2,1)S(1)} %copy-done, bf16[2048,512]{1,0:T(8,128)(2,1)S(1)} %bitcast.10, f32[1024,512]{1,0:T(8,128)S(1)} %copy-done.1), custom_call_target="tpu_custom_call" | custom-call | flops 2000000000 | bytes 8388608 | tf_op jit(solution)/shard_map/pallas_call | solution.py:269
  (8 shorter events, 0.0 us)
Async XLA Ops:
  4.4 11.6 %copy-start.5 = (s32[1,8]{1,0:T(1,128)S(1)}, s32[1,8]{1,0:T(1,128)}, u32[]{:S(2)}) copy-start(s32[1,8]{1,0:T(1,128)} %hub_hbm.1) | copy-start | bytes 100
  4.4 11.6 %copy-start.4 = (s32[1,128,8]{1,2,0:T(8,128)S(1)}, s32[1,128,8]{1,2,0:T(8,128)}, u32[]{:S(2)}) copy-start(s32[1,128,8]{1,2,0:T(8,128)} %param.11) | copy-start | bytes 12292
  4.4 11.6 %copy-start.6 = (s32[1,128]{1,0:T(1,128)S(1)}, s32[1,128]{1,0:T(1,128)}, u32[]{:S(2)}) copy-start(s32[1,128]{1,0:T(1,128)} %count_hbm.1) | copy-start | bytes 1540
  4.5 42.0 %all-to-all-start = ((bf16[128,16,512]{2,1,0:T(8,128)(2,1)}), bf16[128,16,512]{2,1,0:T(8,128)(2,1)S(1)}, u32[]{:S(2)}, u32[]{:S(2)}) async-start(bf16[128,16,512]{2,1,0:T(8,128)(2,1)} %shard_map.94), calls=%async_computation | async-start | bytes 4194304 | tf_op jit(solution)/shard_map/all_to_all | solution.py:297
  46.5 1.3 %copy-start.2 = (bf16[128,16,512]{2,1,0:T(8,128)(2,1)}, bf16[128,16,512]{2,1,0:T(8,128)(2,1)S(1)}, u32[]{:S(2)}) copy-start(bf16[128,16,512]{2,1,0:T(8,128)(2,1)S(1)} %all-to-all-done) | copy-start | bytes 6291460
  59.1 7.6 %collective-permute-start = (bf16[1024,512]{1,0:T(8,128)(2,1)}, bf16[1024,512]{1,0:T(8,128)(2,1)S(1)}, u32[]{:S(2)}, u32[]{:S(2)}) collective-permute-start(bf16[1024,512]{1,0:T(8,128)(2,1)} %get-tuple-element.27), channel_id=1, source_target_pairs={{0,1},{1,0},{2,3},{3,2},{4,5},{5,4},{6,7},{7,6},{8,9},{9,8},{10,11... | collective-permute-start | bytes 3145736 | tf_op jit(solution)/shard_map/ppermute | solution.py:319
  66.7 1.0 copy-start.3
  67.7 38.1 %copy-start.1 = (f32[1024,512]{1,0:T(8,128)S(1)}, f32[1024,512]{1,0:T(8,128)}, u32[]{:S(2)}) copy-start(f32[1024,512]{1,0:T(8,128)} %get-tuple-element.28.own_ref) | copy-start | bytes 6291460
  71.0 34.8 %copy-start = (bf16[1024,2048]{1,0:T(8,128)(2,1)S(1)}, bf16[1024,2048]{1,0:T(8,128)(2,1)}, u32[]{:S(2)}) copy-start(bf16[1024,2048]{1,0:T(8,128)(2,1)} %get-tuple-element.22.st_ref) | copy-start | bytes 12582916

commit v3 on v2

v3 whole, which is shorter than its diff:
```python
import jax
import jax.numpy as jnp
from jax import lax
from jax.experimental import pallas as pl
from jax.experimental.pallas import tpu as pltpu
from jax.sharding import PartitionSpec as P

BF = jnp.bfloat16
F32 = jnp.float32
DEG = 8
AXES = ("row", "col")
VM = pl.BlockSpec(memory_space=pltpu.VMEM)
SM = pl.BlockSpec(memory_space=pltpu.SMEM)
HB = pl.BlockSpec(memory_space=pltpu.HBM)
MIB = 1024 * 1024


def iota(shape, dim):
    return lax.broadcasted_iota(jnp.int32, shape, dim)


def mm(a, b):
    return jnp.dot(a, b, preferred_element_type=F32)


def mm_last(a, b):
    return lax.dot_general(a, b, (((1,), (1,)), ((), ())), preferred_element_type=F32)


def mm_first(a, b):
    return lax.dot_general(a, b, (((0,), (0,)), ((), ())), preferred_element_type=F32)


def send_kernel(f_hbm, rows_hbm, count_hbm, hub_hbm, out_hbm, f_ref, rows_ref, count_ref, hub_ref, idx_ref, out_ref, sem, out_sem):
    loads = [
        pltpu.make_async_copy(src, dst, sem.at[i])
        for i, (src, dst) in enumerate(
            ((f_hbm, f_ref), (rows_hbm, rows_ref), (count_hbm, count_ref), (hub_hbm, hub_ref))
        )
    ]
    for copy in loads:
        copy.start()
    for copy in loads[1:]:
        copy.wait()
    parts = rows_ref.shape[1]
    nodes = f_ref.shape[0]
    live = iota((8, parts), 0) < count_ref[...]
    idx = jnp.where(live, rows_ref[...], -1).astype(F32)
    idx_ref[...] = idx.T
    hub = jnp.broadcast_to(hub_ref[...], (8, 8))
    hub_col = jnp.sum(jnp.where(iota((8, 8), 0) == iota((8, 8), 1), hub, 0), axis=1, keepdims=True)
    hub_hot = (iota((8, nodes), 1) == hub_col).astype(F32).astype(BF)
    loads[0].wait()
    hub_rows = mm(hub_hot, f_ref[...])
    step = 32
    stores = []
    for b in range(parts // step):
        blk = idx_ref[b * step : (b + 1) * step, :]
        wide = jnp.broadcast_to(blk[:, None, :], (step, 8, 8)).reshape(step * 8, 8)
        pick = iota((step * 8, 8), 0) % 8 == iota((step * 8, 8), 1)
        col = jnp.sum(jnp.where(pick, wide, 0.0), axis=1, keepdims=True).astype(jnp.int32)
        hot = (iota((step * 8, nodes), 1) == col).astype(F32).astype(BF)
        listed = mm(hot, f_ref[...]).reshape(step, 8, -1)
        both = jnp.concatenate(
            [listed, jnp.broadcast_to(hub_rows[None], (step, 8, hub_rows.shape[1]))], axis=1
        )
        at = slice(b * step, (b + 1) * step)
        out_ref[at] = both.astype(BF)
        stores.append(pltpu.make_async_copy(out_ref.at[at], out_hbm.at[at], out_sem.at[b]))
        stores[-1].start()
    for copy in stores:
        copy.wait()


def unique(t):
    keep, count = [], []
    for k in range(DEG):
        row = t[k : k + 1]
        total = jnp.zeros_like(row)
        seen = None
        for j in range(DEG):
            same = t[j : j + 1] == row
            total = total + jnp.where(same, 1.0, 0.0)
            if j < k:
                seen = same if seen is None else seen | same
        keep.append(row if seen is None else jnp.where(seen, -1.0, row))
        count.append(total)
    return jnp.concatenate(keep, axis=0), jnp.concatenate(count, axis=0)


def count_matrix(u, m, outs):
    span = 256
    first = 0
    for out_ref in outs:
        lanes = out_ref.shape[1]
        at = slice(first, first + lanes)
        first += lanes
        counts = [jnp.broadcast_to(m[k : k + 1, at], (16, lanes)).astype(BF) for k in range(DEG)]
        base = iota((16, lanes), 0).astype(F32).astype(BF)

        @pl.loop(0, out_ref.shape[0] // span)
        def _(b):
            near = jnp.clip(u[:, at] - (b * span).astype(F32), -1.0, float(span))
            names = [jnp.broadcast_to(near[k : k + 1], (16, lanes)).astype(BF) for k in range(DEG)]
            for h in range(0, span, 16):
                it = base + BF(h)
                acc = jnp.zeros((16, lanes), BF)
                for k in range(DEG):
                    acc = jnp.where(it == names[k], counts[k], acc)
                out_ref[pl.ds(pl.multiple_of(b * span + h, 16), 16), :] = acc


def launch(pairs, sems, first=0):
    copies = [pltpu.make_async_copy(src, dst, sems.at[first + i]) for i, (src, dst) in enumerate(pairs)]
    for copy in copies:
        copy.start()
    return copies


def hot_kernel(nb_ref, slot_ref, f_ref, own_hbm, listed_hbm, hub_hbm, mix_hbm, st_hbm, mown_hbm,
               own_ref, listed_ref, hub_ref, mix_ref, st_ref, mown_ref, sems):
    nodes = f_ref.shape[0]
    halo = hub_ref.shape[0]
    half = nodes // 2
    cols = [slice(0, half), slice(half, nodes)]
    u, m = unique(nb_ref[...].astype(F32))
    w = u.astype(jnp.int32) - nodes
    is_hub = w >= halo
    v = jnp.where(is_hub, w - halo, w)
    v = (v // 8) * 16 + v % 8 + jnp.where(is_hub, 8, 0)
    count_matrix(jnp.where(w < 0, -1, v).astype(F32), m, [mix_ref.at[c] for c in range(mix_ref.shape[0])])
    copies = launch([(mix_ref, mix_hbm)], sems, 0)
    count_matrix(u, m, [own_ref.at[:, c] for c in cols])
    mown_ref[...] = mm_first(own_ref[...], f_ref[...])
    copies += launch([(own_ref, own_hbm), (mown_ref, mown_hbm)], sems, 1)
    count_matrix(u - nodes, m, [listed_ref.at[:, c] for c in cols])
    count_matrix(u - (nodes + halo), m, [hub_ref.at[:, c] for c in cols])
    copies += launch([(listed_ref, listed_hbm), (hub_ref, hub_hbm)], sems, 3)
    slot = slot_ref[...]

    @pl.loop(0, nodes // 16)
    def _(b):
        it = iota((16, slot.shape[1]), 0) + b * 16
        st_ref[pl.ds(pl.multiple_of(b * 16, 16), 16), :] = (it == slot).astype(F32).astype(BF)

    copies += launch([(st_ref, st_hbm)], sems, 5)
    for copy in copies:
        copy.wait()


def mid_kernel(core_ref, recv_hbm, mix_hbm, at_hbm, mown_hbm, w_hbm, f_hbm, cot_hbm,
               act_hbm, delta_hbm, gm_hbm, mean_hbm, give_hbm,
               recv_ref, mix_ref, hub_ref, mown_ref, w_ref, f_ref, cot_ref, pre_ref,
               act_ref, delta_ref, gm_ref, mean_ref, give_ref, in_sem, out_sem):
    nodes, width = delta_ref.shape
    step = 256
    steps = nodes // step
    rows = [slice(b * step, (b + 1) * step) for b in range(steps)]
    early = launch([(w_hbm, w_ref), (f_hbm, f_ref)], in_sem, 0)
    loads = launch([(recv_hbm, recv_ref)], in_sem, 2)
    blocks = []
    for b, r in enumerate(rows):
        pairs = [(mix_hbm.at[b], mix_ref.at[b]), (mown_hbm.at[r, :], mown_ref.at[r, :]), (cot_hbm.at[r, :], cot_ref.at[r, :])]
        blocks.append(launch(pairs, in_sem, 3 + 3 * b))
    first = at_hbm.shape[0] - hub_ref.shape[0]
    hub_load = pltpu.make_async_copy(at_hbm.at[first:, :], hub_ref, in_sem.at[3 + 3 * steps])

    @pl.when(core_ref[0] != 0)
    def _():
        hub_load.start()

    for copy in early:
        copy.wait()
    pre_ref[...] = mm(f_ref[...], w_ref[:width, :])
    for copy in loads:
        copy.wait()
    w2 = w_ref[width:, :]
    stores = []
    for b, r in enumerate(rows):
        for copy in blocks[b]:
            copy.wait()
        mean = ((mm_first(mix_ref[b], recv_ref[...]) + mown_ref[r, :]) / DEG).astype(BF)
        mean_ref[r, :] = mean
        pre = pre_ref[r, :] + mm(mean, w2)
        sig = jax.nn.sigmoid(pre)
        act_ref[r, :] = (pre * sig).astype(BF)
        delta = (cot_ref[r, :].astype(F32) * sig * (1.0 + pre * (1.0 - sig))).astype(BF)
        delta_ref[r, :] = delta
        gm_ref[r, :] = (mm_last(delta, w2) / DEG).astype(BF)
        stores += launch(
            [(x.at[r, :], y.at[r, :]) for x, y in
             ((gm_ref, gm_hbm), (act_ref, act_hbm), (delta_ref, delta_hbm), (mean_ref, mean_hbm))],
            out_sem, 4 * b,
        )
    half = width
    tops = [slice(0, half), slice(half, 2 * half)]

    @pl.when(core_ref[0] == 0)
    def _():
        for i, (r, x) in enumerate(zip(tops, (f_ref, mean_ref))):
            give_ref[r, :] = mm_first(x[...], delta_ref[...]).astype(BF)
            pltpu.make_async_copy(give_ref.at[r, :], give_hbm.at[r, :], out_sem.at[4 * steps + i]).start()

    @pl.when(core_ref[0] != 0)
    def _():
        hub_load.wait()
        for i, r in enumerate(tops):
            give_ref[r, :] = mm(hub_ref[r, :], gm_ref[...]).astype(BF)
            pltpu.make_async_copy(give_ref.at[r, :], give_hbm.at[r, :], out_sem.at[4 * steps + i]).start()

    for i, r in enumerate(tops):
        pltpu.make_async_copy(give_ref.at[r, :], give_hbm.at[r, :], out_sem.at[4 * steps + i]).wait()
    for copy in stores:
        copy.wait()


def keep_kernel(core_ref, gm_hbm, at_hbm, f_hbm, mean_hbm, delta_hbm, keep_hbm,
                gm_ref, at_ref, f_ref, mean_ref, delta_ref, keep_ref, in_sem, out_sem):
    nodes, width = f_ref.shape
    halo = at_ref.shape[0]
    tops = [slice(0, width), slice(width, 2 * width)]

    @pl.when(core_ref[0] == 0)
    def _():
        first = at_hbm.shape[0] - halo
        loads = launch([(gm_hbm, gm_ref)] + [(at_hbm.at[first + r.start : first + r.stop, :], at_ref.at[r, :]) for r in tops], in_sem)
        loads[0].wait()
        stores = []
        for i, r in enumerate(tops):
            loads[1 + i].wait()
            keep_ref[r, :] = mm(at_ref[r, :], gm_ref[...])
            stores += launch([(keep_ref.at[r, :], keep_hbm.at[r, :])], out_sem, i)
        for copy in stores:
            copy.wait()

    @pl.when(core_ref[0] != 0)
    def _():
        loads = launch([(delta_hbm, delta_ref), (f_hbm, f_ref), (mean_hbm, mean_ref)], in_sem)
        loads[0].wait()
        stores = []
        for i, (r, x) in enumerate(zip(tops, (f_ref, mean_ref))):
            loads[1 + i].wait()
            keep_ref[r, :] = mm_first(x[...], delta_ref[...])
            stores += launch([(keep_ref.at[r, :], keep_hbm.at[r, :])], out_sem, i)
        for copy in stores:
            copy.wait()


def pack_kernel(gm_ref, at_ref, keep_hbm, got_ref, out_ref, keep_ref, sems):
    parts = out_ref.shape[0]
    width = out_ref.shape[2]
    step = 32
    rows = [slice(b * step * 8, (b + 1) * step * 8) for b in range(parts // step)]
    loads = launch([(keep_hbm.at[r, :], keep_ref.at[r, :]) for r in rows], sems)
    for b, r in enumerate(rows):
        listed = mm(at_ref[r, :], gm_ref[...])
        loads[b].wait()
        total = keep_ref[r, :] + got_ref[r, :].astype(F32)
        both = jnp.concatenate([listed.reshape(step, 8, width), total.reshape(step, 8, width)], axis=1)
        out_ref[b * step : (b + 1) * step] = both.astype(BF)


def last_kernel(st_ref, back_ref, at_ref, gm_ref, delta_ref, w_ref, out_hbm, weight_ref, out_ref, sems):
    width = out_ref.shape[1]
    step = 256
    shape = (8, back_ref.shape[0])
    row = iota(shape, 1)
    odd = (row // 16) % 2 == 1
    take = jnp.where(odd & (row % 16 == iota(shape, 0) + 8), 1.0, 0.0).astype(BF)
    weight_ref[...] = mm(take, back_ref[...])
    stores = []
    for b in range(out_ref.shape[0] // step):
        r = slice(b * step, (b + 1) * step)
        own = mm(at_ref[r, :], gm_ref[...]) + mm_last(delta_ref[r, :], w_ref[:width, :])
        out_ref[r, :] = (own + mm(st_ref[r, :], back_ref[...])).astype(BF)
        stores += launch([(out_ref.at[r, :], out_hbm.at[r, :])], sems, b)
    for copy in stores:
        copy.wait()


def call(kernel, ins, outs, scratch=(), flops=0, read=0, mib=60, in_specs=None, out_specs=None):
    return pl.pallas_call(
        kernel,
        out_shape=[jax.ShapeDtypeStruct(s, d) for s, d in outs],
        in_specs=in_specs or [HB] * len(ins),
        out_specs=out_specs or [HB] * len(outs),
        scratch_shapes=[pltpu.VMEM(*x) if isinstance(x, tuple) else x for x in scratch],
        compiler_params=pltpu.CompilerParams(vmem_limit_bytes=mib * MIB),
        cost_estimate=pl.CostEstimate(flops=flops, bytes_accessed=read, transcendentals=0),
    )(*ins)


def local(features, weights, cotangent, neighbours, send_rows, send_count, hub_local):
    nodes, width = features.shape
    parts = lax.axis_size(AXES)
    halo = parts * 8
    core = (lax.axis_index("col") % 2).astype(jnp.int32).reshape(1)
    sems = lambda n: pltpu.SemaphoreType.DMA((n,))
    wide, half = ((nodes, width), F32), ((nodes, width), BF)
    packed = ((parts, 16, width), BF)

    (pay,) = call(
        send_kernel,
        [features, send_rows[0].T, send_count, hub_local],
        [packed],
        [half, ((8, parts), jnp.int32), ((1, parts), jnp.int32), ((1, 8), jnp.int32), ((parts, 8), F32), packed, sems(4), sems(parts // 32)],
        flops=2 * nodes * halo * width, read=3 * MIB,
    )
    recv = lax.all_to_all(pay, AXES, split_axis=0, concat_axis=0, tiled=True).reshape(2 * halo, width)

    live = iota((parts, 8), 1) < send_count[0][:, None]
    even = iota((parts, 8), 0) % 2 == 0
    slot = jnp.concatenate(
        [jnp.where(live, send_rows[0], -1), jnp.where(even, hub_local, -1)], axis=1
    ).reshape(1, 2 * halo)
    square = ((nodes, nodes), BF)
    hot = [square, ((halo, nodes), BF), ((halo, nodes), BF), ((4, 2 * halo, nodes // 4), BF), ((nodes, 2 * halo), BF), wide]
    at_own, at_halo, at, mix, st, mean_own = call(
        hot_kernel, [neighbours.T, slot, features], hot, hot + [sems(6)],
        flops=14 * 10**9, read=20 * MIB, mib=63, in_specs=[VM] * 3,
    )
    both = ((2 * width, width), BF)
    mid = [half, half, half, half, both]
    act, delta, gm, mean, give = call(
        mid_kernel,
        [core, recv, mix, at, mean_own, weights, features, cotangent],
        mid,
        [((2 * halo, width), BF), ((4, 2 * halo, nodes // 4), BF), ((halo, nodes), BF), wide, both, half, half, wide]
        + mid + [sems(16), sems(18)],
        flops=6 * 10**9, read=16 * MIB, in_specs=[SM] + [HB] * 7,
    )
    got = lax.ppermute(give, AXES, [(i, i ^ 1) for i in range(parts)])
    (keep,) = call(
        keep_kernel, [core, gm, at, features, mean, delta], [((12 * halo, width), F32)],
        [half, ((halo, nodes), BF), half, half, half, ((halo, width), F32), sems(3), sems(2)],
        flops=2 * 10**9, read=8 * MIB, mib=56, in_specs=[SM] + [HB] * 5,
    )
    (pay_back,) = call(
        pack_kernel, [gm, at_halo, keep, got], [packed], [((halo, width), F32), sems(parts // 32)],
        flops=10**9, read=6 * MIB, mib=44, in_specs=[VM, VM, HB, VM], out_specs=[VM],
    )
    back = lax.all_to_all(pay_back, AXES, split_axis=0, concat_axis=0, tiled=True).reshape(2 * halo, width)
    grad, grad_weights = call(
        last_kernel, [st, back, at_own, gm, delta, weights], [half, ((8, width), F32)], [half, sems(4)],
        flops=4 * 10**9, read=10 * MIB, mib=24, in_specs=[VM] * 6, out_specs=[HB, VM],
    )
    return act, grad, grad_weights


def solution(mesh):
    both = P(AXES, None)
    placed = (both, P(), both, both, P(AXES, None, None), both, both)
    return jax.shard_map(local, mesh=mesh, in_specs=placed, out_specs=(both, both, both), check_vma=False)
```

time: 109 us -> 105 us (0.963)
  Pallas kernels: 41.8 us -> 39.4 us
  local copies, waits for them, and re-layouts: 3.12 us -> 0.84 us
  blocking collectives: 34.8 us -> 33.7 us
    pallas_call x6, Pallas kernels: 41.8 us -> 39.4 us  [call(): pl.pallas_call(kernel, out_shape=[jax.ShapeDtypeStruct(s, d) for s, d in...]
    unnamed x14 -> x18, local copies, waits for them, and re-layouts: 2.33 us -> 0.05 us
    all_to_all x1, blocking collectives: 34.8 us -> 33.7 us  [local(): lax.all_to_all(pay_back, AXES, split_axis=0, concat_axis=0, tiled=True)]
  transfers between devices with their start and end apart: 2 -> 2, of which waited for: 1 -> 1; matrix products, arithmetic and copies ran while one was open for 1% -> 1% of each run, Pallas kernels for 18% -> 16%
where the time goes in v3:
time: 105 us
  Pallas kernels  39.4 us (38%)
  blocking collectives  33.7 us (32%)
  waiting for transfers between devices  16.3 us (16%)
  starting transfers between devices  13.2 us (13%)
    pallas_call x6, Pallas kernels, call(): pl.pallas_call(kernel, out_shape=[jax.ShapeDtypeStruct(s, d) for s, d in...  39.4 us
    all_to_all x1, blocking collectives, local(): lax.all_to_all(pay_back, AXES, split_axis=0, concat_axis=0, tiled=True)  33.7 us
    all_to_all x1, waiting for transfers between devices, local(): lax.all_to_all(pay, AXES, split_axis=0, concat_axis=0, tiled=True)  16.3 us
    all_to_all x1, starting transfers between devices, local(): lax.all_to_all(pay, AXES, split_axis=0, concat_axis=0, tiled=True)  12 us
  transfers between devices with their start and end apart: 2, of which 1 were waited for; matrix products, arithmetic and copies ran while one was open for 1% of the time, Pallas kernels for 16%

profile of v3, /device:TPU:1, one launch (start us, length us, event | category | flops | bytes accessed | tf_op | source)
XLA Modules:
  0.0 104.6 jit_solution(7339334425600025948)
XLA Ops:
  0.6 3.8 %shard_map.94 = bf16[128,16,512]{2,1,0:T(8,128)(2,1)} custom-call(bf16[1024,512]{1,0:T(8,128)(2,1)} %f_hbm.5, s32[8,128]{1,0:T(8,128)} %bitcast.11, s32[1,128]{1,0:T(1,128)} %count_hbm.1, s32[1,8]{1,0:T(1,128)} %hub_hbm.1), custom_call_target="tpu_custom_call" | custom-call | flops 1073741824 | bytes 3145728 | tf_op jit(solution)/shard_map/pallas_call | solution.py:282
  4.4 0.0 copy-start.7
  4.4 0.0 copy-start.6
  4.4 0.0 copy-start.8
  4.5 12.0 %all-to-all-start = ((bf16[128,16,512]{2,1,0:T(8,128)(2,1)}), bf16[128,16,512]{2,1,0:T(8,128)(2,1)}, u32[]{:S(2)}, u32[]{:S(2)}) async-start(bf16[128,16,512]{2,1,0:T(8,128)(2,1)} %shard_map.94), calls=%async_computation | async-start | bytes 4194304 | tf_op jit(solution)/shard_map/all_to_all | solution.py:309
  16.5 0.0 copy-done.7
  16.5 0.1 fusion
  16.5 0.0 copy-done.6
  16.5 0.0 copy-done.8
  16.6 0.1 copy.11
  16.7 0.7 reshape.21.slot_ref
  17.4 12.9 %shard_map.95 = (bf16[1024,1024]{1,0:T(8,128)(2,1)}, bf16[1024,1024]{1,0:T(8,128)(2,1)}, bf16[1024,1024]{1,0:T(8,128)(2,1)}, bf16[4,2048,256]{2,1,0:T(8,128)(2,1...) custom-call(s32[8,1024]{1,0:T(8,128)} %bitcast.14, s32[1,2048]{1,0:T(1,128)} %reshape.21.slot_ref, bf16[1024,512]{1,0:T(8,128)(2,1)} %f_hbm.5), custom_call_target="tpu_custom_call" | custom-call | flops 14000000000 | bytes 20971520 | tf_op jit(solution)/shard_map/pallas_call | solution.py:282
  30.2 16.3 %all-to-all-done = bf16[128,16,512]{2,1,0:T(8,128)(2,1)} async-done(((bf16[128,16,512]{2,1,0:T(8,128)(2,1)}), bf16[128,16,512]{2,1,0:T(8,128)(2,1)}, u32[]{:S(2)}, u32[]{:S(2)}) %all-to-all-start) | async-done | bytes 2097184 | tf_op jit(solution)/shard_map/all_to_all | solution.py:309
  46.6 10.2 %shard_map.96 = (bf16[1024,512]{1,0:T(8,128)(2,1)}, bf16[1024,512]{1,0:T(8,128)(2,1)}, bf16[1024,512]{1,0:T(8,128)(2,1)}, bf16[1024,512]{1,0:T(8,128)(2,1)}, bf16[1024,512]{1,0:T(8,128)(2,1)}) custom-call(s32[1]{0:T(128)} %bitcast.core_ref, bf16[2048,512]{1,0:T(8,128)(2,1)} %bitcast.3.recv_hbm, bf16[4,2048,256]{2,1,0:T(8,128)(2,1)} %get-tuple-element.16.mix_hbm, ...), custom_call_target="tpu_custom_call" | custom-call | flops 6000000000 | bytes 16777216 | tf_op jit(solution)/shard_map/pallas_call | solution.py:282
  56.8 1.3 %collective-permute-start = (bf16[1024,512]{1,0:T(8,128)(2,1)}, bf16[1024,512]{1,0:T(8,128)(2,1)S(1)}, u32[]{:S(2)}, u32[]{:S(2)}) collective-permute-start(bf16[1024,512]{1,0:T(8,128)(2,1)} %get-tuple-element.25), channel_id=1, source_target_pairs={{0,1},{1,0},{2,3},{3,2},{4,5},{5,4},{6,7},{7,6},{8,9},{9,8},{10,11... | collective-permute-start | bytes 3145736 | tf_op jit(solution)/shard_map/ppermute | solution.py:332
  58.0 4.2 %shard_map.97.keep_hbm = f32[12288,512]{1,0:T(8,128)} custom-call(s32[1]{0:T(128)} %bitcast.core_ref, bf16[1024,512]{1,0:T(8,128)(2,1)} %get-tuple-element.21.gm_hbm.gm_ref, bf16[1024,1024]{1,0:T(8,128)(2,1)} %get-tuple-element.17.at_hbm, bf16[1024,512]{1,0:T(8,128)(2,1)} %f_hbm.5, bf16[1024,512]{1,0:T(8,128)(2,1)} %get-tuple-element.23.mean_hbm, ...), custom_call_target="tpu_custom_call" | custom-call | flops 2000000000 | bytes 8388608 | tf_op jit(solution)/shard_map/pallas_call | solution.py:282
  62.2 0.0 collective-permute-done.got_ref
  62.3 2.8 %shard_map.98 = bf16[128,16,512]{2,1,0:T(8,128)(2,1)S(1)} custom-call(bf16[1024,512]{1,0:T(8,128)(2,1)S(1)} %copy-done, bf16[1024,1024]{1,0:T(8,128)(2,1)S(1)} %copy-done.1, f32[12288,512]{1,0:T(8,128)} %shard_map.97.keep_hbm, bf16[1024,512]{1,0:T(8,128)(2,1)S(1)} %collective-permute-done.got_ref), custom_call_target="tpu_custom_call" | custom-call | flops 1000000000 | bytes 6291456 | tf_op jit(solution)/shard_map/pallas_call | solution.py:282
  65.1 0.0 copy-start.2
  65.1 0.0 copy-start.3
  65.1 0.0 copy-start.5
  65.1 33.7 %all_to_all.10 = bf16[128,16,512]{2,1,0:T(8,128)(2,1)S(1)} all-to-all(bf16[128,16,512]{2,1,0:T(8,128)(2,1)S(1)} %shard_map.98), channel_id=1, replica_groups=mesh['row'=16,'col'=8] {'row','col'}, dimensions={0} | all-to-all | bytes 4194304 | tf_op jit(solution)/shard_map/all_to_all | solution.py:342
  98.8 0.0 copy-done.2
  98.9 5.6 %shard_map.99 = (bf16[1024,512]{1,0:T(8,128)(2,1)}, f32[8,512]{1,0:T(8,128)}) custom-call(bf16[1024,2048]{1,0:T(8,128)(2,1)S(1)} %copy-done.4, bf16[2048,512]{1,0:T(8,128)(2,1)S(1)} %bitcast.10, bf16[1024,1024]{1,0:T(8,128)(2,1)S(1)} %copy-done.5, bf16[1024,512]{1,0:T(8,128)(2,1)S(1)} %copy-done, bf16[1024,512]{1,0:T(8,128)(2,1)S(1)} %copy-done.2, ...), custom_call_target="tpu_custom_call" | custom-call | flops 4000000000 | bytes 10485760 | tf_op jit(solution)/shard_map/pallas_call | solution.py:282
  (12 shorter events, 0.0 us)
Async XLA Ops:
  4.4 12.0 %copy-start.7 = (s32[1,8]{1,0:T(1,128)S(1)}, s32[1,8]{1,0:T(1,128)}, u32[]{:S(2)}) copy-start(s32[1,8]{1,0:T(1,128)} %hub_hbm.1) | copy-start | bytes 100
  4.4 12.1 %copy-start.6 = (s32[1,128,8]{1,2,0:T(8,128)S(1)}, s32[1,128,8]{1,2,0:T(8,128)}, u32[]{:S(2)}) copy-start(s32[1,128,8]{1,2,0:T(8,128)} %param.11) | copy-start | bytes 12292
  4.4 12.1 %copy-start.8 = (s32[1,128]{1,0:T(1,128)S(1)}, s32[1,128]{1,0:T(1,128)}, u32[]{:S(2)}) copy-start(s32[1,128]{1,0:T(1,128)} %count_hbm.1) | copy-start | bytes 1540
  4.5 42.1 %all-to-all-start = ((bf16[128,16,512]{2,1,0:T(8,128)(2,1)}), bf16[128,16,512]{2,1,0:T(8,128)(2,1)}, u32[]{:S(2)}, u32[]{:S(2)}) async-start(bf16[128,16,512]{2,1,0:T(8,128)(2,1)} %shard_map.94), calls=%async_computation | async-start | bytes 4194304 | tf_op jit(solution)/shard_map/all_to_all | solution.py:309
  56.8 5.5 %collective-permute-start = (bf16[1024,512]{1,0:T(8,128)(2,1)}, bf16[1024,512]{1,0:T(8,128)(2,1)S(1)}, u32[]{:S(2)}, u32[]{:S(2)}) collective-permute-start(bf16[1024,512]{1,0:T(8,128)(2,1)} %get-tuple-element.25), channel_id=1, source_target_pairs={{0,1},{1,0},{2,3},{3,2},{4,5},{5,4},{6,7},{7,6},{8,9},{9,8},{10,11... | collective-permute-start | bytes 3145736 | tf_op jit(solution)/shard_map/ppermute | solution.py:332
  58.0 4.2 %copy-start = (bf16[1024,512]{1,0:T(8,128)(2,1)S(1)}, bf16[1024,512]{1,0:T(8,128)(2,1)}, u32[]{:S(2)}) copy-start(bf16[1024,512]{1,0:T(8,128)(2,1)} %get-tuple-element.21.gm_hbm.gm_ref) | copy-start | bytes 3145732
  58.0 4.2 %copy-start.1 = (bf16[1024,1024]{1,0:T(8,128)(2,1)S(1)}, bf16[1024,1024]{1,0:T(8,128)(2,1)}, u32[]{:S(2)}) copy-start(bf16[1024,1024]{1,0:T(8,128)(2,1)} %get-tuple-element.22.at_ref) | copy-start | bytes 6291460
  62.3 36.6 %copy-start.4 = (bf16[1024,2048]{1,0:T(8,128)(2,1)S(1)}, bf16[1024,2048]{1,0:T(8,128)(2,1)}, u32[]{:S(2)}) copy-start(bf16[1024,2048]{1,0:T(8,128)(2,1)} %get-tuple-element.20.st_ref) | copy-start | bytes 12582916
  65.1 33.7 %copy-start.2 = (bf16[1024,512]{1,0:T(8,128)(2,1)S(1)}, bf16[1024,512]{1,0:T(8,128)(2,1)}, u32[]{:S(2)}) copy-start(bf16[1024,512]{1,0:T(8,128)(2,1)} %get-tuple-element.24.delta_hbm.delta_ref) | copy-start | bytes 3145732
  65.1 33.7 %copy-start.3 = (bf16[1024,512]{1,0:T(8,128)(2,1)S(1)}, bf16[1024,512]{1,0:T(8,128)(2,1)}, u32[]{:S(2)}) copy-start(bf16[1024,512]{1,0:T(8,128)(2,1)} %w_ref.1) | copy-start | bytes 3145732
  65.1 33.7 %copy-start.5 = (bf16[1024,1024]{1,0:T(8,128)(2,1)S(1)}, bf16[1024,1024]{1,0:T(8,128)(2,1)}, u32[]{:S(2)}) copy-start(bf16[1024,1024]{1,0:T(8,128)(2,1)} %get-tuple-element.26.at_ref) | copy-start | bytes 6291460

commit v4 on v3

--- a/solution.py
+++ b/solution.py
@@ -153,7 +153,7 @@
                recv_ref, mix_ref, hub_ref, mown_ref, w_ref, f_ref, cot_ref, pre_ref,
                act_ref, delta_ref, gm_ref, mean_ref, give_ref, in_sem, out_sem):
     nodes, width = delta_ref.shape
-    step = 256
+    step = 512
     steps = nodes // step
     rows = [slice(b * step, (b + 1) * step) for b in range(steps)]
     early = launch([(w_hbm, w_ref), (f_hbm, f_ref)], in_sem, 0)
@@ -228,7 +228,7 @@
         stores = []
         for i, r in enumerate(tops):
             loads[1 + i].wait()
-            keep_ref[r, :] = mm(at_ref[r, :], gm_ref[...])
+            keep_ref[r, :] = mm(at_ref[r, :], gm_ref[...]).astype(BF)
             stores += launch([(keep_ref.at[r, :], keep_hbm.at[r, :])], out_sem, i)
         for copy in stores:
             copy.wait()
@@ -240,7 +240,7 @@
         stores = []
         for i, (r, x) in enumerate(zip(tops, (f_ref, mean_ref))):
             loads[1 + i].wait()
-            keep_ref[r, :] = mm_first(x[...], delta_ref[...])
+            keep_ref[r, :] = mm_first(x[...], delta_ref[...]).astype(BF)
             stores += launch([(keep_ref.at[r, :], keep_hbm.at[r, :])], out_sem, i)
         for copy in stores:
             copy.wait()
@@ -255,24 +255,33 @@
     for b, r in enumerate(rows):
         listed = mm(at_ref[r, :], gm_ref[...])
         loads[b].wait()
-        total = keep_ref[r, :] + got_ref[r, :].astype(F32)
+        total = keep_ref[r, :].astype(F32) + got_ref[r, :].astype(F32)
         both = jnp.concatenate([listed.reshape(step, 8, width), total.reshape(step, 8, width)], axis=1)
         out_ref[b * step : (b + 1) * step] = both.astype(BF)
 
 
-def last_kernel(st_ref, back_ref, at_ref, gm_ref, delta_ref, w_ref, out_hbm, weight_ref, out_ref, sems):
-    width = out_ref.shape[1]
+def last_kernel(st_ref, back_ref, at_ref, gm_ref, delta_ref, w_ref, hub_ref, out_hbm, weight_ref, list_ref, out_ref, sems):
+    nodes, width = out_ref.shape
     step = 256
-    shape = (8, back_ref.shape[0])
-    row = iota(shape, 1)
-    odd = (row // 16) % 2 == 1
-    take = jnp.where(odd & (row % 16 == iota(shape, 0) + 8), 1.0, 0.0).astype(BF)
-    weight_ref[...] = mm(take, back_ref[...])
+    hub_sum = jnp.zeros(weight_ref.shape, F32)
+    weight_sum = jnp.zeros(weight_ref.shape, F32)
+    for q in range(0, back_ref.shape[0] // 16, 2):
+        even = back_ref[q * 16 : (q + 1) * 16, :].astype(F32)
+        odd = back_ref[(q + 1) * 16 : (q + 2) * 16, :].astype(F32)
+        hub_sum = hub_sum + even[8:, :]
+        weight_sum = weight_sum + odd[8:, :]
+        list_ref[q * 8 : (q + 2) * 8, :] = jnp.concatenate([even[:8, :], odd[:8, :]], axis=0).astype(BF)
+    weight_ref[...] = weight_sum
+    high = hub_sum.astype(BF)
+    low = (hub_sum - high.astype(F32)).astype(BF)
+    hub_rows = jnp.concatenate([high, low], axis=0)
+    hubs = jnp.concatenate([hub_ref[...], hub_ref[...]], axis=1)
     stores = []
-    for b in range(out_ref.shape[0] // step):
+    for b in range(nodes // step):
         r = slice(b * step, (b + 1) * step)
         own = mm(at_ref[r, :], gm_ref[...]) + mm_last(delta_ref[r, :], w_ref[:width, :])
-        out_ref[r, :] = (own + mm(st_ref[r, :], back_ref[...])).astype(BF)
+        hot = (iota((step, hubs.shape[1]), 0) + b * step == hubs).astype(F32).astype(BF)
+        out_ref[r, :] = (own + mm(hot, hub_rows) + mm(st_ref[r, :], list_ref[...])).astype(BF)
         stores += launch([(out_ref.at[r, :], out_hbm.at[r, :])], sems, b)
     for copy in stores:
         copy.wait()
@@ -309,12 +318,9 @@
     recv = lax.all_to_all(pay, AXES, split_axis=0, concat_axis=0, tiled=True).reshape(2 * halo, width)
 
     live = iota((parts, 8), 1) < send_count[0][:, None]
-    even = iota((parts, 8), 0) % 2 == 0
-    slot = jnp.concatenate(
-        [jnp.where(live, send_rows[0], -1), jnp.where(even, hub_local, -1)], axis=1
-    ).reshape(1, 2 * halo)
+    slot = jnp.where(live, send_rows[0], -1).reshape(1, halo)
     square = ((nodes, nodes), BF)
-    hot = [square, ((halo, nodes), BF), ((halo, nodes), BF), ((4, 2 * halo, nodes // 4), BF), ((nodes, 2 * halo), BF), wide]
+    hot = [square, ((halo, nodes), BF), ((halo, nodes), BF), ((2, 2 * halo, nodes // 2), BF), ((nodes, halo), BF), wide]
     at_own, at_halo, at, mix, st, mean_own = call(
         hot_kernel, [neighbours.T, slot, features], hot, hot + [sems(6)],
         flops=14 * 10**9, read=20 * MIB, mib=63, in_specs=[VM] * 3,
@@ -325,24 +331,25 @@
         mid_kernel,
         [core, recv, mix, at, mean_own, weights, features, cotangent],
         mid,
-        [((2 * halo, width), BF), ((4, 2 * halo, nodes // 4), BF), ((halo, nodes), BF), wide, both, half, half, wide]
+        [((2 * halo, width), BF), ((2, 2 * halo, nodes // 2), BF), ((halo, nodes), BF), wide, both, half, half, wide]
         + mid + [sems(16), sems(18)],
         flops=6 * 10**9, read=16 * MIB, in_specs=[SM] + [HB] * 7,
     )
     got = lax.ppermute(give, AXES, [(i, i ^ 1) for i in range(parts)])
     (keep,) = call(
-        keep_kernel, [core, gm, at, features, mean, delta], [((12 * halo, width), F32)],
-        [half, ((halo, nodes), BF), half, half, half, ((halo, width), F32), sems(3), sems(2)],
+        keep_kernel, [core, gm, at, features, mean, delta], [((24 * halo, width), BF)],
+        [half, ((halo, nodes), BF), half, half, half, ((halo, width), BF), sems(3), sems(2)],
         flops=2 * 10**9, read=8 * MIB, mib=56, in_specs=[SM] + [HB] * 5,
     )
     (pay_back,) = call(
-        pack_kernel, [gm, at_halo, keep, got], [packed], [((halo, width), F32), sems(parts // 32)],
+        pack_kernel, [gm, at_halo, keep, got], [packed], [((halo, width), BF), sems(parts // 32)],
         flops=10**9, read=6 * MIB, mib=44, in_specs=[VM, VM, HB, VM], out_specs=[VM],
     )
     back = lax.all_to_all(pay_back, AXES, split_axis=0, concat_axis=0, tiled=True).reshape(2 * halo, width)
     grad, grad_weights = call(
-        last_kernel, [st, back, at_own, gm, delta, weights], [half, ((8, width), F32)], [half, sems(4)],
-        flops=4 * 10**9, read=10 * MIB, mib=24, in_specs=[VM] * 6, out_specs=[HB, VM],
+        last_kernel, [st, back, at_own, gm, delta, weights, hub_local], [half, ((8, width), F32)],
+        [((halo, width), BF), half, sems(4)],
+        flops=4 * 10**9, read=10 * MIB, mib=24, in_specs=[VM] * 7, out_specs=[HB, VM],
     )
     return act, grad, grad_weights
 

time: 105 us -> 103 us (0.981)
  Pallas kernels: 39.4 us -> 37.1 us
    pallas_call x6, Pallas kernels: 39.4 us -> 37.1 us  [call(): pl.pallas_call(kernel, out_shape=[jax.ShapeDtypeStruct(s, d) for s, d in...]
where the time goes in v4:
time: 103 us
  Pallas kernels  37.1 us (36%)
  blocking collectives  33.7 us (33%)
  waiting for transfers between devices  17 us (17%)
  starting transfers between devices  13.2 us (13%)
    pallas_call x6, Pallas kernels, call(): pl.pallas_call(kernel, out_shape=[jax.ShapeDtypeStruct(s, d) for s, d in...  37.1 us
    all_to_all x1, blocking collectives, local(): lax.all_to_all(pay_back, AXES, split_axis=0, concat_axis=0, tiled=True)  33.7 us
    all_to_all x1, waiting for transfers between devices, local(): lax.all_to_all(pay, AXES, split_axis=0, concat_axis=0, tiled=True)  17 us
    all_to_all x1, starting transfers between devices, local(): lax.all_to_all(pay, AXES, split_axis=0, concat_axis=0, tiled=True)  12 us
  transfers between devices with their start and end apart: 2, of which 1 were waited for; matrix products, arithmetic and copies ran while one was open for 1% of the time, Pallas kernels for 16%

profile of v4, /device:TPU:1, one launch (start us, length us, event | category | flops | bytes accessed | tf_op | source)
XLA Modules:
  0.0 102.9 jit_solution(3698509620554554203)
XLA Ops:
  0.6 3.8 %shard_map.94 = bf16[128,16,512]{2,1,0:T(8,128)(2,1)} custom-call(bf16[1024,512]{1,0:T(8,128)(2,1)} %f_hbm.5, s32[8,128]{1,0:T(8,128)} %bitcast.9, s32[1,128]{1,0:T(1,128)} %count_hbm.1, s32[1,8]{1,0:T(1,128)} %hub_ref.1), custom_call_target="tpu_custom_call" | custom-call | flops 1073741824 | bytes 3145728 | tf_op jit(solution)/shard_map/pallas_call | solution.py:291
  4.4 0.0 copy-start.7
  4.4 0.0 copy-start.8
  4.4 12.0 %all-to-all-start = ((bf16[128,16,512]{2,1,0:T(8,128)(2,1)}), bf16[128,16,512]{2,1,0:T(8,128)(2,1)}, u32[]{:S(2)}, u32[]{:S(2)}) async-start(bf16[128,16,512]{2,1,0:T(8,128)(2,1)} %shard_map.94), calls=%async_computation | async-start | bytes 4194304 | tf_op jit(solution)/shard_map/all_to_all | solution.py:318
  16.4 0.1 copy.11
  16.5 0.1 iota_compare_fusion
  16.6 0.1 lt.30
  16.7 0.1 squeeze.7
  16.8 0.6 broadcast_select_fusion.slot_ref
  17.4 12.2 %shard_map.95 = (bf16[1024,1024]{1,0:T(8,128)(2,1)}, bf16[1024,1024]{1,0:T(8,128)(2,1)}, bf16[1024,1024]{1,0:T(8,128)(2,1)}, bf16[2,2048,512]{2,1,0:T(8,128)(2,1...) custom-call(s32[8,1024]{1,0:T(8,128)} %bitcast.11, s32[1,1024]{1,0:T(1,128)} %broadcast_select_fusion.slot_ref, ...), custom_call_target="tpu_custom_call" | custom-call | flops 14000000000 | bytes 20971520 | tf_op jit(solution)/shard_map/pallas_call | solution.py:291
  29.6 17.0 %all-to-all-done = bf16[128,16,512]{2,1,0:T(8,128)(2,1)} async-done(((bf16[128,16,512]{2,1,0:T(8,128)(2,1)}), bf16[128,16,512]{2,1,0:T(8,128)(2,1)}, u32[]{:S(2)}, u32[]{:S(2)}) %all-to-all-start) | async-done | bytes 2097184 | tf_op jit(solution)/shard_map/all_to_all | solution.py:318
  46.6 9.7 %shard_map.96 = (bf16[1024,512]{1,0:T(8,128)(2,1)}, bf16[1024,512]{1,0:T(8,128)(2,1)}, bf16[1024,512]{1,0:T(8,128)(2,1)}, bf16[1024,512]{1,0:T(8,128)(2,1)}, bf16[1024,512]{1,0:T(8,128)(2,1)}) custom-call(s32[1]{0:T(128)} %bitcast.core_ref, bf16[2048,512]{1,0:T(8,128)(2,1)} %bitcast.3.recv_hbm, bf16[2,2048,512]{2,1,0:T(8,128)(2,1)} %get-tuple-element.16.mix_hbm, ...), custom_call_target="tpu_custom_call" | custom-call | flops 6000000000 | bytes 16777216 | tf_op jit(solution)/shard_map/pallas_call | solution.py:291
  56.3 1.2 %collective-permute-start = (bf16[1024,512]{1,0:T(8,128)(2,1)}, bf16[1024,512]{1,0:T(8,128)(2,1)S(1)}, u32[]{:S(2)}, u32[]{:S(2)}) collective-permute-start(bf16[1024,512]{1,0:T(8,128)(2,1)} %get-tuple-element.25), channel_id=1, source_target_pairs={{0,1},{1,0},{2,3},{3,2},{4,5},{5,4},{6,7},{7,6},{8,9},{9,8},{10,11... | collective-permute-start | bytes 3145736 | tf_op jit(solution)/shard_map/ppermute | solution.py:338
  57.5 4.0 %shard_map.97.keep_hbm = bf16[24576,512]{1,0:T(8,128)(2,1)} custom-call(s32[1]{0:T(128)} %bitcast.core_ref, bf16[1024,512]{1,0:T(8,128)(2,1)} %get-tuple-element.21.gm_hbm.gm_ref, bf16[1024,1024]{1,0:T(8,128)(2,1)} %get-tuple-element.17.at_hbm, bf16[1024,512]{1,0:T(8,128)(2,1)} %f_hbm.5, bf16[1024,512]{1,0:T(8,128)(2,1)} %get-tuple-element.23.mean_hbm, ...), custom_call_target="tpu_custom_call" | custom-call | flops 2000000000 | bytes 8388608 | tf_op jit(solution)/shard_map/pallas_call | solution.py:291
  61.5 0.0 collective-permute-done.got_ref
  61.6 2.9 %shard_map.98 = bf16[128,16,512]{2,1,0:T(8,128)(2,1)S(1)} custom-call(bf16[1024,512]{1,0:T(8,128)(2,1)S(1)} %copy-done, bf16[1024,1024]{1,0:T(8,128)(2,1)S(1)} %copy-done.1, bf16[24576,512]{1,0:T(8,128)(2,1)} %shard_map.97.keep_hbm, bf16[1024,512]{1,0:T(8,128)(2,1)S(1)} %collective-permute-done.got_ref), custom_call_target="tpu_custom_call" | custom-call | flops 1000000000 | bytes 6291456 | tf_op jit(solution)/shard_map/pallas_call | solution.py:291
  64.4 0.0 copy-start.2
  64.4 0.0 copy-start.3
  64.5 0.0 copy-start.4
  64.5 33.7 %all_to_all.10 = bf16[128,16,512]{2,1,0:T(8,128)(2,1)S(1)} all-to-all(bf16[128,16,512]{2,1,0:T(8,128)(2,1)S(1)} %shard_map.98), channel_id=1, replica_groups=mesh['row'=16,'col'=8] {'row','col'}, dimensions={0} | all-to-all | bytes 4194304 | tf_op jit(solution)/shard_map/all_to_all | solution.py:348
  98.2 0.0 copy-done.3
  98.2 0.0 copy-done.4
  98.2 0.0 copy-done.5
  98.2 4.6 %shard_map.99 = (bf16[1024,512]{1,0:T(8,128)(2,1)}, f32[8,512]{1,0:T(8,128)}) custom-call(bf16[1024,1024]{1,0:T(8,128)(2,1)S(1)} %copy-done.6, bf16[2048,512]{1,0:T(8,128)(2,1)S(1)} %bitcast.8, bf16[1024,1024]{1,0:T(8,128)(2,1)S(1)} %copy-done.5, bf16[1024,512]{1,0:T(8,128)(2,1)S(1)} %copy-done, bf16[1024,512]{1,0:T(8,128)(2,1)S(1)} %copy-done.2, ...), custom_call_target="tpu_custom_call" | custom-call | flops 4000000000 | bytes 10485760 | tf_op jit(solution)/shard_map/pallas_call | solution.py:291
  (10 shorter events, 0.0 us)
Async XLA Ops:
  4.4 12.0 %copy-start.7 = (s32[1,128,8]{1,2,0:T(8,128)S(1)}, s32[1,128,8]{1,2,0:T(8,128)}, u32[]{:S(2)}) copy-start(s32[1,128,8]{1,2,0:T(8,128)} %param.11) | copy-start | bytes 12292
  4.4 12.1 %copy-start.8 = (s32[1,128]{1,0:T(1,128)S(1)}, s32[1,128]{1,0:T(1,128)}, u32[]{:S(2)}) copy-start(s32[1,128]{1,0:T(1,128)} %count_hbm.1) | copy-start | bytes 1540
  4.4 42.1 %all-to-all-start = ((bf16[128,16,512]{2,1,0:T(8,128)(2,1)}), bf16[128,16,512]{2,1,0:T(8,128)(2,1)}, u32[]{:S(2)}, u32[]{:S(2)}) async-start(bf16[128,16,512]{2,1,0:T(8,128)(2,1)} %shard_map.94), calls=%async_computation | async-start | bytes 4194304 | tf_op jit(solution)/shard_map/all_to_all | solution.py:318
  56.3 5.3 %collective-permute-start = (bf16[1024,512]{1,0:T(8,128)(2,1)}, bf16[1024,512]{1,0:T(8,128)(2,1)S(1)}, u32[]{:S(2)}, u32[]{:S(2)}) collective-permute-start(bf16[1024,512]{1,0:T(8,128)(2,1)} %get-tuple-element.25), channel_id=1, source_target_pairs={{0,1},{1,0},{2,3},{3,2},{4,5},{5,4},{6,7},{7,6},{8,9},{9,8},{10,11... | collective-permute-start | bytes 3145736 | tf_op jit(solution)/shard_map/ppermute | solution.py:338
  57.5 4.0 %copy-start = (bf16[1024,512]{1,0:T(8,128)(2,1)S(1)}, bf16[1024,512]{1,0:T(8,128)(2,1)}, u32[]{:S(2)}) copy-start(bf16[1024,512]{1,0:T(8,128)(2,1)} %get-tuple-element.21.gm_hbm.gm_ref) | copy-start | bytes 3145732
  57.5 4.0 %copy-start.1 = (bf16[1024,1024]{1,0:T(8,128)(2,1)S(1)}, bf16[1024,1024]{1,0:T(8,128)(2,1)}, u32[]{:S(2)}) copy-start(bf16[1024,1024]{1,0:T(8,128)(2,1)} %get-tuple-element.22.at_ref) | copy-start | bytes 6291460
  61.6 36.6 %copy-start.6 = (bf16[1024,1024]{1,0:T(8,128)(2,1)S(1)}, bf16[1024,1024]{1,0:T(8,128)(2,1)}, u32[]{:S(2)}) copy-start(bf16[1024,1024]{1,0:T(8,128)(2,1)} %get-tuple-element.20.st_ref) | copy-start | bytes 6291460
  64.4 33.7 %copy-start.2 = (bf16[1024,512]{1,0:T(8,128)(2,1)S(1)}, bf16[1024,512]{1,0:T(8,128)(2,1)}, u32[]{:S(2)}) copy-start(bf16[1024,512]{1,0:T(8,128)(2,1)} %get-tuple-element.24.delta_hbm.delta_ref) | copy-start | bytes 3145732
  64.4 33.7 %copy-start.3 = (bf16[1024,512]{1,0:T(8,128)(2,1)S(1)}, bf16[1024,512]{1,0:T(8,128)(2,1)}, u32[]{:S(2)}) copy-start(bf16[1024,512]{1,0:T(8,128)(2,1)} %w_ref.1) | copy-start | bytes 3145732
  64.5 33.7 %copy-start.4 = (s32[1,8]{1,0:T(1,128)S(1)}, s32[1,8]{1,0:T(1,128)}, u32[]{:S(2)}) copy-start(s32[1,8]{1,0:T(1,128)} %hub_ref.1) | copy-start | bytes 100
  64.5 33.7 %copy-start.5 = (bf16[1024,1024]{1,0:T(8,128)(2,1)S(1)}, bf16[1024,1024]{1,0:T(8,128)(2,1)}, u32[]{:S(2)}) copy-start(bf16[1024,1024]{1,0:T(8,128)(2,1)} %get-tuple-element.26.at_ref) | copy-start | bytes 6291460

commit v5 on v4

--- a/solution.py
+++ b/solution.py
@@ -8,6 +8,7 @@
 BF = jnp.bfloat16
 F32 = jnp.float32
 DEG = 8
+BIG = 12
 AXES = ("row", "col")
 VM = pl.BlockSpec(memory_space=pltpu.VMEM)
 SM = pl.BlockSpec(memory_space=pltpu.SMEM)
@@ -135,7 +136,7 @@
     copies += launch([(own_ref, own_hbm), (mown_ref, mown_hbm)], sems, 1)
     count_matrix(u - nodes, m, [listed_ref.at[:, c] for c in cols])
     count_matrix(u - (nodes + halo), m, [hub_ref.at[:, c] for c in cols])
-    copies += launch([(listed_ref, listed_hbm), (hub_ref, hub_hbm)], sems, 3)
+    copies += launch([(listed_ref, listed_hbm), (hub_ref, hub_hbm.at[:halo, :])], sems, 3)
     slot = slot_ref[...]
 
     @pl.loop(0, nodes // 16)
@@ -149,7 +150,7 @@
 
 
 def mid_kernel(core_ref, recv_hbm, mix_hbm, at_hbm, mown_hbm, w_hbm, f_hbm, cot_hbm,
-               act_hbm, delta_hbm, gm_hbm, mean_hbm, give_hbm,
+               act_hbm, delta_hbm, gm_hbm, trio_hbm, give_hbm,
                recv_ref, mix_ref, hub_ref, mown_ref, w_ref, f_ref, cot_ref, pre_ref,
                act_ref, delta_ref, gm_ref, mean_ref, give_ref, in_sem, out_sem):
     nodes, width = delta_ref.shape
@@ -162,8 +163,7 @@
     for b, r in enumerate(rows):
         pairs = [(mix_hbm.at[b], mix_ref.at[b]), (mown_hbm.at[r, :], mown_ref.at[r, :]), (cot_hbm.at[r, :], cot_ref.at[r, :])]
         blocks.append(launch(pairs, in_sem, 3 + 3 * b))
-    first = at_hbm.shape[0] - hub_ref.shape[0]
-    hub_load = pltpu.make_async_copy(at_hbm.at[first:, :], hub_ref, in_sem.at[3 + 3 * steps])
+    hub_load = pltpu.make_async_copy(at_hbm.at[: hub_ref.shape[0], :], hub_ref, in_sem.at[3 + 3 * steps])
 
     @pl.when(core_ref[0] != 0)
     def _():
@@ -188,10 +188,14 @@
         delta_ref[r, :] = delta
         gm_ref[r, :] = (mm_last(delta, w2) / DEG).astype(BF)
         stores += launch(
-            [(x.at[r, :], y.at[r, :]) for x, y in
-             ((gm_ref, gm_hbm), (act_ref, act_hbm), (delta_ref, delta_hbm), (mean_ref, mean_hbm))],
-            out_sem, 4 * b,
+            [(x.at[r, :], y.at[r, :]) for x, y in ((gm_ref, gm_hbm), (act_ref, act_hbm), (delta_ref, delta_hbm))]
+            + [
+                (x.at[r, :], trio_hbm.at[i * nodes + r.start : i * nodes + r.stop, :])
+                for i, x in enumerate((gm_ref, delta_ref, mean_ref))
+            ],
+            out_sem, 6 * b,
         )
+
     half = width
     tops = [slice(0, half), slice(half, 2 * half)]
 
@@ -199,65 +203,55 @@
     def _():
         for i, (r, x) in enumerate(zip(tops, (f_ref, mean_ref))):
             give_ref[r, :] = mm_first(x[...], delta_ref[...]).astype(BF)
-            pltpu.make_async_copy(give_ref.at[r, :], give_hbm.at[r, :], out_sem.at[4 * steps + i]).start()
+            pltpu.make_async_copy(give_ref.at[r, :], give_hbm.at[r, :], out_sem.at[6 * steps + i]).start()
 
     @pl.when(core_ref[0] != 0)
     def _():
         hub_load.wait()
         for i, r in enumerate(tops):
             give_ref[r, :] = mm(hub_ref[r, :], gm_ref[...]).astype(BF)
-            pltpu.make_async_copy(give_ref.at[r, :], give_hbm.at[r, :], out_sem.at[4 * steps + i]).start()
+            pltpu.make_async_copy(give_ref.at[r, :], give_hbm.at[r, :], out_sem.at[6 * steps + i]).start()
 
     for i, r in enumerate(tops):
-        pltpu.make_async_copy(give_ref.at[r, :], give_hbm.at[r, :], out_sem.at[4 * steps + i]).wait()
+        pltpu.make_async_copy(give_ref.at[r, :], give_hbm.at[r, :], out_sem.at[6 * steps + i]).wait()
     for copy in stores:
         copy.wait()
 
 
-def keep_kernel(core_ref, gm_hbm, at_hbm, f_hbm, mean_hbm, delta_hbm, keep_hbm,
-                gm_ref, at_ref, f_ref, mean_ref, delta_ref, keep_ref, in_sem, out_sem):
-    nodes, width = f_ref.shape
-    halo = at_ref.shape[0]
-    tops = [slice(0, width), slice(width, 2 * width)]
-
-    @pl.when(core_ref[0] == 0)
-    def _():
-        first = at_hbm.shape[0] - halo
-        loads = launch([(gm_hbm, gm_ref)] + [(at_hbm.at[first + r.start : first + r.stop, :], at_ref.at[r, :]) for r in tops], in_sem)
-        loads[0].wait()
-        stores = []
-        for i, r in enumerate(tops):
-            loads[1 + i].wait()
-            keep_ref[r, :] = mm(at_ref[r, :], gm_ref[...]).astype(BF)
-            stores += launch([(keep_ref.at[r, :], keep_hbm.at[r, :])], out_sem, i)
-        for copy in stores:
-            copy.wait()
-
-    @pl.when(core_ref[0] != 0)
-    def _():
-        loads = launch([(delta_hbm, delta_ref), (f_hbm, f_ref), (mean_hbm, mean_ref)], in_sem)
-        loads[0].wait()
-        stores = []
-        for i, (r, x) in enumerate(zip(tops, (f_ref, mean_ref))):
-            loads[1 + i].wait()
-            keep_ref[r, :] = mm_first(x[...], delta_ref[...]).astype(BF)
-            stores += launch([(keep_ref.at[r, :], keep_hbm.at[r, :])], out_sem, i)
-        for copy in stores:
-            copy.wait()
-
-
-def pack_kernel(gm_ref, at_ref, keep_hbm, got_ref, out_ref, keep_ref, sems):
-    parts = out_ref.shape[0]
-    width = out_ref.shape[2]
+def pack_kernel(core_ref, trio_hbm, at_ref, hub_hbm, f_ref, got_ref, out_ref, gm_ref, delta_ref, mean_ref, hub_ref, sems):
+    parts, _, width = out_ref.shape
+    nodes = gm_ref.shape[0]
     step = 32
     rows = [slice(b * step * 8, (b + 1) * step * 8) for b in range(parts // step)]
-    loads = launch([(keep_hbm.at[r, :], keep_ref.at[r, :]) for r in rows], sems)
-    for b, r in enumerate(rows):
-        listed = mm(at_ref[r, :], gm_ref[...])
-        loads[b].wait()
-        total = keep_ref[r, :].astype(F32) + got_ref[r, :].astype(F32)
-        both = jnp.concatenate([listed.reshape(step, 8, width), total.reshape(step, 8, width)], axis=1)
-        out_ref[b * step : (b + 1) * step] = both.astype(BF)
+
+    def fill(sources, own):
+        loads = launch(sources, sems)
+        loads[0].wait()
+        listed = mm(at_ref[...], gm_ref[...])
+        for load in loads[1:]:
+            load.wait()
+        for b, r in enumerate(rows):
+            total = own(r) + got_ref[r, :].astype(F32)
+            both = jnp.concatenate([listed[r, :].reshape(step, 8, width), total.reshape(step, 8, width)], axis=1)
+            out_ref[b * step : (b + 1) * step] = both.astype(BF)
+
+    gm_load = (trio_hbm.at[:nodes, :], gm_ref)
+
+    def weight_rows(r):
+        x_ref = f_ref if r.start < width else mean_ref
+        first = r.start % width
+        return mm_first(x_ref[:, first : first + step * 8], delta_ref[...])
+
+    @pl.when(core_ref[0] == 0)
+    def _():
+        fill([gm_load, (hub_hbm.at[: hub_ref.shape[0], :], hub_ref)], lambda r: mm(hub_ref[r, :], gm_ref[...]))
+
+    @pl.when(core_ref[0] != 0)
+    def _():
+        fill(
+            [gm_load] + [(trio_hbm.at[i * nodes : (i + 1) * nodes, :], x) for i, x in ((1, delta_ref), (2, mean_ref))],
+            weight_rows,
+        )
 
 
 def last_kernel(st_ref, back_ref, at_ref, gm_ref, delta_ref, w_ref, hub_ref, out_hbm, weight_ref, list_ref, out_ref, sems):
@@ -321,29 +315,26 @@
     slot = jnp.where(live, send_rows[0], -1).reshape(1, halo)
     square = ((nodes, nodes), BF)
     hot = [square, ((halo, nodes), BF), ((halo, nodes), BF), ((2, 2 * halo, nodes // 2), BF), ((nodes, halo), BF), wide]
+    outs = hot[:2] + [((BIG * halo, nodes), BF)] + hot[3:]
     at_own, at_halo, at, mix, st, mean_own = call(
-        hot_kernel, [neighbours.T, slot, features], hot, hot + [sems(6)],
+        hot_kernel, [neighbours.T, slot, features], outs, hot + [sems(6)],
         flops=14 * 10**9, read=20 * MIB, mib=63, in_specs=[VM] * 3,
     )
     both = ((2 * width, width), BF)
     mid = [half, half, half, half, both]
-    act, delta, gm, mean, give = call(
+    act, delta, gm, trio, give = call(
         mid_kernel,
         [core, recv, mix, at, mean_own, weights, features, cotangent],
-        mid,
+        mid[:3] + [((2 * BIG * nodes, width), BF), both],
         [((2 * halo, width), BF), ((2, 2 * halo, nodes // 2), BF), ((halo, nodes), BF), wide, both, half, half, wide]
         + mid + [sems(16), sems(18)],
         flops=6 * 10**9, read=16 * MIB, in_specs=[SM] + [HB] * 7,
     )
     got = lax.ppermute(give, AXES, [(i, i ^ 1) for i in range(parts)])
-    (keep,) = call(
-        keep_kernel, [core, gm, at, features, mean, delta], [((24 * halo, width), BF)],
-        [half, ((halo, nodes), BF), half, half, half, ((halo, width), BF), sems(3), sems(2)],
-        flops=2 * 10**9, read=8 * MIB, mib=56, in_specs=[SM] + [HB] * 5,
-    )
     (pay_back,) = call(
-        pack_kernel, [gm, at_halo, keep, got], [packed], [((halo, width), BF), sems(parts // 32)],
-        flops=10**9, read=6 * MIB, mib=44, in_specs=[VM, VM, HB, VM], out_specs=[VM],
+        pack_kernel, [core, trio, at_halo, at, features, got], [packed],
+        [half, half, half, ((halo, nodes), BF), sems(3)],
+        flops=2 * 10**9, read=6 * MIB, mib=40, in_specs=[SM, HB, VM, HB, VM, VM], out_specs=[VM],
     )
     back = lax.all_to_all(pay_back, AXES, split_axis=0, concat_axis=0, tiled=True).reshape(2 * halo, width)
     grad, grad_weights = call(

time: 103 us -> 104 us (level)
  Pallas kernels: 37.1 us -> 34.6 us
  waiting for transfers between devices: 17 us -> 19.4 us
    ppermute x1, waiting for transfers between devices: 0.01 us -> 2.5 us  [local(): got = lax.ppermute(give, AXES, [(i, i ^ 1) for i in range(parts)])]
    pallas_call x6 -> x5, Pallas kernels: 37.1 us -> 34.6 us  [call(): pl.pallas_call(kernel, out_shape=[jax.ShapeDtypeStruct(s, d) for s, d in...]
  transfers between devices with their start and end apart: 2 -> 2, of which waited for: 1 -> 2; matrix products, arithmetic and copies ran while one was open for 1% -> 1% of each run, Pallas kernels for 16% -> 12%
where the time goes in v5:
time: 104 us; the launch traced here: 103 us
  Pallas kernels  34.6 us (33%)
  blocking collectives  34 us (33%)
  waiting for transfers between devices  19.4 us (19%)
  starting transfers between devices  13.2 us (13%)
    pallas_call x5, Pallas kernels, call(): pl.pallas_call(kernel, out_shape=[jax.ShapeDtypeStruct(s, d) for s, d in...  34.6 us
    all_to_all x1, blocking collectives, local(): lax.all_to_all(pay_back, AXES, split_axis=0, concat_axis=0, tiled=True)  34 us
    all_to_all x1, waiting for transfers between devices, local(): lax.all_to_all(pay, AXES, split_axis=0, concat_axis=0, tiled=True)  16.9 us
    all_to_all x1, starting transfers between devices, local(): lax.all_to_all(pay, AXES, split_axis=0, concat_axis=0, tiled=True)  12 us
    ppermute x1, waiting for transfers between devices, local(): got = lax.ppermute(give, AXES, [(i, i ^ 1) for i in range(parts)])  2.5 us
  transfers between devices with their start and end apart: 2, of which 2 were waited for; matrix products, arithmetic and copies ran while one was open for 1% of the time, Pallas kernels for 12%

profile of v5, /device:TPU:1, one launch (start us, length us, event | category | flops | bytes accessed | tf_op | source)
XLA Modules:
  0.0 103.3 jit_solution(12032508671936899864)
XLA Ops:
  0.6 3.8 %shard_map.94 = bf16[128,16,512]{2,1,0:T(8,128)(2,1)} custom-call(bf16[1024,512]{1,0:T(8,128)(2,1)} %f_ref.3, s32[8,128]{1,0:T(8,128)} %bitcast.9, s32[1,128]{1,0:T(1,128)} %count_hbm.1, s32[1,8]{1,0:T(1,128)} %hub_ref.1), custom_call_target="tpu_custom_call" | custom-call | flops 1073741824 | bytes 3145728 | tf_op jit(solution)/shard_map/pallas_call | solution.py:285
  4.4 0.0 copy-start.8
  4.4 0.0 copy-start.9
  4.4 12.0 %all-to-all-start = ((bf16[128,16,512]{2,1,0:T(8,128)(2,1)}), bf16[128,16,512]{2,1,0:T(8,128)(2,1)}, u32[]{:S(2)}, u32[]{:S(2)}) async-start(bf16[128,16,512]{2,1,0:T(8,128)(2,1)} %shard_map.94), calls=%async_computation | async-start | bytes 4194304 | tf_op jit(solution)/shard_map/all_to_all | solution.py:312
  16.4 0.0 copy-done.8
  16.4 0.1 copy.11
  16.5 0.0 copy-done.9
  16.5 0.1 iota_compare_fusion
  16.6 0.1 lt.30
  16.7 0.1 squeeze.7
  16.8 0.6 broadcast_select_fusion.slot_ref
  17.4 12.2 %shard_map.95 = (bf16[1024,1024]{1,0:T(8,128)(2,1)}, bf16[1024,1024]{1,0:T(8,128)(2,1)}, bf16[12288,1024]{1,0:T(8,128)(2,1)}, bf16[2,2048,512]{2,1,0:T(8,128)(2,...) custom-call(s32[8,1024]{1,0:T(8,128)} %bitcast.11, s32[1,1024]{1,0:T(1,128)} %broadcast_select_fusion.slot_ref, ...), custom_call_target="tpu_custom_call" | custom-call | flops 14000000000 | bytes 20971520 | tf_op jit(solution)/shard_map/pallas_call | solution.py:285
  29.7 16.9 %all-to-all-done = bf16[128,16,512]{2,1,0:T(8,128)(2,1)} async-done(((bf16[128,16,512]{2,1,0:T(8,128)(2,1)}), bf16[128,16,512]{2,1,0:T(8,128)(2,1)}, u32[]{:S(2)}, u32[]{:S(2)}) %all-to-all-start) | async-done | bytes 2097184 | tf_op jit(solution)/shard_map/all_to_all | solution.py:312
  46.6 9.9 %shard_map.96 = (bf16[1024,512]{1,0:T(8,128)(2,1)}, bf16[1024,512]{1,0:T(8,128)(2,1)}, bf16[1024,512]{1,0:T(8,128)(2,1)}, bf16[24576,512]{1,0:T(8,128)(2,1)}, bf16[1024,512]{1,0:T(8,128)(2,1)}) custom-call(s32[1]{0:T(128)} %bitcast.core_ref, bf16[2048,512]{1,0:T(8,128)(2,1)} %bitcast.3.recv_hbm, bf16[2,2048,512]{2,1,0:T(8,128)(2,1)} %get-tuple-element.16.mix_hbm, ...), custom_call_target="tpu_custom_call" | custom-call | flops 6000000000 | bytes 16777216 | tf_op jit(solution)/shard_map/pallas_call | solution.py:285
  56.4 1.3 %collective-permute-start = (bf16[1024,512]{1,0:T(8,128)(2,1)}, bf16[1024,512]{1,0:T(8,128)(2,1)S(1)}, u32[]{:S(2)}, u32[]{:S(2)}) collective-permute-start(bf16[1024,512]{1,0:T(8,128)(2,1)} %get-tuple-element.23), channel_id=1, source_target_pairs={{0,1},{1,0},{2,3},{3,2},{4,5},{5,4},{6,7},{7,6},{8,9},{9,8},{10,11... | collective-permute-start | bytes 3145736 | tf_op jit(solution)/shard_map/ppermute | solution.py:333
  57.7 2.5 %collective-permute-done.got_ref = bf16[1024,512]{1,0:T(8,128)(2,1)S(1)} collective-permute-done((bf16[1024,512]{1,0:T(8,128)(2,1)}, bf16[1024,512]{1,0:T(8,128)(2,1)S(1)}, u32[]{:S(2)}, u32[]{:S(2)}) %collective-permute-start) | collective-permute-done | bytes 1048608 | tf_op jit(solution)/shard_map/ppermute | solution.py:333
  60.2 0.0 copy-done
  60.2 0.0 copy-done.1
  60.2 4.2 %shard_map.97 = bf16[128,16,512]{2,1,0:T(8,128)(2,1)S(1)} custom-call(s32[1]{0:T(128)} %bitcast.core_ref, bf16[24576,512]{1,0:T(8,128)(2,1)} %get-tuple-element.21.trio_hbm, bf16[1024,1024]{1,0:T(8,128)(2,1)S(1)} %copy-done.1, bf16[12288,1024]{1,0:T(8,128)(2,1)} %get-tuple-element.17.at_hbm.hub_hbm, bf16[1024,512]{1,0:T(8,128)(2,1)S(1)} %copy-done, ...), custom_call_target="tpu_custom_call" | custom-call | flops 2000000000 | bytes 6291456 | tf_op jit(solution)/shard_map/pallas_call | solution.py:285
  64.4 0.0 copy-start.2
  64.4 0.0 copy-start.3
  64.4 0.0 copy-start.5
  64.5 34.0 %all_to_all.10 = bf16[128,16,512]{2,1,0:T(8,128)(2,1)S(1)} all-to-all(bf16[128,16,512]{2,1,0:T(8,128)(2,1)S(1)} %shard_map.97), channel_id=1, replica_groups=mesh['row'=16,'col'=8] {'row','col'}, dimensions={0} | all-to-all | bytes 4194304 | tf_op jit(solution)/shard_map/all_to_all | solution.py:339
  98.5 4.6 %shard_map.98 = (bf16[1024,512]{1,0:T(8,128)(2,1)}, f32[8,512]{1,0:T(8,128)}) custom-call(bf16[1024,1024]{1,0:T(8,128)(2,1)S(1)} %copy-done.7, bf16[2048,512]{1,0:T(8,128)(2,1)S(1)} %bitcast.8, bf16[1024,1024]{1,0:T(8,128)(2,1)S(1)} %copy-done.6, bf16[1024,512]{1,0:T(8,128)(2,1)S(1)} %copy-done.4, bf16[1024,512]{1,0:T(8,128)(2,1)S(1)} %copy-done.3, ...), custom_call_target="tpu_custom_call" | custom-call | flops 4000000000 | bytes 10485760 | tf_op jit(solution)/shard_map/pallas_call | solution.py:285
  (11 shorter events, 0.0 us)
Async XLA Ops:
  4.4 12.0 %copy-start.8 = (s32[1,128,8]{1,2,0:T(8,128)S(1)}, s32[1,128,8]{1,2,0:T(8,128)}, u32[]{:S(2)}) copy-start(s32[1,128,8]{1,2,0:T(8,128)} %param.11) | copy-start | bytes 12292
  4.4 12.1 %copy-start.9 = (s32[1,128]{1,0:T(1,128)S(1)}, s32[1,128]{1,0:T(1,128)}, u32[]{:S(2)}) copy-start(s32[1,128]{1,0:T(1,128)} %count_hbm.1) | copy-start | bytes 1540
  4.4 42.1 %all-to-all-start = ((bf16[128,16,512]{2,1,0:T(8,128)(2,1)}), bf16[128,16,512]{2,1,0:T(8,128)(2,1)}, u32[]{:S(2)}, u32[]{:S(2)}) async-start(bf16[128,16,512]{2,1,0:T(8,128)(2,1)} %shard_map.94), calls=%async_computation | async-start | bytes 4194304 | tf_op jit(solution)/shard_map/all_to_all | solution.py:312
  46.6 13.6 %copy-start = (bf16[1024,512]{1,0:T(8,128)(2,1)S(1)}, bf16[1024,512]{1,0:T(8,128)(2,1)}, u32[]{:S(2)}) copy-start(bf16[1024,512]{1,0:T(8,128)(2,1)} %f_ref.3) | copy-start | bytes 3145732
  46.6 13.6 %copy-start.1 = (bf16[1024,1024]{1,0:T(8,128)(2,1)S(1)}, bf16[1024,1024]{1,0:T(8,128)(2,1)}, u32[]{:S(2)}) copy-start(bf16[1024,1024]{1,0:T(8,128)(2,1)} %get-tuple-element.22.at_ref) | copy-start | bytes 6291460
  56.4 3.7 %collective-permute-start = (bf16[1024,512]{1,0:T(8,128)(2,1)}, bf16[1024,512]{1,0:T(8,128)(2,1)S(1)}, u32[]{:S(2)}, u32[]{:S(2)}) collective-permute-start(bf16[1024,512]{1,0:T(8,128)(2,1)} %get-tuple-element.23), channel_id=1, source_target_pairs={{0,1},{1,0},{2,3},{3,2},{4,5},{5,4},{6,7},{7,6},{8,9},{9,8},{10,11... | collective-permute-start | bytes 3145736 | tf_op jit(solution)/shard_map/ppermute | solution.py:333
  60.2 38.3 %copy-start.6 = (bf16[1024,1024]{1,0:T(8,128)(2,1)S(1)}, bf16[1024,1024]{1,0:T(8,128)(2,1)}, u32[]{:S(2)}) copy-start(bf16[1024,1024]{1,0:T(8,128)(2,1)} %get-tuple-element.24.at_ref) | copy-start | bytes 6291460
  60.2 38.3 %copy-start.7 = (bf16[1024,1024]{1,0:T(8,128)(2,1)S(1)}, bf16[1024,1024]{1,0:T(8,128)(2,1)}, u32[]{:S(2)}) copy-start(bf16[1024,1024]{1,0:T(8,128)(2,1)} %get-tuple-element.20.st_ref) | copy-start | bytes 6291460
  64.4 34.1 %copy-start.2 = (bf16[1024,512]{1,0:T(8,128)(2,1)S(1)}, bf16[1024,512]{1,0:T(8,128)(2,1)}, u32[]{:S(2)}) copy-start(bf16[1024,512]{1,0:T(8,128)(2,1)} %w_ref.1) | copy-start | bytes 3145732
  64.4 34.1 %copy-start.3 = (bf16[1024,512]{1,0:T(8,128)(2,1)S(1)}, bf16[1024,512]{1,0:T(8,128)(2,1)}, u32[]{:S(2)}) copy-start(bf16[1024,512]{1,0:T(8,128)(2,1)} %get-tuple-element.26.delta_ref) | copy-start | bytes 3145732
  64.4 34.1 %copy-start.4 = (bf16[1024,512]{1,0:T(8,128)(2,1)S(1)}, bf16[1024,512]{1,0:T(8,128)(2,1)}, u32[]{:S(2)}) copy-start(bf16[1024,512]{1,0:T(8,128)(2,1)} %get-tuple-element.25.gm_ref) | copy-start | bytes 3145732
  64.4 34.1 %copy-start.5 = (s32[1,8]{1,0:T(1,128)S(1)}, s32[1,8]{1,0:T(1,128)}, u32[]{:S(2)}) copy-start(s32[1,8]{1,0:T(1,128)} %hub_ref.1) | copy-start | bytes 100

commit v6 on v5

--- a/solution.py
+++ b/solution.py
@@ -218,40 +218,51 @@
         copy.wait()
 
 
-def pack_kernel(core_ref, trio_hbm, at_ref, hub_hbm, f_ref, got_ref, out_ref, gm_ref, delta_ref, mean_ref, hub_ref, sems):
+def listed_kernel(trio_hbm, at_ref, out_ref, gm_ref, sem):
+    (load,) = launch([(trio_hbm.at[: gm_ref.shape[0], :], gm_ref)], sem)
+    load.wait()
+    out_ref[...] = mm(at_ref[...], gm_ref[...]).astype(BF)
+
+
+def pack_kernel(core_ref, trio_hbm, listed_ref, hub_hbm, f_ref, got_ref, out_ref, gm_ref, delta_ref, mean_ref, hub_ref, sems):
     parts, _, width = out_ref.shape
     nodes = gm_ref.shape[0]
     step = 32
     rows = [slice(b * step * 8, (b + 1) * step * 8) for b in range(parts // step)]
-
-    def fill(sources, own):
-        loads = launch(sources, sems)
+    parts_of = [trio_hbm.at[i * nodes : (i + 1) * nodes, :] for i in range(3)]
+
+    def fill(own):
+        for b, r in enumerate(rows):
+            total = own(b, r) + got_ref[r, :].astype(F32)
+            listed = listed_ref[r, :].astype(F32)
+            both = jnp.concatenate([listed.reshape(step, 8, width), total.reshape(step, 8, width)], axis=1)
+            out_ref[b * step : (b + 1) * step] = both.astype(BF)
+
+    @pl.when(core_ref[0] == 0)
+    def _():
+        loads = launch([(parts_of[0], gm_ref)] + [(hub_hbm.at[r, :], hub_ref.at[r, :]) for r in rows], sems)
         loads[0].wait()
-        listed = mm(at_ref[...], gm_ref[...])
-        for load in loads[1:]:
-            load.wait()
-        for b, r in enumerate(rows):
-            total = own(r) + got_ref[r, :].astype(F32)
-            both = jnp.concatenate([listed[r, :].reshape(step, 8, width), total.reshape(step, 8, width)], axis=1)
-            out_ref[b * step : (b + 1) * step] = both.astype(BF)
-
-    gm_load = (trio_hbm.at[:nodes, :], gm_ref)
-
-    def weight_rows(r):
-        x_ref = f_ref if r.start < width else mean_ref
-        first = r.start % width
-        return mm_first(x_ref[:, first : first + step * 8], delta_ref[...])
-
-    @pl.when(core_ref[0] == 0)
-    def _():
-        fill([gm_load, (hub_hbm.at[: hub_ref.shape[0], :], hub_ref)], lambda r: mm(hub_ref[r, :], gm_ref[...]))
+
+        def hub_rows(b, r):
+            loads[1 + b].wait()
+            return mm(hub_ref[r, :], gm_ref[...])
+
+        fill(hub_rows)
 
     @pl.when(core_ref[0] != 0)
     def _():
-        fill(
-            [gm_load] + [(trio_hbm.at[i * nodes : (i + 1) * nodes, :], x) for i, x in ((1, delta_ref), (2, mean_ref))],
-            weight_rows,
-        )
+        loads = launch([(parts_of[1], delta_ref), (parts_of[2], mean_ref)], sems)
+
+        def weight_rows(b, r):
+            first = r.start % width
+            if b == 0:
+                loads[0].wait()
+            if r.start == width:
+                loads[1].wait()
+            x_ref = f_ref if r.start < width else mean_ref
+            return mm_first(x_ref[:, first : first + step * 8], delta_ref[...])
+
+        fill(weight_rows)
 
 
 def last_kernel(st_ref, back_ref, at_ref, gm_ref, delta_ref, w_ref, hub_ref, out_hbm, weight_ref, list_ref, out_ref, sems):
@@ -331,9 +342,13 @@
         flops=6 * 10**9, read=16 * MIB, in_specs=[SM] + [HB] * 7,
     )
     got = lax.ppermute(give, AXES, [(i, i ^ 1) for i in range(parts)])
+    (listed,) = call(
+        listed_kernel, [trio, at_halo], [((halo, width), BF)], [half, sems(1)],
+        flops=10**9, read=4 * MIB, mib=40, in_specs=[HB, VM], out_specs=[VM],
+    )
     (pay_back,) = call(
-        pack_kernel, [core, trio, at_halo, at, features, got], [packed],
-        [half, half, half, ((halo, nodes), BF), sems(3)],
+        pack_kernel, [core, trio, listed, at, features, got], [packed],
+        [half, half, half, ((halo, nodes), BF), sems(1 + parts // 32)],
         flops=2 * 10**9, read=6 * MIB, mib=40, in_specs=[SM, HB, VM, HB, VM, VM], out_specs=[VM],
     )
     back = lax.all_to_all(pay_back, AXES, split_axis=0, concat_axis=0, tiled=True).reshape(2 * halo, width)

time: 104 us -> 103 us (level)
  waiting for transfers between devices: 19.4 us -> 16.9 us
  Pallas kernels: 34.6 us -> 36.2 us
    ppermute x1, waiting for transfers between devices: 2.5 us -> 0.01 us  [local(): got = lax.ppermute(give, AXES, [(i, i ^ 1) for i in range(parts)])]
    pallas_call x5 -> x6, Pallas kernels: 34.6 us -> 36.2 us  [call(): pl.pallas_call(kernel, out_shape=[jax.ShapeDtypeStruct(s, d) for s, d in...]
  transfers between devices with their start and end apart: 2 -> 2, of which waited for: 2 -> 1; matrix products, arithmetic and copies ran while one was open for 1% -> 1% of each run, Pallas kernels for 12% -> 14%
where the time goes in v6:
time: 103 us
  Pallas kernels  36.2 us (35%)
  blocking collectives  34.3 us (33%)
  waiting for transfers between devices  16.9 us (16%)
  starting transfers between devices  13.2 us (13%)
    pallas_call x6, Pallas kernels, call(): pl.pallas_call(kernel, out_shape=[jax.ShapeDtypeStruct(s, d) for s, d in...  36.2 us
    all_to_all x1, blocking collectives, local(): lax.all_to_all(pay_back, AXES, split_axis=0, concat_axis=0, tiled=True)  34.3 us
    all_to_all x1, waiting for transfers between devices, local(): lax.all_to_all(pay, AXES, split_axis=0, concat_axis=0, tiled=True)  16.9 us
    all_to_all x1, starting transfers between devices, local(): lax.all_to_all(pay, AXES, split_axis=0, concat_axis=0, tiled=True)  12 us
  transfers between devices with their start and end apart: 2, of which 1 were waited for; matrix products, arithmetic and copies ran while one was open for 1% of the time, Pallas kernels for 14%

profile of v6, /device:TPU:1, one launch (start us, length us, event | category | flops | bytes accessed | tf_op | source)
XLA Modules:
  0.0 102.6 jit_solution(8914559848511445978)
XLA Ops:
  0.6 3.8 %shard_map.94 = bf16[128,16,512]{2,1,0:T(8,128)(2,1)} custom-call(bf16[1024,512]{1,0:T(8,128)(2,1)} %f_ref.3, s32[8,128]{1,0:T(8,128)} %bitcast.9, s32[1,128]{1,0:T(1,128)} %count_hbm.1, s32[1,8]{1,0:T(1,128)} %hub_ref.1), custom_call_target="tpu_custom_call" | custom-call | flops 1073741824 | bytes 3145728 | tf_op jit(solution)/shard_map/pallas_call | solution.py:296
  4.4 0.0 copy-start.8
  4.4 0.0 copy-start.9
  4.4 12.0 %all-to-all-start = ((bf16[128,16,512]{2,1,0:T(8,128)(2,1)}), bf16[128,16,512]{2,1,0:T(8,128)(2,1)}, u32[]{:S(2)}, u32[]{:S(2)}) async-start(bf16[128,16,512]{2,1,0:T(8,128)(2,1)} %shard_map.94), calls=%async_computation | async-start | bytes 4194304 | tf_op jit(solution)/shard_map/all_to_all | solution.py:323
  16.4 0.0 copy-done.8
  16.4 0.1 copy.11
  16.5 0.0 copy-done.9
  16.5 0.1 iota_compare_fusion
  16.6 0.1 lt.30
  16.7 0.1 squeeze.7
  16.8 0.6 broadcast_select_fusion.slot_ref
  17.4 12.2 %shard_map.95 = (bf16[1024,1024]{1,0:T(8,128)(2,1)}, bf16[1024,1024]{1,0:T(8,128)(2,1)}, bf16[12288,1024]{1,0:T(8,128)(2,1)}, bf16[2,2048,512]{2,1,0:T(8,128)(2,...) custom-call(s32[8,1024]{1,0:T(8,128)} %bitcast.11, s32[1,1024]{1,0:T(1,128)} %broadcast_select_fusion.slot_ref, ...), custom_call_target="tpu_custom_call" | custom-call | flops 14000000000 | bytes 20971520 | tf_op jit(solution)/shard_map/pallas_call | solution.py:296
  29.7 16.9 %all-to-all-done = bf16[128,16,512]{2,1,0:T(8,128)(2,1)} async-done(((bf16[128,16,512]{2,1,0:T(8,128)(2,1)}), bf16[128,16,512]{2,1,0:T(8,128)(2,1)}, u32[]{:S(2)}, u32[]{:S(2)}) %all-to-all-start) | async-done | bytes 2097184 | tf_op jit(solution)/shard_map/all_to_all | solution.py:323
  46.6 9.9 %shard_map.96 = (bf16[1024,512]{1,0:T(8,128)(2,1)}, bf16[1024,512]{1,0:T(8,128)(2,1)}, bf16[1024,512]{1,0:T(8,128)(2,1)}, bf16[24576,512]{1,0:T(8,128)(2,1)}, bf16[1024,512]{1,0:T(8,128)(2,1)}) custom-call(s32[1]{0:T(128)} %bitcast.core_ref, bf16[2048,512]{1,0:T(8,128)(2,1)} %bitcast.3.recv_hbm, bf16[2,2048,512]{2,1,0:T(8,128)(2,1)} %get-tuple-element.16.mix_hbm, ...), custom_call_target="tpu_custom_call" | custom-call | flops 6000000000 | bytes 16777216 | tf_op jit(solution)/shard_map/pallas_call | solution.py:296
  56.4 1.3 %collective-permute-start = (bf16[1024,512]{1,0:T(8,128)(2,1)}, bf16[1024,512]{1,0:T(8,128)(2,1)S(1)}, u32[]{:S(2)}, u32[]{:S(2)}) collective-permute-start(bf16[1024,512]{1,0:T(8,128)(2,1)} %get-tuple-element.23), channel_id=1, source_target_pairs={{0,1},{1,0},{2,3},{3,2},{4,5},{5,4},{6,7},{7,6},{8,9},{9,8},{10,11... | collective-permute-start | bytes 3145736 | tf_op jit(solution)/shard_map/ppermute | solution.py:344
  57.7 0.0 copy-done.1
  57.7 2.6 %shard_map.97.listed_ref = bf16[1024,512]{1,0:T(8,128)(2,1)S(1)} custom-call(bf16[24576,512]{1,0:T(8,128)(2,1)} %get-tuple-element.21.trio_hbm, bf16[1024,1024]{1,0:T(8,128)(2,1)S(1)} %copy-done.1), custom_call_target="tpu_custom_call" | custom-call | flops 1000000000 | bytes 4194304 | tf_op jit(solution)/shard_map/pallas_call | solution.py:296
  60.3 0.0 collective-permute-done.got_ref
  60.3 3.2 %shard_map.98 = bf16[128,16,512]{2,1,0:T(8,128)(2,1)S(1)} custom-call(s32[1]{0:T(128)} %bitcast.core_ref, bf16[24576,512]{1,0:T(8,128)(2,1)} %get-tuple-element.21.trio_hbm, bf16[1024,512]{1,0:T(8,128)(2,1)S(1)} %shard_map.97.listed_ref, bf16[12288,1024]{1,0:T(8,128)(2,1)} %get-tuple-element.17.at_hbm.hub_hbm, bf16[1024,512]{1,0:T(8,128)(2,1)S(1)} %copy-done, ...), custom_call_target="tpu_custom_call" | custom-call | flops 2000000000 | bytes 6291456 | tf_op jit(solution)/shard_map/pallas_call | solution.py:296
  63.5 0.0 copy-start.2
  63.5 0.0 copy-start.3
  63.5 0.0 copy-start.5
  63.5 34.3 %all_to_all.10 = bf16[128,16,512]{2,1,0:T(8,128)(2,1)S(1)} all-to-all(bf16[128,16,512]{2,1,0:T(8,128)(2,1)S(1)} %shard_map.98), channel_id=1, replica_groups=mesh['row'=16,'col'=8] {'row','col'}, dimensions={0} | all-to-all | bytes 4194304 | tf_op jit(solution)/shard_map/all_to_all | solution.py:354
  97.9 4.6 %shard_map.99 = (bf16[1024,512]{1,0:T(8,128)(2,1)}, f32[8,512]{1,0:T(8,128)}) custom-call(bf16[1024,1024]{1,0:T(8,128)(2,1)S(1)} %copy-done.7, bf16[2048,512]{1,0:T(8,128)(2,1)S(1)} %bitcast.8, bf16[1024,1024]{1,0:T(8,128)(2,1)S(1)} %copy-done.6, bf16[1024,512]{1,0:T(8,128)(2,1)S(1)} %copy-done.4, bf16[1024,512]{1,0:T(8,128)(2,1)S(1)} %copy-done.3, ...), custom_call_target="tpu_custom_call" | custom-call | flops 4000000000 | bytes 10485760 | tf_op jit(solution)/shard_map/pallas_call | solution.py:296
  (12 shorter events, 0.0 us)
Async XLA Ops:
  4.4 12.0 %copy-start.8 = (s32[1,128,8]{1,2,0:T(8,128)S(1)}, s32[1,128,8]{1,2,0:T(8,128)}, u32[]{:S(2)}) copy-start(s32[1,128,8]{1,2,0:T(8,128)} %param.11) | copy-start | bytes 12292
  4.4 12.1 %copy-start.9 = (s32[1,128]{1,0:T(1,128)S(1)}, s32[1,128]{1,0:T(1,128)}, u32[]{:S(2)}) copy-start(s32[1,128]{1,0:T(1,128)} %count_hbm.1) | copy-start | bytes 1540
  4.4 42.1 %all-to-all-start = ((bf16[128,16,512]{2,1,0:T(8,128)(2,1)}), bf16[128,16,512]{2,1,0:T(8,128)(2,1)}, u32[]{:S(2)}, u32[]{:S(2)}) async-start(bf16[128,16,512]{2,1,0:T(8,128)(2,1)} %shard_map.94), calls=%async_computation | async-start | bytes 4194304 | tf_op jit(solution)/shard_map/all_to_all | solution.py:323
  46.6 11.1 %copy-start.1 = (bf16[1024,1024]{1,0:T(8,128)(2,1)S(1)}, bf16[1024,1024]{1,0:T(8,128)(2,1)}, u32[]{:S(2)}) copy-start(bf16[1024,1024]{1,0:T(8,128)(2,1)} %get-tuple-element.22.at_ref) | copy-start | bytes 6291460
  56.4 3.8 %collective-permute-start = (bf16[1024,512]{1,0:T(8,128)(2,1)}, bf16[1024,512]{1,0:T(8,128)(2,1)S(1)}, u32[]{:S(2)}, u32[]{:S(2)}) collective-permute-start(bf16[1024,512]{1,0:T(8,128)(2,1)} %get-tuple-element.23), channel_id=1, source_target_pairs={{0,1},{1,0},{2,3},{3,2},{4,5},{5,4},{6,7},{7,6},{8,9},{9,8},{10,11... | collective-permute-start | bytes 3145736 | tf_op jit(solution)/shard_map/ppermute | solution.py:344
  57.7 2.6 %copy-start = (bf16[1024,512]{1,0:T(8,128)(2,1)S(1)}, bf16[1024,512]{1,0:T(8,128)(2,1)}, u32[]{:S(2)}) copy-start(bf16[1024,512]{1,0:T(8,128)(2,1)} %f_ref.3) | copy-start | bytes 3145732
  60.3 37.5 %copy-start.6 = (bf16[1024,1024]{1,0:T(8,128)(2,1)S(1)}, bf16[1024,1024]{1,0:T(8,128)(2,1)}, u32[]{:S(2)}) copy-start(bf16[1024,1024]{1,0:T(8,128)(2,1)} %get-tuple-element.24.at_ref) | copy-start | bytes 6291460
  60.3 37.5 %copy-start.7 = (bf16[1024,1024]{1,0:T(8,128)(2,1)S(1)}, bf16[1024,1024]{1,0:T(8,128)(2,1)}, u32[]{:S(2)}) copy-start(bf16[1024,1024]{1,0:T(8,128)(2,1)} %get-tuple-element.20.st_ref) | copy-start | bytes 6291460
  63.5 34.3 %copy-start.2 = (bf16[1024,512]{1,0:T(8,128)(2,1)S(1)}, bf16[1024,512]{1,0:T(8,128)(2,1)}, u32[]{:S(2)}) copy-start(bf16[1024,512]{1,0:T(8,128)(2,1)} %w_ref.1) | copy-start | bytes 3145732
  63.5 34.3 %copy-start.3 = (bf16[1024,512]{1,0:T(8,128)(2,1)S(1)}, bf16[1024,512]{1,0:T(8,128)(2,1)}, u32[]{:S(2)}) copy-start(bf16[1024,512]{1,0:T(8,128)(2,1)} %get-tuple-element.26.delta_ref) | copy-start | bytes 3145732
  63.5 34.3 %copy-start.4 = (bf16[1024,512]{1,0:T(8,128)(2,1)S(1)}, bf16[1024,512]{1,0:T(8,128)(2,1)}, u32[]{:S(2)}) copy-start(bf16[1024,512]{1,0:T(8,128)(2,1)} %get-tuple-element.25.gm_ref) | copy-start | bytes 3145732
  63.5 34.3 %copy-start.5 = (s32[1,8]{1,0:T(1,128)S(1)}, s32[1,8]{1,0:T(1,128)}, u32[]{:S(2)}) copy-start(s32[1,8]{1,0:T(1,128)} %hub_ref.1) | copy-start | bytes 100

commit v7 on v5

--- a/solution.py
+++ b/solution.py
@@ -150,7 +150,7 @@
 
 
 def mid_kernel(core_ref, recv_hbm, mix_hbm, at_hbm, mown_hbm, w_hbm, f_hbm, cot_hbm,
-               act_hbm, delta_hbm, gm_hbm, trio_hbm, give_hbm,
+               act_hbm, trio_hbm, give_hbm,
                recv_ref, mix_ref, hub_ref, mown_ref, w_ref, f_ref, cot_ref, pre_ref,
                act_ref, delta_ref, gm_ref, mean_ref, give_ref, in_sem, out_sem):
     nodes, width = delta_ref.shape
@@ -188,12 +188,12 @@
         delta_ref[r, :] = delta
         gm_ref[r, :] = (mm_last(delta, w2) / DEG).astype(BF)
         stores += launch(
-            [(x.at[r, :], y.at[r, :]) for x, y in ((gm_ref, gm_hbm), (act_ref, act_hbm), (delta_ref, delta_hbm))]
+            [(act_ref.at[r, :], act_hbm.at[r, :])]
             + [
                 (x.at[r, :], trio_hbm.at[i * nodes + r.start : i * nodes + r.stop, :])
                 for i, x in enumerate((gm_ref, delta_ref, mean_ref))
             ],
-            out_sem, 6 * b,
+            out_sem, 4 * b,
         )
 
     half = width
@@ -203,39 +203,48 @@
     def _():
         for i, (r, x) in enumerate(zip(tops, (f_ref, mean_ref))):
             give_ref[r, :] = mm_first(x[...], delta_ref[...]).astype(BF)
-            pltpu.make_async_copy(give_ref.at[r, :], give_hbm.at[r, :], out_sem.at[6 * steps + i]).start()
+            pltpu.make_async_copy(give_ref.at[r, :], give_hbm.at[r, :], out_sem.at[4 * steps + i]).start()
 
     @pl.when(core_ref[0] != 0)
     def _():
         hub_load.wait()
         for i, r in enumerate(tops):
             give_ref[r, :] = mm(hub_ref[r, :], gm_ref[...]).astype(BF)
-            pltpu.make_async_copy(give_ref.at[r, :], give_hbm.at[r, :], out_sem.at[6 * steps + i]).start()
+            pltpu.make_async_copy(give_ref.at[r, :], give_hbm.at[r, :], out_sem.at[4 * steps + i]).start()
 
     for i, r in enumerate(tops):
-        pltpu.make_async_copy(give_ref.at[r, :], give_hbm.at[r, :], out_sem.at[6 * steps + i]).wait()
+        pltpu.make_async_copy(give_ref.at[r, :], give_hbm.at[r, :], out_sem.at[4 * steps + i]).wait()
     for copy in stores:
         copy.wait()
 
 
-def pack_kernel(core_ref, trio_hbm, at_ref, hub_hbm, f_ref, got_ref, out_ref, gm_ref, delta_ref, mean_ref, hub_ref, sems):
+def listed_kernel(core_ref, trio_hbm, hub_hbm, at_ref, out_ref, gm_ref, delta_ref, mean_ref, hub_ref, sems):
+    nodes = gm_ref.shape[0]
+    parts_of = [trio_hbm.at[i * nodes : (i + 1) * nodes, :] for i in range(3)]
+    first, second = launch([(parts_of[0], gm_ref), (parts_of[1], delta_ref)], sems)
+    hub_load = pltpu.make_async_copy(hub_hbm.at[: hub_ref.shape[0], :], hub_ref, sems.at[2])
+    mean_load = pltpu.make_async_copy(parts_of[2], mean_ref, sems.at[3])
+    even = core_ref[0] == 0
+    pl.when(even)(hub_load.start)
+    pl.when(jnp.logical_not(even))(mean_load.start)
+    first.wait()
+    out_ref[...] = mm(at_ref[...], gm_ref[...]).astype(BF)
+    second.wait()
+    pl.when(even)(hub_load.wait)
+    pl.when(jnp.logical_not(even))(mean_load.wait)
+
+
+def pack_kernel(core_ref, listed_ref, gm_ref, delta_ref, mean_ref, hub_ref, f_ref, got_ref, out_ref):
     parts, _, width = out_ref.shape
-    nodes = gm_ref.shape[0]
     step = 32
     rows = [slice(b * step * 8, (b + 1) * step * 8) for b in range(parts // step)]
 
-    def fill(sources, own):
-        loads = launch(sources, sems)
-        loads[0].wait()
-        listed = mm(at_ref[...], gm_ref[...])
-        for load in loads[1:]:
-            load.wait()
+    def fill(own):
         for b, r in enumerate(rows):
             total = own(r) + got_ref[r, :].astype(F32)
-            both = jnp.concatenate([listed[r, :].reshape(step, 8, width), total.reshape(step, 8, width)], axis=1)
+            listed = listed_ref[r, :].astype(F32)
+            both = jnp.concatenate([listed.reshape(step, 8, width), total.reshape(step, 8, width)], axis=1)
             out_ref[b * step : (b + 1) * step] = both.astype(BF)
-
-    gm_load = (trio_hbm.at[:nodes, :], gm_ref)
 
     def weight_rows(r):
         x_ref = f_ref if r.start < width else mean_ref
@@ -244,14 +253,11 @@
 
     @pl.when(core_ref[0] == 0)
     def _():
-        fill([gm_load, (hub_hbm.at[: hub_ref.shape[0], :], hub_ref)], lambda r: mm(hub_ref[r, :], gm_ref[...]))
+        fill(lambda r: mm(hub_ref[r, :], gm_ref[...]))
 
     @pl.when(core_ref[0] != 0)
     def _():
-        fill(
-            [gm_load] + [(trio_hbm.at[i * nodes : (i + 1) * nodes, :], x) for i, x in ((1, delta_ref), (2, mean_ref))],
-            weight_rows,
-        )
+        fill(weight_rows)
 
 
 def last_kernel(st_ref, back_ref, at_ref, gm_ref, delta_ref, w_ref, hub_ref, out_hbm, weight_ref, list_ref, out_ref, sems):
@@ -322,19 +328,22 @@
     )
     both = ((2 * width, width), BF)
     mid = [half, half, half, half, both]
-    act, delta, gm, trio, give = call(
+    act, trio, give = call(
         mid_kernel,
         [core, recv, mix, at, mean_own, weights, features, cotangent],
-        mid[:3] + [((2 * BIG * nodes, width), BF), both],
+        [half, ((2 * BIG * nodes, width), BF), both],
         [((2 * halo, width), BF), ((2, 2 * halo, nodes // 2), BF), ((halo, nodes), BF), wide, both, half, half, wide]
         + mid + [sems(16), sems(18)],
         flops=6 * 10**9, read=16 * MIB, in_specs=[SM] + [HB] * 7,
     )
     got = lax.ppermute(give, AXES, [(i, i ^ 1) for i in range(parts)])
+    listed, gm, delta, mean, hub_counts = call(
+        listed_kernel, [core, trio, at, at_halo], [half, half, half, half, ((halo, nodes), BF)], [sems(4)],
+        flops=10**9, read=4 * MIB, mib=24, in_specs=[SM, HB, HB, VM], out_specs=[VM] * 5,
+    )
     (pay_back,) = call(
-        pack_kernel, [core, trio, at_halo, at, features, got], [packed],
-        [half, half, half, ((halo, nodes), BF), sems(3)],
-        flops=2 * 10**9, read=6 * MIB, mib=40, in_specs=[SM, HB, VM, HB, VM, VM], out_specs=[VM],
+        pack_kernel, [core, listed, gm, delta, mean, hub_counts, features, got], [packed],
+        flops=2 * 10**9, read=6 * MIB, mib=24, in_specs=[SM] + [VM] * 7, out_specs=[VM],
     )
     back = lax.all_to_all(pay_back, AXES, split_axis=0, concat_axis=0, tiled=True).reshape(2 * halo, width)
     grad, grad_weights = call(

time: 104 us -> 101 us (0.971)
  waiting for transfers between devices: 19.4 us -> 16.9 us
    ppermute x1, waiting for transfers between devices: 2.5 us -> 0.01 us  [local(): got = lax.ppermute(give, AXES, [(i, i ^ 1) for i in range(parts)])]
    pallas_call x5 -> x6, Pallas kernels: 34.6 us -> 34.5 us  [call(): pl.pallas_call(kernel, out_shape=[jax.ShapeDtypeStruct(s, d) for s, d in...]
  transfers between devices with their start and end apart: 2 -> 2, of which waited for: 2 -> 1; matrix products, arithmetic and copies ran while one was open for 1% -> 1% of each run, Pallas kernels for 12% -> 15%
where the time goes in v7:
time: 101 us; the launch traced here: 100 us
  Pallas kernels  34.5 us (34%)
  blocking collectives  33.7 us (33%)
  waiting for transfers between devices  16.9 us (17%)
  starting transfers between devices  13.2 us (13%)
    pallas_call x6, Pallas kernels, call(): pl.pallas_call(kernel, out_shape=[jax.ShapeDtypeStruct(s, d) for s, d in...  34.5 us
    all_to_all x1, blocking collectives, local(): lax.all_to_all(pay_back, AXES, split_axis=0, concat_axis=0, tiled=True)  33.7 us
    all_to_all x1, waiting for transfers between devices, local(): lax.all_to_all(pay, AXES, split_axis=0, concat_axis=0, tiled=True)  16.9 us
    all_to_all x1, starting transfers between devices, local(): lax.all_to_all(pay, AXES, split_axis=0, concat_axis=0, tiled=True)  12 us
  transfers between devices with their start and end apart: 2, of which 1 were waited for; matrix products, arithmetic and copies ran while one was open for 1% of the time, Pallas kernels for 15%

profile of v7, /device:TPU:1, one launch (start us, length us, event | category | flops | bytes accessed | tf_op | source)
XLA Modules:
  0.0 100.3 jit_solution(17450586135780845430)
XLA Ops:
  0.6 3.8 %shard_map.94 = bf16[128,16,512]{2,1,0:T(8,128)(2,1)} custom-call(bf16[1024,512]{1,0:T(8,128)(2,1)} %f_ref.3, s32[8,128]{1,0:T(8,128)} %bitcast.9, s32[1,128]{1,0:T(1,128)} %count_hbm.1, s32[1,8]{1,0:T(1,128)} %hub_ref.1), custom_call_target="tpu_custom_call" | custom-call | flops 1073741824 | bytes 3145728 | tf_op jit(solution)/shard_map/pallas_call | solution.py:291
  4.4 0.0 copy-start.6
  4.4 0.0 copy-start.7
  4.4 12.0 %all-to-all-start = ((bf16[128,16,512]{2,1,0:T(8,128)(2,1)}), bf16[128,16,512]{2,1,0:T(8,128)(2,1)}, u32[]{:S(2)}, u32[]{:S(2)}) async-start(bf16[128,16,512]{2,1,0:T(8,128)(2,1)} %shard_map.94), calls=%async_computation | async-start | bytes 4194304 | tf_op jit(solution)/shard_map/all_to_all | solution.py:318
  16.4 0.1 copy.11
  16.5 0.0 copy-done.7
  16.5 0.1 iota_compare_fusion
  16.6 0.1 lt.30
  16.7 0.1 squeeze.7
  16.8 0.6 broadcast_select_fusion.slot_ref
  17.4 12.2 %shard_map.95 = (bf16[1024,1024]{1,0:T(8,128)(2,1)}, bf16[1024,1024]{1,0:T(8,128)(2,1)}, bf16[12288,1024]{1,0:T(8,128)(2,1)}, bf16[2,2048,512]{2,1,0:T(8,128)(2,...) custom-call(s32[8,1024]{1,0:T(8,128)} %bitcast.11, s32[1,1024]{1,0:T(1,128)} %broadcast_select_fusion.slot_ref, ...), custom_call_target="tpu_custom_call" | custom-call | flops 14000000000 | bytes 20971520 | tf_op jit(solution)/shard_map/pallas_call | solution.py:291
  29.7 16.9 %all-to-all-done = bf16[128,16,512]{2,1,0:T(8,128)(2,1)} async-done(((bf16[128,16,512]{2,1,0:T(8,128)(2,1)}), bf16[128,16,512]{2,1,0:T(8,128)(2,1)}, u32[]{:S(2)}, u32[]{:S(2)}) %all-to-all-start) | async-done | bytes 2097184 | tf_op jit(solution)/shard_map/all_to_all | solution.py:318
  46.6 9.8 %shard_map.96 = (bf16[1024,512]{1,0:T(8,128)(2,1)}, bf16[24576,512]{1,0:T(8,128)(2,1)}, bf16[1024,512]{1,0:T(8,128)(2,1)}) custom-call(s32[1]{0:T(128)} %bitcast.core_ref, bf16[2048,512]{1,0:T(8,128)(2,1)} %bitcast.3.recv_hbm, bf16[2,2048,512]{2,1,0:T(8,128)(2,1)} %get-tuple-element.19.mix_hbm, bf16[12288,1024]{1,0:T(8,128)(2,1)} %get-tuple-element.20.at_hbm.hub_hbm, ...), custom_call_target="tpu_custom_call" | custom-call | flops 6000000000 | bytes 16777216 | tf_op jit(solution)/shard_map/pallas_call | solution.py:291
  56.4 1.3 %collective-permute-start = (bf16[1024,512]{1,0:T(8,128)(2,1)}, bf16[1024,512]{1,0:T(8,128)(2,1)S(1)}, u32[]{:S(2)}, u32[]{:S(2)}) collective-permute-start(bf16[1024,512]{1,0:T(8,128)(2,1)} %get-tuple-element.31), channel_id=1, source_target_pairs={{0,1},{1,0},{2,3},{3,2},{4,5},{5,4},{6,7},{7,6},{8,9},{9,8},{10,11... | collective-permute-start | bytes 3145736 | tf_op jit(solution)/shard_map/ppermute | solution.py:339
  57.7 0.0 copy-done.1
  57.7 2.6 %shard_map.97 = (bf16[1024,512]{1,0:T(8,128)(2,1)S(1)}, bf16[1024,512]{1,0:T(8,128)(2,1)S(1)}, bf16[1024,512]{1,0:T(8,128)(2,1)S(1)}, bf16[1024,512]{1,0:T(8,128)(2,1)S(1)}, bf16[1024,1024]{1,0:T(8,128)(2,1)S(1)}) custom-call(s32[1]{0:T(128)} %bitcast.core_ref, bf16[24576,512]{1,0:T(8,128)(2,1)} %get-tuple-element.24.trio_hbm, ...), custom_call_target="tpu_custom_call" | custom-call | flops 1000000000 | bytes 4194304 | tf_op jit(solution)/shard_map/pallas_call | solution.py:291
  60.3 0.0 collective-permute-done.got_ref
  60.3 1.5 %shard_map.98 = bf16[128,16,512]{2,1,0:T(8,128)(2,1)S(1)} custom-call(s32[1]{0:T(128)} %bitcast.core_ref, bf16[1024,512]{1,0:T(8,128)(2,1)S(1)} %get-tuple-element.26.listed_ref, bf16[1024,512]{1,0:T(8,128)(2,1)S(1)} %get-tuple-element.27.gm_ref, bf16[1024,512]{1,0:T(8,128)(2,1)S(1)} %get-tuple-element.28.delta_ref, ...), custom_call_target="tpu_custom_call" | custom-call | flops 2000000000 | bytes 6291456 | tf_op jit(solution)/shard_map/pallas_call | solution.py:291
  61.8 0.0 copy-start.2
  61.8 0.0 copy-start.3
  61.8 0.0 copy-start.4
  61.8 33.7 %all_to_all.10 = bf16[128,16,512]{2,1,0:T(8,128)(2,1)S(1)} all-to-all(bf16[128,16,512]{2,1,0:T(8,128)(2,1)S(1)} %shard_map.98), channel_id=1, replica_groups=mesh['row'=16,'col'=8] {'row','col'}, dimensions={0} | all-to-all | bytes 4194304 | tf_op jit(solution)/shard_map/all_to_all | solution.py:348
  95.6 0.0 copy-done.2
  95.6 4.6 %shard_map.99 = (bf16[1024,512]{1,0:T(8,128)(2,1)}, f32[8,512]{1,0:T(8,128)}) custom-call(bf16[1024,1024]{1,0:T(8,128)(2,1)S(1)} %copy-done.5, bf16[2048,512]{1,0:T(8,128)(2,1)S(1)} %bitcast.8, bf16[1024,1024]{1,0:T(8,128)(2,1)S(1)} %copy-done.4, bf16[1024,512]{1,0:T(8,128)(2,1)S(1)} %get-tuple-element.27.gm_ref, ...), custom_call_target="tpu_custom_call" | custom-call | flops 4000000000 | bytes 10485760 | tf_op jit(solution)/shard_map/pallas_call | solution.py:291
  (8 shorter events, 0.0 us)
Async XLA Ops:
  4.4 12.0 %copy-start.6 = (s32[1,128,8]{1,2,0:T(8,128)S(1)}, s32[1,128,8]{1,2,0:T(8,128)}, u32[]{:S(2)}) copy-start(s32[1,128,8]{1,2,0:T(8,128)} %param.11) | copy-start | bytes 12292
  4.4 12.1 %copy-start.7 = (s32[1,128]{1,0:T(1,128)S(1)}, s32[1,128]{1,0:T(1,128)}, u32[]{:S(2)}) copy-start(s32[1,128]{1,0:T(1,128)} %count_hbm.1) | copy-start | bytes 1540
  4.4 42.1 %all-to-all-start = ((bf16[128,16,512]{2,1,0:T(8,128)(2,1)}), bf16[128,16,512]{2,1,0:T(8,128)(2,1)}, u32[]{:S(2)}, u32[]{:S(2)}) async-start(bf16[128,16,512]{2,1,0:T(8,128)(2,1)} %shard_map.94), calls=%async_computation | async-start | bytes 4194304 | tf_op jit(solution)/shard_map/all_to_all | solution.py:318
  46.6 11.1 %copy-start.1 = (bf16[1024,1024]{1,0:T(8,128)(2,1)S(1)}, bf16[1024,1024]{1,0:T(8,128)(2,1)}, u32[]{:S(2)}) copy-start(bf16[1024,1024]{1,0:T(8,128)(2,1)} %get-tuple-element.25.at_ref) | copy-start | bytes 6291460
  56.4 3.9 %collective-permute-start = (bf16[1024,512]{1,0:T(8,128)(2,1)}, bf16[1024,512]{1,0:T(8,128)(2,1)S(1)}, u32[]{:S(2)}, u32[]{:S(2)}) collective-permute-start(bf16[1024,512]{1,0:T(8,128)(2,1)} %get-tuple-element.31), channel_id=1, source_target_pairs={{0,1},{1,0},{2,3},{3,2},{4,5},{5,4},{6,7},{7,6},{8,9},{9,8},{10,11... | collective-permute-start | bytes 3145736 | tf_op jit(solution)/shard_map/ppermute | solution.py:339
  57.7 2.6 %copy-start = (bf16[1024,512]{1,0:T(8,128)(2,1)S(1)}, bf16[1024,512]{1,0:T(8,128)(2,1)}, u32[]{:S(2)}) copy-start(bf16[1024,512]{1,0:T(8,128)(2,1)} %f_ref.3) | copy-start | bytes 3145732
  60.3 35.2 %copy-start.5 = (bf16[1024,1024]{1,0:T(8,128)(2,1)S(1)}, bf16[1024,1024]{1,0:T(8,128)(2,1)}, u32[]{:S(2)}) copy-start(bf16[1024,1024]{1,0:T(8,128)(2,1)} %get-tuple-element.23.st_ref) | copy-start | bytes 6291460
  61.8 33.8 %copy-start.2 = (bf16[1024,512]{1,0:T(8,128)(2,1)S(1)}, bf16[1024,512]{1,0:T(8,128)(2,1)}, u32[]{:S(2)}) copy-start(bf16[1024,512]{1,0:T(8,128)(2,1)} %w_ref.1) | copy-start | bytes 3145732
  61.8 33.7 %copy-start.3 = (s32[1,8]{1,0:T(1,128)S(1)}, s32[1,8]{1,0:T(1,128)}, u32[]{:S(2)}) copy-start(s32[1,8]{1,0:T(1,128)} %hub_ref.1) | copy-start | bytes 100
  61.8 33.7 %copy-start.4 = (bf16[1024,1024]{1,0:T(8,128)(2,1)S(1)}, bf16[1024,1024]{1,0:T(8,128)(2,1)}, u32[]{:S(2)}) copy-start(bf16[1024,1024]{1,0:T(8,128)(2,1)} %get-tuple-element.32.at_ref) | copy-start | bytes 6291460

commit v8 on v7

--- a/solution.py
+++ b/solution.py
@@ -133,7 +133,7 @@
     copies = launch([(mix_ref, mix_hbm)], sems, 0)
     count_matrix(u, m, [own_ref.at[:, c] for c in cols])
     mown_ref[...] = mm_first(own_ref[...], f_ref[...])
-    copies += launch([(own_ref, own_hbm), (mown_ref, mown_hbm)], sems, 1)
+    copies += launch([(own_ref, own_hbm.at[:nodes, :]), (mown_ref, mown_hbm)], sems, 1)
     count_matrix(u - nodes, m, [listed_ref.at[:, c] for c in cols])
     count_matrix(u - (nodes + halo), m, [hub_ref.at[:, c] for c in cols])
     copies += launch([(listed_ref, listed_hbm), (hub_ref, hub_hbm.at[:halo, :])], sems, 3)
@@ -218,10 +218,11 @@
         copy.wait()
 
 
-def listed_kernel(core_ref, trio_hbm, hub_hbm, at_ref, out_ref, gm_ref, delta_ref, mean_ref, hub_ref, sems):
+def listed_kernel(core_ref, trio_hbm, hub_hbm, own_at_hbm, at_ref, w_ref, out_ref, own_ref, gm_ref, delta_ref, mean_ref, hub_ref, own_at_ref, sems):
     nodes = gm_ref.shape[0]
     parts_of = [trio_hbm.at[i * nodes : (i + 1) * nodes, :] for i in range(3)]
     first, second = launch([(parts_of[0], gm_ref), (parts_of[1], delta_ref)], sems)
+    (third,) = launch([(own_at_hbm.at[:nodes, :], own_at_ref)], sems, 4)
     hub_load = pltpu.make_async_copy(hub_hbm.at[: hub_ref.shape[0], :], hub_ref, sems.at[2])
     mean_load = pltpu.make_async_copy(parts_of[2], mean_ref, sems.at[3])
     even = core_ref[0] == 0
@@ -229,7 +230,11 @@
     pl.when(jnp.logical_not(even))(mean_load.start)
     first.wait()
     out_ref[...] = mm(at_ref[...], gm_ref[...]).astype(BF)
+    width = own_ref.shape[1]
+    third.wait()
+    own = mm(own_at_ref[...], gm_ref[...])
     second.wait()
+    own_ref[...] = own + mm_last(delta_ref[...], w_ref[:width, :])
     pl.when(even)(hub_load.wait)
     pl.when(jnp.logical_not(even))(mean_load.wait)
 
@@ -260,7 +265,7 @@
         fill(weight_rows)
 
 
-def last_kernel(st_ref, back_ref, at_ref, gm_ref, delta_ref, w_ref, hub_ref, out_hbm, weight_ref, list_ref, out_ref, sems):
+def last_kernel(st_ref, back_ref, own_ref, hub_ref, out_hbm, weight_ref, list_ref, out_ref, sems):
     nodes, width = out_ref.shape
     step = 256
     hub_sum = jnp.zeros(weight_ref.shape, F32)
@@ -279,9 +284,8 @@
     stores = []
     for b in range(nodes // step):
         r = slice(b * step, (b + 1) * step)
-        own = mm(at_ref[r, :], gm_ref[...]) + mm_last(delta_ref[r, :], w_ref[:width, :])
         hot = (iota((step, hubs.shape[1]), 0) + b * step == hubs).astype(F32).astype(BF)
-        out_ref[r, :] = (own + mm(hot, hub_rows) + mm(st_ref[r, :], list_ref[...])).astype(BF)
+        out_ref[r, :] = (own_ref[r, :] + mm(hot, hub_rows) + mm(st_ref[r, :], list_ref[...])).astype(BF)
         stores += launch([(out_ref.at[r, :], out_hbm.at[r, :])], sems, b)
     for copy in stores:
         copy.wait()
@@ -321,7 +325,7 @@
     slot = jnp.where(live, send_rows[0], -1).reshape(1, halo)
     square = ((nodes, nodes), BF)
     hot = [square, ((halo, nodes), BF), ((halo, nodes), BF), ((2, 2 * halo, nodes // 2), BF), ((nodes, halo), BF), wide]
-    outs = hot[:2] + [((BIG * halo, nodes), BF)] + hot[3:]
+    outs = [((BIG * nodes, nodes), BF), hot[1], ((BIG * halo, nodes), BF)] + hot[3:]
     at_own, at_halo, at, mix, st, mean_own = call(
         hot_kernel, [neighbours.T, slot, features], outs, hot + [sems(6)],
         flops=14 * 10**9, read=20 * MIB, mib=63, in_specs=[VM] * 3,
@@ -337,9 +341,9 @@
         flops=6 * 10**9, read=16 * MIB, in_specs=[SM] + [HB] * 7,
     )
     got = lax.ppermute(give, AXES, [(i, i ^ 1) for i in range(parts)])
-    listed, gm, delta, mean, hub_counts = call(
-        listed_kernel, [core, trio, at, at_halo], [half, half, half, half, ((halo, nodes), BF)], [sems(4)],
-        flops=10**9, read=4 * MIB, mib=24, in_specs=[SM, HB, HB, VM], out_specs=[VM] * 5,
+    listed, own, gm, delta, mean, hub_counts = call(
+        listed_kernel, [core, trio, at, at_own, at_halo, weights], [half, wide, half, half, half, ((halo, nodes), BF)], [square, sems(5)],
+        flops=3 * 10**9, read=8 * MIB, mib=24, in_specs=[SM, HB, HB, HB, VM, VM], out_specs=[VM] * 6,
     )
     (pay_back,) = call(
         pack_kernel, [core, listed, gm, delta, mean, hub_counts, features, got], [packed],
@@ -347,9 +351,9 @@
     )
     back = lax.all_to_all(pay_back, AXES, split_axis=0, concat_axis=0, tiled=True).reshape(2 * halo, width)
     grad, grad_weights = call(
-        last_kernel, [st, back, at_own, gm, delta, weights, hub_local], [half, ((8, width), F32)],
+        last_kernel, [st, back, own, hub_local], [half, ((8, width), F32)],
         [((halo, width), BF), half, sems(4)],
-        flops=4 * 10**9, read=10 * MIB, mib=24, in_specs=[VM] * 7, out_specs=[HB, VM],
+        flops=4 * 10**9, read=10 * MIB, mib=24, in_specs=[VM] * 4, out_specs=[HB, VM],
     )
     return act, grad, grad_weights
 

time: 101 us -> 101 us (level)
  transfers between devices with their start and end apart: 2 -> 2, of which waited for: 1 -> 1; matrix products, arithmetic and copies ran while one was open for 1% -> 1% of each run, Pallas kernels for 15% -> 17%
where the time goes in v8:
time: 101 us
  Pallas kernels  34.9 us (35%)
  blocking collectives  33.6 us (33%)
  waiting for transfers between devices  16.7 us (17%)
  starting transfers between devices  13.4 us (13%)
    pallas_call x6, Pallas kernels, call(): pl.pallas_call(kernel, out_shape=[jax.ShapeDtypeStruct(s, d) for s, d in...  34.9 us
    all_to_all x1, blocking collectives, local(): lax.all_to_all(pay_back, AXES, split_axis=0, concat_axis=0, tiled=True)  33.6 us
    all_to_all x1, waiting for transfers between devices, local(): lax.all_to_all(pay, AXES, split_axis=0, concat_axis=0, tiled=True)  16.7 us
    all_to_all x1, starting transfers between devices, local(): lax.all_to_all(pay, AXES, split_axis=0, concat_axis=0, tiled=True)  12 us
  transfers between devices with their start and end apart: 2, of which 1 were waited for; matrix products, arithmetic and copies ran while one was open for 1% of the time, Pallas kernels for 17%

profile of v8, /device:TPU:1, one launch (start us, length us, event | category | flops | bytes accessed | tf_op | source)
XLA Modules:
  0.0 100.6 jit_solution(3817918436998956586)
XLA Ops:
  0.6 3.8 %shard_map.94 = bf16[128,16,512]{2,1,0:T(8,128)(2,1)} custom-call(bf16[1024,512]{1,0:T(8,128)(2,1)} %f_ref.3, s32[8,128]{1,0:T(8,128)} %bitcast.9, s32[1,128]{1,0:T(1,128)} %count_hbm.1, s32[1,8]{1,0:T(1,128)} %hub_ref.1), custom_call_target="tpu_custom_call" | custom-call | flops 1073741824 | bytes 3145728 | tf_op jit(solution)/shard_map/pallas_call | solution.py:295
  4.4 0.0 copy-start.5
  4.4 0.0 copy-start.6
  4.4 12.0 %all-to-all-start = ((bf16[128,16,512]{2,1,0:T(8,128)(2,1)}), bf16[128,16,512]{2,1,0:T(8,128)(2,1)}, u32[]{:S(2)}, u32[]{:S(2)}) async-start(bf16[128,16,512]{2,1,0:T(8,128)(2,1)} %shard_map.94), calls=%async_computation | async-start | bytes 4194304 | tf_op jit(solution)/shard_map/all_to_all | solution.py:322
  16.4 0.0 copy-done.5
  16.4 0.1 copy.11
  16.5 0.0 copy-done.6
  16.5 0.1 iota_compare_fusion
  16.6 0.1 lt.30
  16.7 0.1 squeeze.7
  16.8 0.6 broadcast_select_fusion.slot_ref
  17.4 12.4 %shard_map.95 = (bf16[12288,1024]{1,0:T(8,128)(2,1)}, bf16[1024,1024]{1,0:T(8,128)(2,1)}, bf16[12288,1024]{1,0:T(8,128)(2,1)}, bf16[2,2048,512]{2,1,0:T(8,128)(2...) custom-call(s32[8,1024]{1,0:T(8,128)} %bitcast.11, s32[1,1024]{1,0:T(1,128)} %broadcast_select_fusion.slot_ref, ...), custom_call_target="tpu_custom_call" | custom-call | flops 14000000000 | bytes 20971520 | tf_op jit(solution)/shard_map/pallas_call | solution.py:295
  29.8 16.7 %all-to-all-done = bf16[128,16,512]{2,1,0:T(8,128)(2,1)} async-done(((bf16[128,16,512]{2,1,0:T(8,128)(2,1)}), bf16[128,16,512]{2,1,0:T(8,128)(2,1)}, u32[]{:S(2)}, u32[]{:S(2)}) %all-to-all-start) | async-done | bytes 2097184 | tf_op jit(solution)/shard_map/all_to_all | solution.py:322
  46.6 9.8 %shard_map.96 = (bf16[1024,512]{1,0:T(8,128)(2,1)}, bf16[24576,512]{1,0:T(8,128)(2,1)}, bf16[1024,512]{1,0:T(8,128)(2,1)}) custom-call(s32[1]{0:T(128)} %bitcast.core_ref, bf16[2048,512]{1,0:T(8,128)(2,1)} %bitcast.3.recv_hbm, bf16[2,2048,512]{2,1,0:T(8,128)(2,1)} %get-tuple-element.20.mix_hbm, bf16[12288,1024]{1,0:T(8,128)(2,1)} %get-tuple-element.21.at_hbm.hub_hbm, ...), custom_call_target="tpu_custom_call" | custom-call | flops 6000000000 | bytes 16777216 | tf_op jit(solution)/shard_map/pallas_call | solution.py:295
  56.4 1.4 %collective-permute-start = (bf16[1024,512]{1,0:T(8,128)(2,1)}, bf16[1024,512]{1,0:T(8,128)(2,1)S(1)}, u32[]{:S(2)}, u32[]{:S(2)}) collective-permute-start(bf16[1024,512]{1,0:T(8,128)(2,1)} %get-tuple-element.33), channel_id=1, source_target_pairs={{0,1},{1,0},{2,3},{3,2},{4,5},{5,4},{6,7},{7,6},{8,9},{9,8},{10,11... | collective-permute-start | bytes 3145736 | tf_op jit(solution)/shard_map/ppermute | solution.py:343
  57.8 0.0 copy-done
  57.8 0.0 copy-done.2
  57.8 4.6 %shard_map.97 = (bf16[1024,512]{1,0:T(8,128)(2,1)S(1)}, f32[1024,512]{1,0:T(8,128)S(1)}, bf16[1024,512]{1,0:T(8,128)(2,1)S(1)}, bf16[1024,512]{1,0:T(8,128)(2,1)...) custom-call(s32[1]{0:T(128)} %bitcast.core_ref, bf16[24576,512]{1,0:T(8,128)(2,1)} %get-tuple-element.25.trio_hbm, ...), custom_call_target="tpu_custom_call" | custom-call | flops 3000000000 | bytes 8388608 | tf_op jit(solution)/shard_map/pallas_call | solution.py:295
  62.5 0.0 collective-permute-done.got_ref
  62.5 0.0 copy-done.1
  62.5 1.3 %shard_map.98 = bf16[128,16,512]{2,1,0:T(8,128)(2,1)S(1)} custom-call(s32[1]{0:T(128)} %bitcast.core_ref, bf16[1024,512]{1,0:T(8,128)(2,1)S(1)} %get-tuple-element.28.listed_ref, bf16[1024,512]{1,0:T(8,128)(2,1)S(1)} %get-tuple-element.29.gm_ref, bf16[1024,512]{1,0:T(8,128)(2,1)S(1)} %get-tuple-element.30.delta_ref, ...), custom_call_target="tpu_custom_call" | custom-call | flops 2000000000 | bytes 6291456 | tf_op jit(solution)/shard_map/pallas_call | solution.py:295
  63.8 0.0 copy-start.3
  63.8 33.6 %all_to_all.10 = bf16[128,16,512]{2,1,0:T(8,128)(2,1)S(1)} all-to-all(bf16[128,16,512]{2,1,0:T(8,128)(2,1)S(1)} %shard_map.98), channel_id=1, replica_groups=mesh['row'=16,'col'=8] {'row','col'}, dimensions={0} | all-to-all | bytes 4194304 | tf_op jit(solution)/shard_map/all_to_all | solution.py:352
  97.4 3.0 %shard_map.99 = (bf16[1024,512]{1,0:T(8,128)(2,1)}, f32[8,512]{1,0:T(8,128)}) custom-call(bf16[1024,1024]{1,0:T(8,128)(2,1)S(1)} %copy-done.4, bf16[2048,512]{1,0:T(8,128)(2,1)S(1)} %bitcast.8, f32[1024,512]{1,0:T(8,128)S(1)} %get-tuple-element.34.own_ref, s32[1,8]{1,0:T(1,128)S(1)} %copy-done.3), custom_call_target="tpu_custom_call" | custom-call | flops 4000000000 | bytes 10485760 | tf_op jit(solution)/shard_map/pallas_call | solution.py:295
  (6 shorter events, 0.0 us)
Async XLA Ops:
  4.4 12.0 %copy-start.5 = (s32[1,128,8]{1,2,0:T(8,128)S(1)}, s32[1,128,8]{1,2,0:T(8,128)}, u32[]{:S(2)}) copy-start(s32[1,128,8]{1,2,0:T(8,128)} %param.11) | copy-start | bytes 12292
  4.4 12.1 %copy-start.6 = (s32[1,128]{1,0:T(1,128)S(1)}, s32[1,128]{1,0:T(1,128)}, u32[]{:S(2)}) copy-start(s32[1,128]{1,0:T(1,128)} %count_hbm.1) | copy-start | bytes 1540
  4.4 42.1 %all-to-all-start = ((bf16[128,16,512]{2,1,0:T(8,128)(2,1)}), bf16[128,16,512]{2,1,0:T(8,128)(2,1)}, u32[]{:S(2)}, u32[]{:S(2)}) async-start(bf16[128,16,512]{2,1,0:T(8,128)(2,1)} %shard_map.94), calls=%async_computation | async-start | bytes 4194304 | tf_op jit(solution)/shard_map/all_to_all | solution.py:322
  46.6 11.3 %copy-start = (bf16[1024,512]{1,0:T(8,128)(2,1)S(1)}, bf16[1024,512]{1,0:T(8,128)(2,1)}, u32[]{:S(2)}) copy-start(bf16[1024,512]{1,0:T(8,128)(2,1)} %w_ref.1) | copy-start | bytes 3145732
  46.6 11.3 %copy-start.2 = (bf16[1024,1024]{1,0:T(8,128)(2,1)S(1)}, bf16[1024,1024]{1,0:T(8,128)(2,1)}, u32[]{:S(2)}) copy-start(bf16[1024,1024]{1,0:T(8,128)(2,1)} %get-tuple-element.27.at_ref) | copy-start | bytes 6291460
  56.4 6.1 %collective-permute-start = (bf16[1024,512]{1,0:T(8,128)(2,1)}, bf16[1024,512]{1,0:T(8,128)(2,1)S(1)}, u32[]{:S(2)}, u32[]{:S(2)}) collective-permute-start(bf16[1024,512]{1,0:T(8,128)(2,1)} %get-tuple-element.33), channel_id=1, source_target_pairs={{0,1},{1,0},{2,3},{3,2},{4,5},{5,4},{6,7},{7,6},{8,9},{9,8},{10,11... | collective-permute-start | bytes 3145736 | tf_op jit(solution)/shard_map/ppermute | solution.py:343
  57.8 4.6 %copy-start.1 = (bf16[1024,512]{1,0:T(8,128)(2,1)S(1)}, bf16[1024,512]{1,0:T(8,128)(2,1)}, u32[]{:S(2)}) copy-start(bf16[1024,512]{1,0:T(8,128)(2,1)} %f_ref.3) | copy-start | bytes 3145732
  63.8 33.6 %copy-start.3 = (s32[1,8]{1,0:T(1,128)S(1)}, s32[1,8]{1,0:T(1,128)}, u32[]{:S(2)}) copy-start(s32[1,8]{1,0:T(1,128)} %hub_ref.1) | copy-start | bytes 100
  63.8 33.6 %copy-start.4 = (bf16[1024,1024]{1,0:T(8,128)(2,1)S(1)}, bf16[1024,1024]{1,0:T(8,128)(2,1)}, u32[]{:S(2)}) copy-start(bf16[1024,1024]{1,0:T(8,128)(2,1)} %get-tuple-element.24.st_ref) | copy-start | bytes 6291460

commit v9 on v7

--- a/solution.py
+++ b/solution.py
@@ -218,7 +218,7 @@
         copy.wait()
 
 
-def listed_kernel(core_ref, trio_hbm, hub_hbm, at_ref, out_ref, gm_ref, delta_ref, mean_ref, hub_ref, sems):
+def listed_kernel(core_ref, trio_hbm, hub_hbm, at_ref, w_ref, out_ref, own_ref, gm_ref, delta_ref, mean_ref, hub_ref, sems):
     nodes = gm_ref.shape[0]
     parts_of = [trio_hbm.at[i * nodes : (i + 1) * nodes, :] for i in range(3)]
     first, second = launch([(parts_of[0], gm_ref), (parts_of[1], delta_ref)], sems)
@@ -230,6 +230,7 @@
     first.wait()
     out_ref[...] = mm(at_ref[...], gm_ref[...]).astype(BF)
     second.wait()
+    own_ref[...] = mm_last(delta_ref[...], w_ref[: own_ref.shape[1], :])
     pl.when(even)(hub_load.wait)
     pl.when(jnp.logical_not(even))(mean_load.wait)
 
@@ -260,7 +261,7 @@
         fill(weight_rows)
 
 
-def last_kernel(st_ref, back_ref, at_ref, gm_ref, delta_ref, w_ref, hub_ref, out_hbm, weight_ref, list_ref, out_ref, sems):
+def last_kernel(st_ref, back_ref, at_ref, gm_ref, own_ref, hub_ref, out_hbm, weight_ref, list_ref, out_ref, sems):
     nodes, width = out_ref.shape
     step = 256
     hub_sum = jnp.zeros(weight_ref.shape, F32)
@@ -279,7 +280,7 @@
     stores = []
     for b in range(nodes // step):
         r = slice(b * step, (b + 1) * step)
-        own = mm(at_ref[r, :], gm_ref[...]) + mm_last(delta_ref[r, :], w_ref[:width, :])
+        own = mm(at_ref[r, :], gm_ref[...]) + own_ref[r, :]
         hot = (iota((step, hubs.shape[1]), 0) + b * step == hubs).astype(F32).astype(BF)
         out_ref[r, :] = (own + mm(hot, hub_rows) + mm(st_ref[r, :], list_ref[...])).astype(BF)
         stores += launch([(out_ref.at[r, :], out_hbm.at[r, :])], sems, b)
@@ -337,9 +338,9 @@
         flops=6 * 10**9, read=16 * MIB, in_specs=[SM] + [HB] * 7,
     )
     got = lax.ppermute(give, AXES, [(i, i ^ 1) for i in range(parts)])
-    listed, gm, delta, mean, hub_counts = call(
-        listed_kernel, [core, trio, at, at_halo], [half, half, half, half, ((halo, nodes), BF)], [sems(4)],
-        flops=10**9, read=4 * MIB, mib=24, in_specs=[SM, HB, HB, VM], out_specs=[VM] * 5,
+    listed, own, gm, delta, mean, hub_counts = call(
+        listed_kernel, [core, trio, at, at_halo, weights], [half, wide, half, half, half, ((halo, nodes), BF)], [sems(4)],
+        flops=10**9, read=4 * MIB, mib=24, in_specs=[SM, HB, HB, VM, VM], out_specs=[VM] * 6,
     )
     (pay_back,) = call(
         pack_kernel, [core, listed, gm, delta, mean, hub_counts, features, got], [packed],
@@ -347,9 +348,9 @@
     )
     back = lax.all_to_all(pay_back, AXES, split_axis=0, concat_axis=0, tiled=True).reshape(2 * halo, width)
     grad, grad_weights = call(
-        last_kernel, [st, back, at_own, gm, delta, weights, hub_local], [half, ((8, width), F32)],
+        last_kernel, [st, back, at_own, gm, own, hub_local], [half, ((8, width), F32)],
         [((halo, width), BF), half, sems(4)],
-        flops=4 * 10**9, read=10 * MIB, mib=24, in_specs=[VM] * 7, out_specs=[HB, VM],
+        flops=4 * 10**9, read=10 * MIB, mib=24, in_specs=[VM] * 6, out_specs=[HB, VM],
     )
     return act, grad, grad_weights
 

time: 101 us -> 101 us (level)
  no operation moved by 1% of the time
where the time goes in v9:
time: 101 us; the launch traced here: 100 us
  Pallas kernels  34.7 us (34%)
  blocking collectives  33.7 us (33%)
  waiting for transfers between devices  16.9 us (17%)
  starting transfers between devices  13.2 us (13%)
    pallas_call x6, Pallas kernels, call(): pl.pallas_call(kernel, out_shape=[jax.ShapeDtypeStruct(s, d) for s, d in...  34.7 us
    all_to_all x1, blocking collectives, local(): lax.all_to_all(pay_back, AXES, split_axis=0, concat_axis=0, tiled=True)  33.7 us
    all_to_all x1, waiting for transfers between devices, local(): lax.all_to_all(pay, AXES, split_axis=0, concat_axis=0, tiled=True)  16.9 us
    all_to_all x1, starting transfers between devices, local(): lax.all_to_all(pay, AXES, split_axis=0, concat_axis=0, tiled=True)  12 us
  transfers between devices with their start and end apart: 2, of which 1 were waited for; matrix products, arithmetic and copies ran while one was open for 1% of the time, Pallas kernels for 15%

profile of v9, /device:TPU:1, one launch (start us, length us, event | category | flops | bytes accessed | tf_op | source)
XLA Modules:
  0.0 100.5 jit_solution(11346861035468308461)
XLA Ops:
  0.6 3.8 %shard_map.94 = bf16[128,16,512]{2,1,0:T(8,128)(2,1)} custom-call(bf16[1024,512]{1,0:T(8,128)(2,1)} %f_ref.3, s32[8,128]{1,0:T(8,128)} %bitcast.9, s32[1,128]{1,0:T(1,128)} %count_hbm.1, s32[1,8]{1,0:T(1,128)} %hub_ref.1), custom_call_target="tpu_custom_call" | custom-call | flops 1073741824 | bytes 3145728 | tf_op jit(solution)/shard_map/pallas_call | solution.py:292
  4.4 0.0 copy-start.6
  4.4 0.0 copy-start.7
  4.4 12.0 %all-to-all-start = ((bf16[128,16,512]{2,1,0:T(8,128)(2,1)}), bf16[128,16,512]{2,1,0:T(8,128)(2,1)}, u32[]{:S(2)}, u32[]{:S(2)}) async-start(bf16[128,16,512]{2,1,0:T(8,128)(2,1)} %shard_map.94), calls=%async_computation | async-start | bytes 4194304 | tf_op jit(solution)/shard_map/all_to_all | solution.py:319
  16.4 0.1 copy.11
  16.5 0.1 iota_compare_fusion
  16.6 0.1 lt.30
  16.7 0.1 squeeze.7
  16.8 0.6 broadcast_select_fusion.slot_ref
  17.4 12.2 %shard_map.95 = (bf16[1024,1024]{1,0:T(8,128)(2,1)}, bf16[1024,1024]{1,0:T(8,128)(2,1)}, bf16[12288,1024]{1,0:T(8,128)(2,1)}, bf16[2,2048,512]{2,1,0:T(8,128)(2,...) custom-call(s32[8,1024]{1,0:T(8,128)} %bitcast.11, s32[1,1024]{1,0:T(1,128)} %broadcast_select_fusion.slot_ref, ...), custom_call_target="tpu_custom_call" | custom-call | flops 14000000000 | bytes 20971520 | tf_op jit(solution)/shard_map/pallas_call | solution.py:292
  29.7 16.9 %all-to-all-done = bf16[128,16,512]{2,1,0:T(8,128)(2,1)} async-done(((bf16[128,16,512]{2,1,0:T(8,128)(2,1)}), bf16[128,16,512]{2,1,0:T(8,128)(2,1)}, u32[]{:S(2)}, u32[]{:S(2)}) %all-to-all-start) | async-done | bytes 2097184 | tf_op jit(solution)/shard_map/all_to_all | solution.py:319
  46.6 9.8 %shard_map.96 = (bf16[1024,512]{1,0:T(8,128)(2,1)}, bf16[24576,512]{1,0:T(8,128)(2,1)}, bf16[1024,512]{1,0:T(8,128)(2,1)}) custom-call(s32[1]{0:T(128)} %bitcast.core_ref, bf16[2048,512]{1,0:T(8,128)(2,1)} %bitcast.3.recv_hbm, bf16[2,2048,512]{2,1,0:T(8,128)(2,1)} %get-tuple-element.20.mix_hbm, bf16[12288,1024]{1,0:T(8,128)(2,1)} %get-tuple-element.21.at_hbm.hub_hbm, ...), custom_call_target="tpu_custom_call" | custom-call | flops 6000000000 | bytes 16777216 | tf_op jit(solution)/shard_map/pallas_call | solution.py:292
  56.4 1.3 %collective-permute-start = (bf16[1024,512]{1,0:T(8,128)(2,1)}, bf16[1024,512]{1,0:T(8,128)(2,1)S(1)}, u32[]{:S(2)}, u32[]{:S(2)}) collective-permute-start(bf16[1024,512]{1,0:T(8,128)(2,1)} %get-tuple-element.32), channel_id=1, source_target_pairs={{0,1},{1,0},{2,3},{3,2},{4,5},{5,4},{6,7},{7,6},{8,9},{9,8},{10,11... | collective-permute-start | bytes 3145736 | tf_op jit(solution)/shard_map/ppermute | solution.py:340
  57.7 0.0 copy-done.2
  57.7 3.3 %shard_map.97 = (bf16[1024,512]{1,0:T(8,128)(2,1)S(1)}, f32[1024,512]{1,0:T(8,128)S(1)}, bf16[1024,512]{1,0:T(8,128)(2,1)S(1)}, bf16[1024,512]{1,0:T(8,128)(2,1)...) custom-call(s32[1]{0:T(128)} %bitcast.core_ref, bf16[24576,512]{1,0:T(8,128)(2,1)} %get-tuple-element.25.trio_hbm, ...), custom_call_target="tpu_custom_call" | custom-call | flops 1000000000 | bytes 4194304 | tf_op jit(solution)/shard_map/pallas_call | solution.py:292
  61.0 0.0 collective-permute-done.got_ref
  61.0 1.5 %shard_map.98 = bf16[128,16,512]{2,1,0:T(8,128)(2,1)S(1)} custom-call(s32[1]{0:T(128)} %bitcast.core_ref, bf16[1024,512]{1,0:T(8,128)(2,1)S(1)} %get-tuple-element.27.listed_ref, bf16[1024,512]{1,0:T(8,128)(2,1)S(1)} %get-tuple-element.28.gm_ref, bf16[1024,512]{1,0:T(8,128)(2,1)S(1)} %get-tuple-element.29.delta_ref, ...), custom_call_target="tpu_custom_call" | custom-call | flops 2000000000 | bytes 6291456 | tf_op jit(solution)/shard_map/pallas_call | solution.py:292
  62.5 0.0 copy-start.3
  62.5 0.0 copy-start.4
  62.5 0.0 copy-start.5
  62.5 33.7 %all_to_all.10 = bf16[128,16,512]{2,1,0:T(8,128)(2,1)S(1)} all-to-all(bf16[128,16,512]{2,1,0:T(8,128)(2,1)S(1)} %shard_map.98), channel_id=1, replica_groups=mesh['row'=16,'col'=8] {'row','col'}, dimensions={0} | all-to-all | bytes 4194304 | tf_op jit(solution)/shard_map/all_to_all | solution.py:349
  96.3 0.0 copy-done.3
  96.3 0.0 copy-done.5
  96.3 4.0 %shard_map.99 = (bf16[1024,512]{1,0:T(8,128)(2,1)}, f32[8,512]{1,0:T(8,128)}) custom-call(bf16[1024,1024]{1,0:T(8,128)(2,1)S(1)} %copy-done.5, bf16[2048,512]{1,0:T(8,128)(2,1)S(1)} %bitcast.8, bf16[1024,1024]{1,0:T(8,128)(2,1)S(1)} %copy-done.4, bf16[1024,512]{1,0:T(8,128)(2,1)S(1)} %get-tuple-element.28.gm_ref, f32[1024,512]{1,0:T(8,128)S(1)} %get-tuple-element.34.own_ref, ...), custom_call_target="tpu_custom_call" | custom-call | flops 4000000000 | bytes 10485760 | tf_op jit(solution)/shard_map/pallas_call | solution.py:292
  (8 shorter events, 0.0 us)
Async XLA Ops:
  4.4 12.0 %copy-start.6 = (s32[1,128,8]{1,2,0:T(8,128)S(1)}, s32[1,128,8]{1,2,0:T(8,128)}, u32[]{:S(2)}) copy-start(s32[1,128,8]{1,2,0:T(8,128)} %param.11) | copy-start | bytes 12292
  4.4 12.1 %copy-start.7 = (s32[1,128]{1,0:T(1,128)S(1)}, s32[1,128]{1,0:T(1,128)}, u32[]{:S(2)}) copy-start(s32[1,128]{1,0:T(1,128)} %count_hbm.1) | copy-start | bytes 1540
  4.4 42.1 %all-to-all-start = ((bf16[128,16,512]{2,1,0:T(8,128)(2,1)}), bf16[128,16,512]{2,1,0:T(8,128)(2,1)}, u32[]{:S(2)}, u32[]{:S(2)}) async-start(bf16[128,16,512]{2,1,0:T(8,128)(2,1)} %shard_map.94), calls=%async_computation | async-start | bytes 4194304 | tf_op jit(solution)/shard_map/all_to_all | solution.py:319
  46.6 11.1 %copy-start = (bf16[1024,512]{1,0:T(8,128)(2,1)S(1)}, bf16[1024,512]{1,0:T(8,128)(2,1)}, u32[]{:S(2)}) copy-start(bf16[1024,512]{1,0:T(8,128)(2,1)} %w_ref.1) | copy-start | bytes 3145732
  46.6 11.1 %copy-start.2 = (bf16[1024,1024]{1,0:T(8,128)(2,1)S(1)}, bf16[1024,1024]{1,0:T(8,128)(2,1)}, u32[]{:S(2)}) copy-start(bf16[1024,1024]{1,0:T(8,128)(2,1)} %get-tuple-element.26.at_ref) | copy-start | bytes 6291460
  56.4 4.6 %collective-permute-start = (bf16[1024,512]{1,0:T(8,128)(2,1)}, bf16[1024,512]{1,0:T(8,128)(2,1)S(1)}, u32[]{:S(2)}, u32[]{:S(2)}) collective-permute-start(bf16[1024,512]{1,0:T(8,128)(2,1)} %get-tuple-element.32), channel_id=1, source_target_pairs={{0,1},{1,0},{2,3},{3,2},{4,5},{5,4},{6,7},{7,6},{8,9},{9,8},{10,11... | collective-permute-start | bytes 3145736 | tf_op jit(solution)/shard_map/ppermute | solution.py:340
  57.7 3.4 %copy-start.1 = (bf16[1024,512]{1,0:T(8,128)(2,1)S(1)}, bf16[1024,512]{1,0:T(8,128)(2,1)}, u32[]{:S(2)}) copy-start(bf16[1024,512]{1,0:T(8,128)(2,1)} %f_ref.3) | copy-start | bytes 3145732
  62.5 33.8 %copy-start.3 = (s32[1,8]{1,0:T(1,128)S(1)}, s32[1,8]{1,0:T(1,128)}, u32[]{:S(2)}) copy-start(s32[1,8]{1,0:T(1,128)} %hub_ref.1) | copy-start | bytes 100
  62.5 33.7 %copy-start.4 = (bf16[1024,1024]{1,0:T(8,128)(2,1)S(1)}, bf16[1024,1024]{1,0:T(8,128)(2,1)}, u32[]{:S(2)}) copy-start(bf16[1024,1024]{1,0:T(8,128)(2,1)} %get-tuple-element.33.at_ref) | copy-start | bytes 6291460
  62.5 33.7 %copy-start.5 = (bf16[1024,1024]{1,0:T(8,128)(2,1)S(1)}, bf16[1024,1024]{1,0:T(8,128)(2,1)}, u32[]{:S(2)}) copy-start(bf16[1024,1024]{1,0:T(8,128)(2,1)} %get-tuple-element.24.st_ref) | copy-start | bytes 6291460
